TPU v7x, 32 devices: a whole 2x2x4 slice. The times are simulated.
32 devices in a mesh: ctx: 4 (over x, core), tsp: 4 (over z), dp: 2 (over y).
Axes of the slice: x: 2, y: 2, z: 4, core: 2. Of those that a mesh axis runs over, the one named last changes fastest.
Arguments:
- queries: bfloat16 [2, 2048, 2048], P('dp', 'ctx', 'tsp'), may hold values from -6 to 6
- keys: bfloat16 [2, 2048, 2048], P('dp', 'ctx', 'tsp'), may hold values from -6 to 6
- values: bfloat16 [2, 2048, 2048], P('dp', 'ctx', 'tsp'), may hold values from -6 to 6
- attn_out: bfloat16 [2, 2048, 2048], P('dp', 'ctx', 'tsp'), may hold values from -6 to 6
- out_grad: bfloat16 [2, 2048, 4096], P('dp', ('ctx', 'tsp')), may hold values from -3 to 3
- out_weight: bfloat16 [4096, 2048], P('ctx', 'tsp'), may hold values from -0.09375 to 0.09375
- block_mask: int32 [2, 4, 8, 8], P('dp', 'ctx'), may hold values 0 or 1
Outputs:
- query_grads: bfloat16 [2, 2048, 2048], P('dp', 'ctx', 'tsp')
- key_grads: bfloat16 [2, 2048, 2048], P('dp', 'ctx', 'tsp')
- value_grads: bfloat16 [2, 2048, 2048], P('dp', 'ctx', 'tsp')
- weight_grad: float32 [4096, 2048], P('ctx', 'tsp')
Inputs may be any that keep to these rules, and one draw needn't show every extreme that they name: `block_mask`: 1 lets a key block feed a later query block of the same group.
All inputs are finite; a program needn't handle non-finite values.
Results may differ from a plain program's by a relative error of at most 0.0058.
Values may be sent and summed in bfloat16 or wider, within the bound.
No kernel may reach another device: no remote copies, remote signals or barrier semaphores. Data moves between devices by JAX's collectives and lax.ppermute only.
A program may use at most 128 MiB of HBM per device.

v0:
```python
import math

import jax
import jax.numpy as jnp
from jax import lax
from jax.sharding import PartitionSpec as P

HEAD = 128
BLK = 64


def entering(array, axis, combine, identity, reverse):
    length, here = (lax.axis_size(axis), lax.axis_index(axis))
    everything = lax.all_gather(array, axis)
    start = jnp.broadcast_to(jnp.asarray(identity, array.dtype), array.shape)

    def turn(k, before):
        at = length - 1 - k if reverse else k
        reached = at > here if reverse else at < here
        new = combine(before, everything[at])
        return jnp.where(reached, new, before)

    return lax.fori_loop(0, length, turn, start)


def allowed_pairs(block_table):
    blocks = block_table.shape[0]
    length = blocks * BLK
    wide_table = jnp.broadcast_to(
        block_table[:, None, :, None], (blocks, BLK, blocks, BLK)
    ).reshape(length, length)
    row_pos = jnp.arange(length)[:, None]
    col_pos = jnp.arange(length)[None, :]
    row_blk = row_pos // BLK
    col_blk = col_pos // BLK
    return (row_blk > col_blk) & (wide_table == 1) | (row_blk == col_blk) & (row_pos >= col_pos)


def add_states(earlier, coming):
    return jax.tree.map(jnp.add, earlier, coming)


def shards(queries, keys, values, attn_out, out_grad, out_weight, block_mask):
    f32 = jnp.float32
    batch_size, group_len, width_here = queries.shape
    heads_here = width_here // HEAD
    seq_len = group_len * lax.axis_size("ctx")
    score_scale = 1.0 / math.sqrt(HEAD * seq_len)
    norm_factor = 1.0 / math.sqrt(seq_len * batch_size * lax.axis_size("dp"))
    gathered = lax.all_gather(out_grad, "tsp", axis=1, tiled=True)
    flat_grad = gathered.reshape(batch_size * group_len, gathered.shape[2])
    columns = flat_grad
    out_grads = jnp.dot(
        columns, lax.all_gather(out_weight, "ctx", axis=0, tiled=True), preferred_element_type=f32
    ).astype(jnp.bfloat16)
    opened = attn_out.reshape(batch_size * group_len, width_here)
    columns = flat_grad
    product = lax.dot_general(columns, opened, (((0,), (0,)), ((), ())), preferred_element_type=f32)
    partial_grad = lax.psum_scatter(product * norm_factor, "ctx", scatter_dimension=0, tiled=True)
    weight_grad = lax.psum(partial_grad, "dp")
    shape_four = (batch_size, group_len, heads_here, HEAD)
    query_heads = queries.reshape(shape_four)
    key_heads = keys.reshape(shape_four)
    value_heads = values.reshape(shape_four)
    grad_heads = out_grads.reshape(shape_four)
    key_value = jnp.einsum("bthd,bthe->bhde", key_heads, value_heads, preferred_element_type=f32)
    query_grad = jnp.einsum("bthd,bthe->bhde", query_heads, grad_heads, preferred_element_type=f32)
    zero_state = jnp.zeros_like(key_value)
    earlier_sum = entering(key_value, "ctx", add_states, zero_state, False)
    later_sum = entering(query_grad, "ctx", add_states, zero_state, True)
    prev_state = (earlier_sum * score_scale).astype(jnp.bfloat16)
    later_state = (later_sum * score_scale).astype(jnp.bfloat16)
    allowed = jax.vmap(allowed_pairs)(block_mask[:, 0])[:, None]
    scores = (
        jnp.einsum("bthd,bshd->bhts", query_heads, key_heads, preferred_element_type=f32)
        * score_scale
    )
    score_weights = jnp.where(allowed, scores, 0.0).astype(jnp.bfloat16)
    mixing = (
        jnp.einsum("bthe,bshe->bhts", grad_heads, value_heads, preferred_element_type=f32)
        * score_scale
    )
    grad_weights = jnp.where(allowed, mixing, 0.0).astype(jnp.bfloat16)
    query_out = jnp.einsum(
        "bhts,bshd->bthd", grad_weights, key_heads, preferred_element_type=f32
    ) + jnp.einsum("bthe,bhde->bthd", grad_heads, prev_state, preferred_element_type=f32)
    key_out = jnp.einsum(
        "bhts,bthd->bshd", grad_weights, query_heads, preferred_element_type=f32
    ) + jnp.einsum("bshe,bhde->bshd", value_heads, later_state, preferred_element_type=f32)
    value_out = jnp.einsum(
        "bhts,bthe->bshe", score_weights, grad_heads, preferred_element_type=f32
    ) + jnp.einsum("bshd,bhde->bshe", key_heads, later_state, preferred_element_type=f32)
    out_shape = (batch_size, group_len, width_here)
    return (
        query_out.astype(jnp.bfloat16).reshape(out_shape),
        key_out.astype(jnp.bfloat16).reshape(out_shape),
        value_out.astype(jnp.bfloat16).reshape(out_shape),
        weight_grad,
    )


def solution(mesh):
    placed = (
        P("dp", "ctx", "tsp"),
        P("dp", "ctx", "tsp"),
        P("dp", "ctx", "tsp"),
        P("dp", "ctx", "tsp"),
        P("dp", ("ctx", "tsp"), None),
        P("ctx", "tsp"),
        P("dp", "ctx", None, None),
    )
    return jax.shard_map(
        shards,
        mesh=mesh,
        in_specs=placed,
        out_specs=(
            P("dp", "ctx", "tsp"),
            P("dp", "ctx", "tsp"),
            P("dp", "ctx", "tsp"),
            P("ctx", "tsp"),
        ),
        check_vma=False,
    )
```

profile of v0, /device:TPU:0, one launch (start us, length us, event | category | flops | bytes accessed | tf_op | source)
XLA Modules:
  0.0 314.1 jit_solution(18247178082178274773)
XLA Ops:
  8.7 1.2 reshape.289
  9.9 1.4 reshape.288
  11.3 1.1 fusion.19
  12.4 80.7 %all-gather.7.cloned.1.call-done = bf16[1,512,4096]{2,1,0:T(8,128)(2,1)} async-done(((bf16[1,128,4096]{2,1,0:T(8,128)(2,1)}), bf16[1,512,4096]{2,1,0:T(8,128)(2,1)}) %all-gather.7.cloned.1.call-update) | async-done | bytes 4194320 | tf_op jit(solution)/shard_map/all_gather | solution.py:50
  93.1 8.1 %convolution_multiply_fusion = f32[4096,512]{1,0:T(8,128)} fusion(bf16[1,512,4096]{2,1,0:T(8,128)(2,1)} %all-gather.7.cloned.1.call-done, bf16[1,512,512]{2,1,0:T(8,128)(2,1)S(1)} %copy-done), kind=kOutput, calls=%fused_computation.2 | convolution fusion | flops 2149580800 | bytes 13107200 | tf_op jit(solution)/shard_map/dot_general | solution.py:58
  103.4 24.3 %all-gather.9.cloned.1.call-done = bf16[4096,512]{1,0:T(8,128)(2,1)} async-done(((bf16[1024,512]{1,0:T(8,128)(2,1)}), bf16[4096,512]{1,0:T(8,128)(2,1)}) %all-gather.9.cloned.1.call-update) | async-done | bytes 4194320 | tf_op jit(solution)/shard_map/all_gather | solution.py:54
  127.7 5.8 %fusion.6 = bf16[512,512]{0,1:T(8,128)(2,1)S(1)} fusion(bf16[4096,512]{1,0:T(8,128)(2,1)} %all-gather.9.cloned.1.call-done, bf16[1,512,4096]{2,1,0:T(8,128)(2,1)} %all-gather.7.cloned.1.call-done), kind=kOutput, calls=%fused_computation.15 | convolution fusion | flops 2147745792 | bytes 8912896 | tf_op jit(solution)/shard_map/dot_general | solution.py:53
  134.6 0.9 copy.36
  135.7 10.9 %all-gather.11.cloned.1.call-done = f32[16,128,128]{2,1,0:T(8,128)} async-done(((f32[4,128,128]{2,1,0:T(8,128)}), f32[16,128,128]{2,1,0:T(8,128)}) %all-gather.11.cloned.1.call-update) | async-done | bytes 1048592 | tf_op jit(solution)/shard_map/all_gather | solution.py:14
  146.6 4.2 %while.30 = (s32[]{:T(128)}, f32[1,4,128,128]{3,2,1,0:T(8,128)S(1)}, s32[]{:T(128)}, f32[4,1,4,128,128]{4,3,2,1,0:T(8,128)}, s32[]{:T(128)}, /*index=5*/s32[]{:T(128)}) while((s32[]{:T(128)}, f32[1,4,128,128]{3,2,1,0:T(8,128)S(1)}, s32[]{:T(128)}, f32[4,1,4,128,128]{4,3,2,1,0:T(8,128)}, s32[]{:T(128)}, /*index=5*/s32[]{:T(128)}) %tuple.97), condition=%wide.region_1.0_spmd.clone, body=%wide.region_0.0_spmd.clone.sunk | while | flops 196612 | bytes 786533 | solution.py:23
  146.6 1.0 add_select_fusion.5
  147.6 1.0 add_select_fusion.5
  148.7 1.0 add_select_fusion.5
  149.8 1.0 add_select_fusion.5
  150.9 2.2 select_convert_fusion.1
  153.1 0.8 convolution_bitcast_fusion.1
  153.9 1.1 fusion.9
  155.0 2.1 copy.41
  157.0 63.7 %reduce-scatter.2.cloned.1.call-done = f32[1024,512]{1,0:T(8,128)} async-done(((f32[4096,512]{1,0:T(8,128)}), f32[1024,512]{1,0:T(8,128)}) %reduce-scatter.2.cloned.1.call-update) | async-done | bytes 2097168 | tf_op jit(solution)/shard_map/reduce_scatter | solution.py:59
  220.8 2.5 convolution_bitcast_fusion
  223.3 15.7 %all-gather.13.cloned.1.call-done = f32[16,128,128]{2,1,0:T(8,128)} async-done(((f32[4,128,128]{2,1,0:T(8,128)}), f32[16,128,128]{2,1,0:T(8,128)}) %all-gather.13.cloned.1.call-update) | async-done | bytes 1048592 | tf_op jit(solution)/shard_map/all_gather | solution.py:14
  239.0 4.3 %while.31 = (s32[]{:T(128)}, f32[1,4,128,128]{3,2,1,0:T(8,128)S(1)}, s32[]{:T(128)}, f32[4,1,4,128,128]{4,3,2,1,0:T(8,128)}, s32[]{:T(128)}, /*index=5*/s32[]{:T(128)}, s32[]{:T(128)}, s32[]{:T(128)}) while((s32[]{:T(128)}, f32[1,4,128,128]{3,2,1,0:T(8,128)S(1)}, s32[]{:T(128)}, f32[4,1,4,128,128]{4,3,2,1,0:T(8,128)}, s32[]{:T(128)}, ...), condition=%wide.region_3.4_spmd.clone, body=%wide.region_2.3_spmd.clone.sunk | while | flops 196616 | bytes 786595 | solution.py:23
  239.0 1.0 add_select_fusion.6
  240.1 1.0 add_select_fusion.6
  241.2 1.0 add_select_fusion.6
  242.2 1.0 add_select_fusion.6
  243.3 1.3 fusion.26
  244.6 3.5 %fusion.5 = bf16[4,128,512]{2,1,0:T(8,128)(2,1)} fusion(f32[4,128,512]{2,1,0:T(8,128)} %fusion.26, bf16[512,4,128]{0,2,1:T(8,128)(2,1)} %bitcast.66, pred[512,512]{1,0:T(8,128)(4,1)} %copy-done.12, bf16[512,4,128]{2,1,0:T(4,128)(2,1)S(1)} %copy-done.5, bf16[512,4,128]{2,1,0:T(4,128)(2,1)S(1)} %copy-done.3), kind=kOutput, calls=%fused_computation.14 | convolution fusion | flops 540540928 | bytes 3407872 | tf_op jit(solution)/shard_map/bhts,bthe->bshe/dot_general | solution.py:90
  248.1 2.0 copy.43
  250.5 1.0 copy.42
  251.5 52.7 %all-reduce.2.cloned.1.call-done = f32[1024,512]{1,0:T(8,128)} async-done(((f32[1024,512]{1,0:T(8,128)}), f32[1024,512]{1,0:T(8,128)}) %all-reduce.2.cloned.1.call-update) | async-done | bytes 2097168 | tf_op jit(solution)/shard_map/psum | solution.py:60
  304.2 3.1 copy.82
  (50 shorter events, 5.3 us)
Async XLA Ops:
  7.2 85.9 %copy-start = (bf16[1,512,512]{2,1,0:T(8,128)(2,1)S(1)}, bf16[1,512,512]{2,1,0:T(8,128)(2,1)}, u32[]{:S(2)}) copy-start(bf16[1,512,512]{2,1,0:T(8,128)(2,1)} %param.14) | copy-start | bytes 1572868
  7.2 85.9 %all-gather.7.cloned.1.call-start = ((), (), s32[]{:S(2)}) async-start(), calls=%async_computation.1 | async-start | bytes 5242880 | tf_op jit(solution)/shard_map/all_gather | solution.py:50
  7.9 119.8 %all-gather.9.cloned.1.call-start = ((), (), s32[]{:S(2)}) async-start(), calls=%async_computation.2 | async-start | bytes 5242880 | tf_op jit(solution)/shard_map/all_gather | solution.py:54
  8.7 137.9 %all-gather.11.cloned.1.call-start = ((), (), s32[]{:S(2)}) async-start(), calls=%async_computation.5 | async-start | bytes 1310720 | tf_op jit(solution)/shard_map/all_gather | solution.py:14
  9.9 91.3 %copy-start.1 = (bf16[512,4,128]{2,1,0:T(4,128)(2,1)}, bf16[512,4,128]{2,1,0:T(4,128)(2,1)S(1)}, u32[]{:S(2)}) copy-start(bf16[512,4,128]{2,1,0:T(4,128)(2,1)S(1)} %reshape.289) | copy-start | bytes 1572868
  11.3 90.0 %copy-start.7 = (bf16[512,4,128]{2,1,0:T(4,128)(2,1)}, bf16[512,4,128]{2,1,0:T(4,128)(2,1)S(1)}, u32[]{:S(2)}) copy-start(bf16[512,4,128]{2,1,0:T(4,128)(2,1)S(1)} %reshape.288) | copy-start | bytes 1572868
  12.3 208.4 %reduce-scatter.2.cloned.1.call-start = ((), (), s32[]{:S(2)}) async-start(), calls=%async_computation.3 | async-start | bytes 10485760 | tf_op jit(solution)/shard_map/reduce_scatter | solution.py:59
  101.2 0.7 copy-start.13
  101.2 1.6 copy-start.11
  101.3 137.8 %all-gather.13.cloned.1.call-start = ((), (), s32[]{:S(2)}) async-start(), calls=%async_computation.6 | async-start | bytes 1310720 | tf_op jit(solution)/shard_map/all_gather | solution.py:14
  103.0 30.6 %copy-start.4 = (bf16[512,4,128]{2,1,0:T(4,128)(2,1)}, bf16[512,4,128]{2,1,0:T(4,128)(2,1)S(1)}, u32[]{:S(2)}) copy-start(bf16[512,4,128]{2,1,0:T(4,128)(2,1)S(1)} %reshape.292) | copy-start | bytes 1572868
  103.3 47.5 %copy-start.12 = (pred[512,512]{1,0:T(8,128)(4,1)}, pred[512,512]{1,0:T(8,128)(4,1)S(1)}, u32[]{:S(2)}) copy-start(pred[512,512]{1,0:T(8,128)(4,1)S(1)} %fusion.12) | copy-start | bytes 786436
  133.5 0.8 copy-start.9
  135.5 168.7 %all-reduce.2.cloned.1.call-start = ((), (), s32[]{:S(2)}) async-start(), calls=%async_computation.4 | async-start | bytes 4194304 | tf_op jit(solution)/shard_map/psum | solution.py:60
  150.8 2.2 copy-start.2
  150.8 3.1 copy-start.10
  223.3 20.0 %copy-start.3 = (bf16[512,4,128]{2,1,0:T(4,128)(2,1)S(1)}, bf16[512,4,128]{2,1,0:T(4,128)(2,1)}, u32[]{:S(2)}) copy-start(bf16[512,4,128]{2,1,0:T(4,128)(2,1)} %copy-done.1) | copy-start | bytes 1572868
  223.3 21.3 %copy-start.5 = (bf16[512,4,128]{2,1,0:T(4,128)(2,1)S(1)}, bf16[512,4,128]{2,1,0:T(4,128)(2,1)}, u32[]{:S(2)}) copy-start(bf16[512,4,128]{2,1,0:T(4,128)(2,1)} %copy-done.4) | copy-start | bytes 1572868
  244.6 5.5 %copy-start.6 = (f32[4,128,512]{2,1,0:T(8,128)S(1)}, f32[4,128,512]{2,1,0:T(8,128)}, u32[]{:S(2)}) copy-start(f32[4,128,512]{2,1,0:T(8,128)} %convolution_bitcast_fusion) | copy-start | bytes 3145732
  244.6 5.5 %copy-start.8 = (bf16[512,4,128]{2,1,0:T(4,128)(2,1)S(1)}, bf16[512,4,128]{2,1,0:T(4,128)(2,1)}, u32[]{:S(2)}) copy-start(bf16[512,4,128]{2,1,0:T(4,128)(2,1)} %copy-done.7) | copy-start | bytes 1572868
Sparse Core Ops, SparseCore 0:
  9.6 83.4 all-gather.6
  94.6 32.9 all-gather.8
  129.8 16.7 all-gather.10
  149.0 71.7 reduce-scatter.1
  222.3 16.7 all-gather.12
  241.3 62.9 all-reduce.1
where the time goes:
time: 315 us; the launch traced here: 314 us
  waiting for transfers between devices  249 us (79%)
  matrix products  27.1 us (9%)
  between operations  14.4 us (5%)
  local copies, waits for them, and re-layouts  14 us (4%)
  other arithmetic  8.69 us (3%)
    all_gather x1, waiting for transfers between devices, shards(): gathered = lax.all_gather(out_grad, 'tsp', axis=1, tiled=True)  80.7 us
    reduce_scatter x1, waiting for transfers between devices, shards(): lax.psum_scatter(product * norm_factor, 'ctx', scatter_dimension=0, tiled...  63.7 us
    psum x1, waiting for transfers between devices, shards(): weight_grad = lax.psum(partial_grad, 'dp')  52.7 us
    all_gather x2, waiting for transfers between devices, entering(): everything = lax.all_gather(array, axis)  26.6 us
    all_gather x1, waiting for transfers between devices, shards(): lax.all_gather(out_weight, 'ctx', axis=0, tiled=True)  24.3 us
    unnamed x32, local copies, waits for them, and re-layouts  9.6 us
    select_n x8, other arithmetic, turn(): return jnp.where(reached, new, before)  8.32 us
    dot_general x1, matrix products, shards(): lax.dot_general(columns, opened, (((0,), (0,)), ((), ())), preferred_elem...  8.13 us
  transfers between devices with their start and end apart: 6, of which 6 were waited for; matrix products, arithmetic and copies ran while one was open for 14% of the time, Pallas kernels for 0%

commit v1 on v0

v1 whole, which is shorter than its diff:
```python
import functools
import math

import jax
import jax.numpy as jnp
from jax import lax
from jax.experimental import pallas as pl
from jax.experimental.pallas import tpu as pltpu
from jax.sharding import PartitionSpec as P

HEAD = 128
BLK = 64
CHUNKS = 4
F32 = jnp.float32
BF16 = jnp.bfloat16
NT = (((1,), (1,)), ((), ()))
NN = (((1,), (0,)), ((), ()))
TN = (((0,), (0,)), ((), ()))
VMEM_LIMIT = 48 * 1024 * 1024


def mm(a, b, dims):
    return lax.dot_general(a, b, dims, preferred_element_type=F32)


def params():
    return pltpu.CompilerParams(vmem_limit_bytes=VMEM_LIMIT)


def allowed_pairs(block_table):
    blocks = block_table.shape[0]
    length = blocks * BLK
    wide_table = jnp.broadcast_to(
        block_table[:, None, :, None], (blocks, BLK, blocks, BLK)
    ).reshape(length, length)
    row_pos = jnp.arange(length)[:, None]
    col_pos = jnp.arange(length)[None, :]
    row_blk = row_pos // BLK
    col_blk = col_pos // BLK
    return (row_blk > col_blk) & (wide_table == 1) | (row_blk == col_blk) & (row_pos >= col_pos)


def bits_of(count):
    return [1 << b for b in range(count.bit_length() - 1)]


def reversed_order(count):
    order = [0]
    for bit in reversed(bits_of(count)):
        order = order + [j | bit for j in order]
    width = count.bit_length() - 1
    return [int(format(p, "b").zfill(width)[::-1], 2) if width else 0 for p in range(count)]


def swap(array, axis, bit):
    count = lax.axis_size(axis)
    return lax.ppermute(array, axis, [(i, i ^ bit) for i in range(count)])


def scan_states(state, axis, later, sent):
    here = lax.axis_index(axis)
    outside, total = jnp.zeros_like(state), state
    bits = bits_of(lax.axis_size(axis))
    for bit in bits:
        coming = swap(total.astype(sent), axis, bit).astype(F32)
        high = (here & bit) != 0
        outside = outside + jnp.where(high != later, coming, 0.0)
        if bit != bits[-1]:
            total = total + coming
    return outside


def early_kernel(q_ref, k_ref, v_ref, maskt_ref, st_ref, kv_ref):
    k = k_ref[...]
    st_ref[0] = (mm(k, q_ref[...], NT) * maskt_ref[...]).astype(BF16)
    kv_ref[0] = mm(k, v_ref[...], TN)


def early(q, k, v, maskt):
    length, width = q.shape
    heads = width // HEAD
    one = pl.BlockSpec((length, HEAD), lambda h: (0, h))
    return pl.pallas_call(
        early_kernel,
        grid=(heads,),
        in_specs=[one, one, one, pl.BlockSpec((length, length), lambda h: (0, 0))],
        out_specs=[
            pl.BlockSpec((1, length, length), lambda h: (h, 0, 0)),
            pl.BlockSpec((1, HEAD, HEAD), lambda h: (h, 0, 0)),
        ],
        out_shape=[
            jax.ShapeDtypeStruct((heads, length, length), BF16),
            jax.ShapeDtypeStruct((heads, HEAD, HEAD), F32),
        ],
        compiler_params=params(),
        name="early",
    )(q, k, v, maskt)


def late_kernel(q_ref, k_ref, v_ref, g_ref, st_ref, prev_ref, mask_ref, maskt_ref, dq_ref, dk_ref, dv_ref):
    q, k, v, g = q_ref[...], k_ref[...], v_ref[...], g_ref[...]
    m = (mm(g, v, NT) * mask_ref[...]).astype(BF16)
    dq_ref[...] = (mm(m, k, NN) + mm(g, prev_ref[0], NT)).astype(BF16)
    mt = (mm(v, g, NT) * maskt_ref[...]).astype(BF16)
    dk_ref[...] = mm(mt, q, NN)
    dv_ref[...] = mm(st_ref[0], g, NN)


def late(q, k, v, g, st, prev, mask, maskt):
    length, width = q.shape
    heads = width // HEAD
    one = pl.BlockSpec((length, HEAD), lambda h: (0, h))
    full = pl.BlockSpec((length, length), lambda h: (0, 0))
    return pl.pallas_call(
        late_kernel,
        grid=(heads,),
        in_specs=[
            one, one, one, one,
            pl.BlockSpec((1, length, length), lambda h: (h, 0, 0)),
            pl.BlockSpec((1, HEAD, HEAD), lambda h: (h, 0, 0)),
            full, full,
        ],
        out_specs=[one, one, one],
        out_shape=[
            jax.ShapeDtypeStruct((length, width), BF16),
            jax.ShapeDtypeStruct((length, width), F32),
            jax.ShapeDtypeStruct((length, width), F32),
        ],
        compiler_params=params(),
        name="late",
    )(q, k, v, g, st, prev, mask, maskt)


def final_kernel(k_ref, v_ref, later_ref, dkp_ref, dvp_ref, dk_ref, dv_ref):
    s = later_ref[0]
    dk_ref[...] = (dkp_ref[...] + mm(v_ref[...], s, NT)).astype(BF16)
    dv_ref[...] = (dvp_ref[...] + mm(k_ref[...], s, NN)).astype(BF16)


def final(k, v, later, dkp, dvp):
    length, width = k.shape
    heads = width // HEAD
    one = pl.BlockSpec((length, HEAD), lambda h: (0, h))
    return pl.pallas_call(
        final_kernel,
        grid=(heads,),
        in_specs=[one, one, pl.BlockSpec((1, HEAD, HEAD), lambda h: (h, 0, 0)), one, one],
        out_specs=[one, one],
        out_shape=[jax.ShapeDtypeStruct((length, width), BF16)] * 2,
        compiler_params=params(),
        name="final",
    )(k, v, later, dkp, dvp)


def fold_kernel(chunk, turns, parts, norm, first, last, *refs):
    refs = list(refs)
    z_ref, own_ref = refs.pop(0), refs.pop(0)
    right_refs = [refs.pop(0) for _ in range(turns - 1)]
    left_refs = [refs.pop(0) for _ in range(turns - 1)]
    w_refs = [refs.pop(0) for _ in range(parts)]
    opened_ref = refs.pop(0)
    acc_ref = None if first else refs.pop(0)
    q_ref = refs.pop(0) if last else None
    og_ref = refs.pop(0)
    qg_ref = refs.pop(0) if last else None
    keep_ref, send_ref, grad, weight, g_sem, w_sem = refs
    z = z_ref[0]
    rows = own_ref.shape[0]
    wide = own_ref.shape[1]
    part = wide // parts

    def place(ref, at):
        pltpu.make_async_copy(ref, grad.at[pl.ds(pl.multiple_of(at * rows, rows), rows)], g_sem).start()

    place(own_ref, z)
    for r in range(1, turns):
        pl.when(z >= r)(functools.partial(place, right_refs[r - 1], z - r))
        pl.when(z + r < turns)(functools.partial(place, left_refs[r - 1], z + r))
    for p in range(parts):
        pltpu.make_async_copy(
            w_refs[p].at[pl.ds(chunk * part, part)], weight.at[pl.ds(p * part, part)], w_sem
        ).start()
    pltpu.make_async_copy(grad, grad, g_sem).wait()
    half = wide // 2
    step = 256
    opened = opened_ref[...]
    for f in range(0, wide, step):
        piece = mm(grad[:, f:f + step], opened, TN) * norm
        if f < half:
            keep_ref[f:f + step, :] = piece
        else:
            send_ref[f - half:f - half + step, :] = piece.astype(BF16)
    pltpu.make_async_copy(weight, weight, w_sem).wait()
    total = mm(grad[...], weight[...], NN)
    if not first:
        total = total + acc_ref[...]
    if last:
        total = total.astype(BF16)
        og_ref[...] = total
        for h in range(total.shape[1] // HEAD):
            at = slice(h * HEAD, (h + 1) * HEAD)
            qg_ref[h] = mm(q_ref[:, at], total[:, at], TN)
    else:
        og_ref[...] = total


def fold(chunk, z, own, rights, lefts, ws, opened, acc, q, norm):
    rows, wide = own.shape
    turns = len(rights) + 1
    length, width = opened.shape
    first, last = acc is None, q is not None
    anyspec = pl.BlockSpec(memory_space=pl.ANY)
    vmem = pl.BlockSpec(memory_space=pltpu.VMEM)
    args = [z, own, *rights, *lefts, *ws, opened]
    specs = [pl.BlockSpec(memory_space=pltpu.SMEM)] + [anyspec] * (len(args) - 2) + [vmem]
    if not first:
        args.append(acc)
        specs.append(vmem)
    if last:
        args.append(q)
        specs.append(vmem)
    outs = [jax.ShapeDtypeStruct((length, width), BF16 if last else F32)]
    if last:
        outs.append(jax.ShapeDtypeStruct((width // HEAD, HEAD, HEAD), F32))
    outs += [
        jax.ShapeDtypeStruct((wide // 2, width), F32),
        jax.ShapeDtypeStruct((wide // 2, width), BF16),
    ]
    return pl.pallas_call(
        functools.partial(fold_kernel, chunk, turns, len(ws), norm, first, last),
        in_specs=specs,
        out_specs=[vmem] * len(outs),
        out_shape=outs,
        scratch_shapes=[
            pltpu.VMEM((length, wide), BF16),
            pltpu.VMEM((wide, width), BF16),
            pltpu.SemaphoreType.DMA,
            pltpu.SemaphoreType.DMA,
        ],
        compiler_params=params(),
        name="fold",
    )(*args)


def shards(queries, keys, values, attn_out, out_grad, out_weight, block_mask):
    ctx, tsp = lax.axis_size("ctx"), lax.axis_size("tsp")
    _, group_len, width = queries.shape
    heads = width // HEAD
    seq_len = group_len * ctx
    sc = 1.0 / math.sqrt(HEAD * seq_len)
    norm = 1.0 / math.sqrt(seq_len * lax.axis_size("dp"))
    me, z = lax.axis_index("ctx"), lax.axis_index("tsp")
    q, k, v, opened = queries[0], keys[0], values[0], attn_out[0]
    grad = out_grad[0]
    rows, model = grad.shape
    order = reversed_order(ctx)
    block = model // ctx
    piece = block // CHUNKS

    own = []
    for c in range(CHUNKS):
        own.append(jnp.concatenate(
            [lax.dynamic_slice(grad, (0, (me ^ j) * block + c * piece), (rows, piece)) for j in order], axis=1))

    held = {0: out_weight}
    for bit in reversed(bits_of(ctx)):
        for j in list(held):
            held[j | bit] = swap(held[j], "ctx", bit)
    ws = [held[j] for j in order]

    merged = tsp >= 4

    def hop(array, r, right):
        if right:
            pairs = [(i, i + 1) for i in range(r - 1, tsp - 1)]
        else:
            pairs = [(i, i - 1) for i in range(1, tsp - r + 1)]
        return lax.ppermute(array, "tsp", pairs)

    rights = [[] for _ in range(CHUNKS)]
    lefts = [[] for _ in range(CHUNKS)]
    for wave in range(CHUNKS + tsp - 2):
        for r in range(1, tsp):
            c = wave - (r - 1)
            if not 0 <= c < CHUNKS:
                continue
            if merged and r == tsp - 1:
                both = jnp.where(z == tsp - 2, rights[c][-1], lefts[c][-1])
                got = lax.ppermute(both, "tsp", [(tsp - 2, tsp - 1), (1, 0)])
                rights[c].append(got)
                lefts[c].append(got)
            else:
                rights[c].append(hop(rights[c][-1] if r > 1 else own[c], r, True))
                lefts[c].append(hop(lefts[c][-1] if r > 1 else own[c], r, False))

    allowed = allowed_pairs(block_mask[0, 0])
    mask = jnp.where(allowed, sc, 0.0).astype(F32)
    maskt = mask.T
    st, kv = early(q, k, v, maskt)
    prev = (scan_states(kv, "ctx", False, F32) * sc).astype(BF16)

    acc = None
    zs = jnp.reshape(z, (1,)).astype(jnp.int32)
    done = []
    for c in range(CHUNKS):
        last = c == CHUNKS - 1
        got = fold(c, zs, own[c], rights[c], lefts[c], ws, opened, acc, q if last else None, norm)
        if last:
            acc, qg, keep, send = got
        else:
            acc, keep, send = got
        for bit in bits_of(ctx):
            coming = swap(send, "ctx", bit).astype(F32)
            total = keep + coming
            if total.shape[0] > piece:
                keep, send = total[: total.shape[0] // 2], total[total.shape[0] // 2:].astype(BF16)
        mine = total.astype(BF16)
        done.append((mine, lax.ppermute(mine, "dp", [(0, 1), (1, 0)])))
    og = acc
    later_sum = scan_states(qg, "ctx", True, BF16)
    dq, dkp, dvp = late(q, k, v, og, st, prev, mask, maskt)
    later = (later_sum * sc).astype(BF16)
    dk, dv = final(k, v, later, dkp, dvp)
    weight_grad = jnp.concatenate([a.astype(F32) + b.astype(F32) for a, b in done], axis=0)
    return dq[None], dk[None], dv[None], weight_grad


def solution(mesh):
    placed = (
        P("dp", "ctx", "tsp"),
        P("dp", "ctx", "tsp"),
        P("dp", "ctx", "tsp"),
        P("dp", "ctx", "tsp"),
        P("dp", ("ctx", "tsp"), None),
        P("ctx", "tsp"),
        P("dp", "ctx", None, None),
    )
    return jax.shard_map(
        shards,
        mesh=mesh,
        in_specs=placed,
        out_specs=(
            P("dp", "ctx", "tsp"),
            P("dp", "ctx", "tsp"),
            P("dp", "ctx", "tsp"),
            P("ctx", "tsp"),
        ),
        check_vma=False,
    )
```

time: 315 us -> 160 us (0.51)
  waiting for transfers between devices: 249 us -> 52.8 us
  starting transfers between devices: 0.42 us -> 52.6 us
  matrix products: 27.1 us -> 0 us
  Pallas kernels: 0 us -> 24.2 us
  between operations: 14.4 us -> 1.57 us
  local copies, waits for them, and re-layouts: 14 us -> 22.1 us
    all_gather x4 -> x0, waiting for transfers between devices: 132 us -> none  [the longest x1 80.7 us: shards(): gathered = lax.all_gather(out_grad, 'tsp', axis=1, tiled=True)]
    reduce_scatter x1 -> x0, waiting for transfers between devices: 63.7 us -> none  [shards(): lax.psum_scatter(product * norm_factor, 'ctx', scatter_dimension=0, tiled...]
    ppermute x0 -> x39, waiting for transfers between devices: none -> 52.8 us  [the longest x16 21.4 us: hop(): return lax.ppermute(array, 'tsp', pairs)]
    psum x1 -> x0, waiting for transfers between devices: 52.7 us -> none  [shards(): weight_grad = lax.psum(partial_grad, 'dp')]
    ppermute x0 -> x39, starting transfers between devices: none -> 52.6 us  [the longest x16 32.3 us: hop(): return lax.ppermute(array, 'tsp', pairs)]
    dot_general x11 -> x0, matrix products: 27.1 us -> none  [the longest x1 8.13 us: shards(): lax.dot_general(columns, opened, (((0,), (0,)), ((), ())), preferred_elem...]
    pallas_call x0 -> x7, Pallas kernels: none -> 24.2 us  [the longest x4 14 us: fold(): pl.pallas_call(functools.partial(fold_kernel, chunk, turns, len(ws), norm...]
    select_n x8 -> x5, other arithmetic: 8.32 us -> 1.47 us  [the longest x1 1.35 us: shards(): mask = jnp.where(allowed, sc, 0.0).astype(F32)]
  transfers between devices with their start and end apart: 6 -> 39, of which waited for: 6 -> 14; matrix products, arithmetic and copies ran while one was open for 14% -> 6% of each run, Pallas kernels for 0% -> 15%
where the time goes in v1:
time: 160 us; the launch traced here: 159 us
  waiting for transfers between devices  52.8 us (33%)
  starting transfers between devices  52.6 us (33%)
  Pallas kernels  24.2 us (15%)
  local copies, waits for them, and re-layouts  22.1 us (14%)
  other arithmetic  5.83 us (4%)
    ppermute x16, starting transfers between devices, hop(): return lax.ppermute(array, 'tsp', pairs)  32.3 us
    ppermute x16, waiting for transfers between devices, hop(): return lax.ppermute(array, 'tsp', pairs)  21.4 us
    ppermute x15, waiting for transfers between devices, swap(): return lax.ppermute(array, axis, [(i, i ^ bit) for i in range(count)])  21 us
    unnamed x102, local copies, waits for them, and re-layouts  15.3 us
    pallas_call x4, Pallas kernels, fold(): pl.pallas_call(functools.partial(fold_kernel, chunk, turns, len(ws), norm...  14 us
    ppermute x15, starting transfers between devices, swap(): return lax.ppermute(array, axis, [(i, i ^ bit) for i in range(count)])  8.65 us
    ppermute x4, starting transfers between devices, shards(): done.append((mine, lax.ppermute(mine, 'dp', [(0, 1), (1, 0)])))  6.33 us
    ppermute x4, waiting for transfers between devices, shards(): done.append((mine, lax.ppermute(mine, 'dp', [(0, 1), (1, 0)])))  6.11 us
  transfers between devices with their start and end apart: 39, of which 14 were waited for; matrix products, arithmetic and copies ran while one was open for 6% of the time, Pallas kernels for 15%

profile of v1, /device:TPU:0, one launch (start us, length us, event | category | flops | bytes accessed | tf_op | source)
XLA Modules:
  0.0 159.0 jit_solution(1612546001523762109)
XLA Ops:
  2.2 4.9 %collective-permute-start.18 = (bf16[128,1024]{1,0:T(8,128)(2,1)S(1)}, bf16[128,1024]{1,0:T(8,128)(2,1)S(1)}, u32[]{:S(2)}, u32[]{:S(2)}) collective-permute-start(bf16[128,1024]{1,0:T(8,128)(2,1)S(1)} %pad_maximum_fusion.4.refs_1_), channel_id=1, source_target_pairs={{0,2},{2,4},{4,6},{1,3},{3,5},{5,7},{8,10},{10,12},{12,14},{9,11},... | collective-permute-start | bytes 786440 | tf_op jit(solution)/shard_map/ppermute | solution.py:278
  8.5 4.6 %collective-permute-start.13 = (bf16[128,1024]{1,0:T(8,128)(2,1)S(1)}, bf16[128,1024]{1,0:T(8,128)(2,1)S(1)}, u32[]{:S(2)}, u32[]{:S(2)}) collective-permute-start(bf16[128,1024]{1,0:T(8,128)(2,1)S(1)} %pad_maximum_fusion.3.refs_1_), channel_id=1, source_target_pairs={{0,2},{2,4},{4,6},{1,3},{3,5},{5,7},{8,10},{10,12},{12,14},{9,11},... | collective-permute-start | bytes 786440 | tf_op jit(solution)/shard_map/ppermute | solution.py:278
  14.4 1.6 collective-permute-start.5
  17.3 5.9 %collective-permute-start.8 = (bf16[128,1024]{1,0:T(8,128)(2,1)S(1)}, bf16[128,1024]{1,0:T(8,128)(2,1)}, u32[]{:S(2)}, u32[]{:S(2)}) collective-permute-start(bf16[128,1024]{1,0:T(8,128)(2,1)S(1)} %pad_maximum_fusion.2.refs_1_), channel_id=1, source_target_pairs={{0,2},{2,4},{4,6},{1,3},{3,5},{5,7},{8,10},{10,12},{12,14},{9,11},... | collective-permute-start | bytes 786440 | tf_op jit(solution)/shard_map/ppermute | solution.py:278
  23.2 4.0 %collective-permute-start = (bf16[128,1024]{1,0:T(8,128)(2,1)S(1)}, bf16[128,1024]{1,0:T(8,128)(2,1)}, u32[]{:S(2)}, u32[]{:S(2)}) collective-permute-start(bf16[128,1024]{1,0:T(8,128)(2,1)S(1)} %pad_maximum_fusion.1.refs_1_), channel_id=1, source_target_pairs={{0,2},{2,4},{4,6},{1,3},{3,5},{5,7},{8,10},{10,12},{12,14},{9,11},... | collective-permute-start | bytes 786440 | tf_op jit(solution)/shard_map/ppermute | solution.py:278
  30.5 1.8 %collective-permute-done.refs_2_ = bf16[128,1024]{1,0:T(8,128)(2,1)} collective-permute-done((bf16[128,1024]{1,0:T(8,128)(2,1)S(1)}, bf16[128,1024]{1,0:T(8,128)(2,1)}, u32[]{:S(2)}, u32[]{:S(2)}) %collective-permute-start) | collective-permute-done | bytes 262176 | tf_op jit(solution)/shard_map/ppermute | solution.py:278
  33.0 2.8 %collective-permute-done.2.refs_5_ = bf16[128,1024]{1,0:T(8,128)(2,1)} collective-permute-done((bf16[128,1024]{1,0:T(8,128)(2,1)S(1)}, bf16[128,1024]{1,0:T(8,128)(2,1)}, u32[]{:S(2)}, u32[]{:S(2)}) %collective-permute-start.2) | collective-permute-done | bytes 262176 | tf_op jit(solution)/shard_map/ppermute | solution.py:278
  39.5 2.4 %eq.32 = pred[512,512]{0,1:T(8,128)(4,1)} reshape(pred[8,64,8,64]{1,0,3,2:T(8,128)(4,1)} %broadcast_in_dim.31) | data formatting | bytes 524288 | tf_op jit(solution)/shard_map/eq | solution.py:40
  42.8 6.9 %collective-permute-done.16.refs_6_ = bf16[128,1024]{1,0:T(8,128)(2,1)S(1)} collective-permute-done((bf16[128,1024]{1,0:T(8,128)(2,1)}, bf16[128,1024]{1,0:T(8,128)(2,1)S(1)}, u32[]{:S(2)}, u32[]{:S(2)}) %collective-permute-start.16) | collective-permute-done | bytes 262176 | tf_op jit(solution)/shard_map/ppermute | solution.py:278
  50.4 2.1 %collective-permute-done.11.refs_6_ = bf16[128,1024]{1,0:T(8,128)(2,1)S(1)} collective-permute-done((bf16[128,1024]{1,0:T(8,128)(2,1)}, bf16[128,1024]{1,0:T(8,128)(2,1)S(1)}, u32[]{:S(2)}, u32[]{:S(2)}) %collective-permute-start.11) | collective-permute-done | bytes 262176 | tf_op jit(solution)/shard_map/ppermute | solution.py:278
  57.6 7.6 %collective-permute-done.3.refs_6_ = bf16[128,1024]{1,0:T(8,128)(2,1)S(1)} collective-permute-done((bf16[128,1024]{1,0:T(8,128)(2,1)}, bf16[128,1024]{1,0:T(8,128)(2,1)S(1)}, u32[]{:S(2)}, u32[]{:S(2)}) %collective-permute-start.3) | collective-permute-done | bytes 262176 | tf_op jit(solution)/shard_map/ppermute | solution.py:278
  66.5 4.2 %collective-permute-done.22.refs_4_.refs_7_ = bf16[128,1024]{1,0:T(8,128)(2,1)S(1)} collective-permute-done((bf16[128,1024]{1,0:T(8,128)(2,1)S(1)}, bf16[128,1024]{1,0:T(8,128)(2,1)S(1)}, u32[]{:S(2)}, u32[]{:S(2)}) %collective-permute-start.22) | collective-permute-done | bytes 262176 | tf_op jit(solution)/shard_map/ppermute | solution.py:289
  73.4 1.7 %early.1 = (bf16[4,512,512]{2,1,0:T(8,128)(2,1)S(1)}, f32[4,128,128]{2,1,0:T(8,128)S(1)}) custom-call(bf16[512,512]{1,0:T(8,128)(2,1)S(1)} %bitcast.52, bf16[512,512]{1,0:T(8,128)(2,1)S(1)} %bitcast.55, bf16[512,512]{1,0:T(8,128)(2,1)S(1)} %bitcast.58, f32[512,512]{1,0:T(8,128)S(1)} %get-tuple-element.61.maskt_ref), custom_call_target="tpu_custom_call" | custom-call | tf_op jit(solution)/shard_map/early/pallas_call | solution.py:83
  77.8 2.6 %fold.4 = (f32[512,512]{1,0:T(8,128)S(1)}, f32[512,512]{1,0:T(8,128)S(1)}, bf16[512,512]{1,0:T(8,128)(2,1)S(1)}) custom-call(s32[1]{0:T(128)} %bitcast.3.refs_0_, bf16[128,1024]{1,0:T(8,128)(2,1)S(1)} %copy-done.30, bf16[128,1024]{1,0:T(8,128)(2,1)S(1)} %copy-done.40, bf16[128,1024]{1,0:T(8,128)(2,1)S(1)} %copy-done.32, ...), custom_call_target="tpu_custom_call" | custom-call | tf_op jit(solution)/shard_map/fold/pallas_call | solution.py:229
  83.4 3.8 %fold.5 = (f32[512,512]{1,0:T(8,128)S(1)}, f32[512,512]{1,0:T(8,128)S(1)}, bf16[512,512]{1,0:T(8,128)(2,1)S(1)}) custom-call(s32[1]{0:T(128)} %bitcast.3.refs_0_, bf16[128,1024]{1,0:T(8,128)(2,1)S(1)} %copy-done.9, bf16[128,1024]{1,0:T(8,128)(2,1)S(1)} %copy-done.38, bf16[128,1024]{1,0:T(8,128)(2,1)S(1)} %copy-done.21, ...), custom_call_target="tpu_custom_call" | custom-call | tf_op jit(solution)/shard_map/fold/pallas_call | solution.py:229
  90.1 3.7 %fold.6 = (f32[512,512]{1,0:T(8,128)S(1)}, f32[512,512]{1,0:T(8,128)S(1)}, bf16[512,512]{1,0:T(8,128)(2,1)S(1)}) custom-call(s32[1]{0:T(128)} %bitcast.3.refs_0_, bf16[128,1024]{1,0:T(8,128)(2,1)S(1)} %copy-done.11, bf16[128,1024]{1,0:T(8,128)(2,1)} %collective-permute-done.8.refs_2_, bf16[128,1024]{1,0:T(8,128)(2,1)S(1)} %collective-permute-done.9.refs_3_, ...), custom_call_target="tpu_custom_call" | custom-call | tf_op jit(solution)/shard_map/fold/pallas_call | solution.py:229
  96.6 4.0 %fold.7 = (bf16[512,512]{1,0:T(8,128)(2,1)S(1)}, f32[4,128,128]{2,1,0:T(8,128)S(1)}, f32[512,512]{1,0:T(8,128)S(1)}, bf16[512,512]{1,0:T(8,128)(2,1)S(1)}) custom-call(s32[1]{0:T(128)} %bitcast.3.refs_0_, bf16[128,1024]{1,0:T(8,128)(2,1)S(1)} %pad_maximum_fusion.1.refs_1_, bf16[128,1024]{1,0:T(8,128)(2,1)} %collective-permute-done.refs_2_, ...), custom_call_target="tpu_custom_call" | custom-call | tf_op jit(solution)/shard_map/fold/pallas_call | solution.py:229
  104.5 1.6 %copy.12.mask_ref = f32[512,512]{1,0:T(8,128)S(1)} copy(f32[512,512]{0,1:T(8,128)} %get-tuple-element.60) | data formatting | bytes 2097152 | tf_op jit(solution)/shard_map/jit(_where)/select_n | solution.py:297
  106.4 1.6 collective-permute-start.26
  108.0 5.4 %collective-permute-done.24 = f32[4,128,128]{2,1,0:T(8,128)S(1)} collective-permute-done((f32[4,128,128]{2,1,0:T(8,128)}, f32[4,128,128]{2,1,0:T(8,128)S(1)}, u32[]{:S(2)}, u32[]{:S(2)}) %collective-permute-start.24) | collective-permute-done | bytes 262176 | tf_op jit(solution)/shard_map/ppermute | solution.py:57
  115.1 6.1 %late.1 = (bf16[512,512]{1,0:T(8,128)(2,1)}, f32[512,512]{1,0:T(8,128)S(1)}, f32[512,512]{1,0:T(8,128)S(1)}) custom-call(bf16[512,512]{1,0:T(8,128)(2,1)S(1)} %bitcast.54, bf16[512,512]{1,0:T(8,128)(2,1)S(1)} %bitcast.56, bf16[512,512]{1,0:T(8,128)(2,1)S(1)} %bitcast.59, bf16[512,512]{1,0:T(8,128)(2,1)S(1)} %copy-done.36, bf16[4,512,512]{2,1,0:T(8,128)(2,1)} %copy-done.7, ...), custom_call_target="tpu_custom_call" | custom-call | tf_op jit(solution)/shard_map/late/pallas_call | solution.py:114
  121.2 2.5 %final.1 = (bf16[512,512]{1,0:T(8,128)(2,1)}, bf16[512,512]{1,0:T(8,128)(2,1)}) custom-call(bf16[512,512]{1,0:T(8,128)(2,1)S(1)} %bitcast.57, bf16[512,512]{1,0:T(8,128)(2,1)S(1)} %bitcast.60, bf16[4,128,128]{2,1,0:T(8,128)(2,1)S(1)} %fusion.9.later_ref, f32[512,512]{1,0:T(8,128)S(1)} %get-tuple-element.32.dkp_ref, f32[512,512]{1,0:T(8,128)S(1)} %get-tuple-element.33.dvp_ref), custom_call_target="tpu_custom_call" | custom-call | tf_op jit(solution)/shard_map/final/pallas_call | solution.py:144
  128.8 4.2 %collective-permute-done.28 = bf16[256,512]{1,0:T(8,128)(2,1)S(1)} collective-permute-done((bf16[256,512]{1,0:T(8,128)(2,1)S(1)}, bf16[256,512]{1,0:T(8,128)(2,1)S(1)}, u32[]{:S(2)}, u32[]{:S(2)}) %collective-permute-start.28) | collective-permute-done | bytes 262176 | tf_op jit(solution)/shard_map/ppermute | solution.py:57
  133.1 1.6 collective-permute-start.29
  134.7 4.0 %collective-permute-done.31 = bf16[256,512]{1,0:T(8,128)(2,1)S(1)} collective-permute-done((bf16[256,512]{1,0:T(8,128)(2,1)S(1)}, bf16[256,512]{1,0:T(8,128)(2,1)S(1)}, u32[]{:S(2)}, u32[]{:S(2)}) %collective-permute-start.31) | collective-permute-done | bytes 262176 | tf_op jit(solution)/shard_map/ppermute | solution.py:57
  138.8 1.6 collective-permute-start.32
  140.3 4.0 %collective-permute-done.34 = bf16[256,512]{1,0:T(8,128)(2,1)S(1)} collective-permute-done((bf16[256,512]{1,0:T(8,128)(2,1)S(1)}, bf16[256,512]{1,0:T(8,128)(2,1)S(1)}, u32[]{:S(2)}, u32[]{:S(2)}) %collective-permute-start.34) | collective-permute-done | bytes 262176 | tf_op jit(solution)/shard_map/ppermute | solution.py:57
  144.4 1.6 collective-permute-start.35
  146.0 3.5 %collective-permute-done.37 = bf16[256,512]{1,0:T(8,128)(2,1)S(1)} collective-permute-done((bf16[256,512]{1,0:T(8,128)(2,1)S(1)}, bf16[256,512]{1,0:T(8,128)(2,1)S(1)}, u32[]{:S(2)}, u32[]{:S(2)}) %collective-permute-start.37) | collective-permute-done | bytes 262176 | tf_op jit(solution)/shard_map/ppermute | solution.py:57
  149.5 1.6 collective-permute-start.38
  151.9 5.6 %collective-permute-done.38 = bf16[256,512]{1,0:T(8,128)(2,1)S(1)} collective-permute-done((bf16[256,512]{1,0:T(8,128)(2,1)S(1)}, bf16[256,512]{1,0:T(8,128)(2,1)S(1)}, u32[]{:S(2)}, u32[]{:S(2)}) %collective-permute-start.38) | collective-permute-done | bytes 262176 | tf_op jit(solution)/shard_map/ppermute | solution.py:318
  157.5 1.5 pad_maximum_fusion
  (193 shorter events, 46.9 us)
Async XLA Ops:
  2.2 13.8 %collective-permute-start.18 = (bf16[128,1024]{1,0:T(8,128)(2,1)S(1)}, bf16[128,1024]{1,0:T(8,128)(2,1)S(1)}, u32[]{:S(2)}, u32[]{:S(2)}) collective-permute-start(bf16[128,1024]{1,0:T(8,128)(2,1)S(1)} %pad_maximum_fusion.4.refs_1_), channel_id=1, source_target_pairs={{0,2},{2,4},{4,6},{1,3},{3,5},{5,7},{8,10},{10,12},{12,14},{9,11},... | collective-permute-start | bytes 786440 | tf_op jit(solution)/shard_map/ppermute | solution.py:278
  7.2 10.2 %collective-permute-start.20 = (bf16[128,1024]{1,0:T(8,128)(2,1)S(1)}, bf16[128,1024]{1,0:T(8,128)(2,1)}, u32[]{:S(2)}, u32[]{:S(2)}) collective-permute-start(bf16[128,1024]{1,0:T(8,128)(2,1)S(1)} %pad_maximum_fusion.4.refs_1_), channel_id=1, source_target_pairs={{2,0},{4,2},{6,4},{3,1},{5,3},{7,5},{10,8},{12,10},{14,12},{11,9},... | collective-permute-start | bytes 786440 | tf_op jit(solution)/shard_map/ppermute | solution.py:278
  8.5 14.7 %collective-permute-start.13 = (bf16[128,1024]{1,0:T(8,128)(2,1)S(1)}, bf16[128,1024]{1,0:T(8,128)(2,1)S(1)}, u32[]{:S(2)}, u32[]{:S(2)}) collective-permute-start(bf16[128,1024]{1,0:T(8,128)(2,1)S(1)} %pad_maximum_fusion.3.refs_1_), channel_id=1, source_target_pairs={{0,2},{2,4},{4,6},{1,3},{3,5},{5,7},{8,10},{10,12},{12,14},{9,11},... | collective-permute-start | bytes 786440 | tf_op jit(solution)/shard_map/ppermute | solution.py:278
  13.1 14.1 %collective-permute-start.15 = (bf16[128,1024]{1,0:T(8,128)(2,1)S(1)}, bf16[128,1024]{1,0:T(8,128)(2,1)}, u32[]{:S(2)}, u32[]{:S(2)}) collective-permute-start(bf16[128,1024]{1,0:T(8,128)(2,1)S(1)} %pad_maximum_fusion.3.refs_1_), channel_id=1, source_target_pairs={{2,0},{4,2},{6,4},{3,1},{5,3},{7,5},{10,8},{12,10},{14,12},{11,9},... | collective-permute-start | bytes 786440 | tf_op jit(solution)/shard_map/ppermute | solution.py:278
  14.4 39.5 %collective-permute-start.5 = (bf16[1024,512]{1,0:T(8,128)(2,1)S(1)}, bf16[1024,512]{1,0:T(8,128)(2,1)}, u32[]{:S(2)}, u32[]{:S(2)}) collective-permute-start(bf16[1024,512]{1,0:T(8,128)(2,1)S(1)} %copy-done), channel_id=1, source_target_pairs={{0,16},{8,24},{16,0},{24,8},{1,17},{9,25},{17,1},{25,9},{2,18},{10... | collective-permute-start | bytes 3145736 | tf_op jit(solution)/shard_map/ppermute | solution.py:57
  16.0 12.5 %collective-permute-start.10 = (bf16[128,1024]{1,0:T(8,128)(2,1)S(1)}, bf16[128,1024]{1,0:T(8,128)(2,1)}, u32[]{:S(2)}, u32[]{:S(2)}) collective-permute-start(bf16[128,1024]{1,0:T(8,128)(2,1)S(1)} %pad_maximum_fusion.2.refs_1_), channel_id=1, source_target_pairs={{2,0},{4,2},{6,4},{3,1},{5,3},{7,5},{10,8},{12,10},{14,12},{11,9},... | collective-permute-start | bytes 786440 | tf_op jit(solution)/shard_map/ppermute | solution.py:278
  17.3 11.8 %collective-permute-start.8 = (bf16[128,1024]{1,0:T(8,128)(2,1)S(1)}, bf16[128,1024]{1,0:T(8,128)(2,1)}, u32[]{:S(2)}, u32[]{:S(2)}) collective-permute-start(bf16[128,1024]{1,0:T(8,128)(2,1)S(1)} %pad_maximum_fusion.2.refs_1_), channel_id=1, source_target_pairs={{0,2},{2,4},{4,6},{1,3},{3,5},{5,7},{8,10},{10,12},{12,14},{9,11},... | collective-permute-start | bytes 786440 | tf_op jit(solution)/shard_map/ppermute | solution.py:278
  29.2 12.9 %collective-permute-start.21 = (bf16[128,1024]{1,0:T(8,128)(2,1)}, bf16[128,1024]{1,0:T(8,128)(2,1)S(1)}, u32[]{:S(2)}, u32[]{:S(2)}) collective-permute-start(bf16[128,1024]{1,0:T(8,128)(2,1)} %collective-permute-done.20.refs_5_), channel_id=1, source_target_pairs={{2,0},{4,2},{3,1},{5,3},{10,8},{12,10},{11,9},{13,11},{18,16},{20,... | collective-permute-start | bytes 786440 | tf_op jit(solution)/shard_map/ppermute | solution.py:278
  32.3 9.8 %collective-permute-start.14 = (bf16[128,1024]{1,0:T(8,128)(2,1)S(1)}, bf16[128,1024]{1,0:T(8,128)(2,1)S(1)}, u32[]{:S(2)}, u32[]{:S(2)}) collective-permute-start(bf16[128,1024]{1,0:T(8,128)(2,1)S(1)} %collective-permute-done.13.refs_2_), channel_id=1, source_target_pairs={{2,4},{4,6},{3,5},{5,7},{10,12},{12,14},{11,13},{13,15},{18,20},{2... | collective-permute-start | bytes 786440 | tf_op jit(solution)/shard_map/ppermute | solution.py:278
  35.8 14.0 %collective-permute-start.16 = (bf16[128,1024]{1,0:T(8,128)(2,1)}, bf16[128,1024]{1,0:T(8,128)(2,1)S(1)}, u32[]{:S(2)}, u32[]{:S(2)}) collective-permute-start(bf16[128,1024]{1,0:T(8,128)(2,1)} %collective-permute-done.15.refs_5_), channel_id=1, source_target_pairs={{2,0},{4,2},{3,1},{5,3},{10,8},{12,10},{11,9},{13,11},{18,16},{20,... | collective-permute-start | bytes 786440 | tf_op jit(solution)/shard_map/ppermute | solution.py:278
  37.1 15.5 %collective-permute-start.11 = (bf16[128,1024]{1,0:T(8,128)(2,1)}, bf16[128,1024]{1,0:T(8,128)(2,1)S(1)}, u32[]{:S(2)}, u32[]{:S(2)}) collective-permute-start(bf16[128,1024]{1,0:T(8,128)(2,1)} %collective-permute-done.10.refs_5_), channel_id=1, source_target_pairs={{2,0},{4,2},{3,1},{5,3},{10,8},{12,10},{11,9},{13,11},{18,16},{20,... | collective-permute-start | bytes 786440 | tf_op jit(solution)/shard_map/ppermute | solution.py:278
  42.1 34.4 %collective-permute-start.6 = (bf16[1024,512]{1,0:T(8,128)(2,1)S(1)}, bf16[1024,512]{1,0:T(8,128)(2,1)S(1)}, u32[]{:S(2)}, u32[]{:S(2)}) collective-permute-start(bf16[1024,512]{1,0:T(8,128)(2,1)S(1)} %copy-done), channel_id=1, source_target_pairs={{0,8},{8,0},{16,24},{24,16},{1,9},{9,1},{17,25},{25,17},{2,10},{10... | collective-permute-start | bytes 3145736 | tf_op jit(solution)/shard_map/ppermute | solution.py:57
  42.1 12.7 %collective-permute-start.9 = (bf16[128,1024]{1,0:T(8,128)(2,1)}, bf16[128,1024]{1,0:T(8,128)(2,1)S(1)}, u32[]{:S(2)}, u32[]{:S(2)}) collective-permute-start(bf16[128,1024]{1,0:T(8,128)(2,1)} %collective-permute-done.8.refs_2_), channel_id=1, source_target_pairs={{2,4},{4,6},{3,5},{5,7},{10,12},{12,14},{11,13},{13,15},{18,20},{2... | collective-permute-start | bytes 786440 | tf_op jit(solution)/shard_map/ppermute | solution.py:278
  52.6 12.5 %collective-permute-start.3 = (bf16[128,1024]{1,0:T(8,128)(2,1)}, bf16[128,1024]{1,0:T(8,128)(2,1)S(1)}, u32[]{:S(2)}, u32[]{:S(2)}) collective-permute-start(bf16[128,1024]{1,0:T(8,128)(2,1)} %collective-permute-done.2.refs_5_), channel_id=1, source_target_pairs={{2,0},{4,2},{3,1},{5,3},{10,8},{12,10},{11,9},{13,11},{18,16},{20,... | collective-permute-start | bytes 786440 | tf_op jit(solution)/shard_map/ppermute | solution.py:278
  53.9 22.6 %collective-permute-start.7 = (bf16[1024,512]{1,0:T(8,128)(2,1)}, bf16[1024,512]{1,0:T(8,128)(2,1)S(1)}, u32[]{:S(2)}, u32[]{:S(2)}) collective-permute-start(bf16[1024,512]{1,0:T(8,128)(2,1)} %collective-permute-done.5.refs_9_), channel_id=1, source_target_pairs={{0,8},{8,0},{16,24},{24,16},{1,9},{9,1},{17,25},{25,17},{2,10},{10... | collective-permute-start | bytes 3145736 | tf_op jit(solution)/shard_map/ppermute | solution.py:57
  54.8 16.0 %collective-permute-start.22 = (bf16[128,1024]{1,0:T(8,128)(2,1)S(1)}, bf16[128,1024]{1,0:T(8,128)(2,1)S(1)}, u32[]{:S(2)}, u32[]{:S(2)}) collective-permute-start(bf16[128,1024]{1,0:T(8,128)(2,1)S(1)} %broadcast_select_fusion), channel_id=1, source_target_pairs={{4,6},{2,0},{5,7},{3,1},{12,14},{10,8},{13,15},{11,9},{20,22},{18,... | collective-permute-start | bytes 786440 | tf_op jit(solution)/shard_map/ppermute | solution.py:289
  56.3 26.3 %collective-permute-start.17 = (bf16[128,1024]{1,0:T(8,128)(2,1)S(1)}, bf16[128,1024]{1,0:T(8,128)(2,1)S(1)}, u32[]{:S(2)}, u32[]{:S(2)}) collective-permute-start(bf16[128,1024]{1,0:T(8,128)(2,1)S(1)} %broadcast_select_fusion.1), channel_id=1, source_target_pairs={{4,6},{2,0},{5,7},{3,1},{12,14},{10,8},{13,15},{11,9},{20,22},{18,... | collective-permute-start | bytes 786440 | tf_op jit(solution)/shard_map/ppermute | solution.py:289
  65.1 24.2 %collective-permute-start.12 = (bf16[128,1024]{1,0:T(8,128)(2,1)S(1)}, bf16[128,1024]{1,0:T(8,128)(2,1)S(1)}, u32[]{:S(2)}, u32[]{:S(2)}) collective-permute-start(bf16[128,1024]{1,0:T(8,128)(2,1)S(1)} %broadcast_select_fusion.2), channel_id=1, source_target_pairs={{4,6},{2,0},{5,7},{3,1},{12,14},{10,8},{13,15},{11,9},{20,22},{18,... | collective-permute-start | bytes 786440 | tf_op jit(solution)/shard_map/ppermute | solution.py:289
  70.7 25.9 %collective-permute-start.4 = (bf16[128,1024]{1,0:T(8,128)(2,1)S(1)}, bf16[128,1024]{1,0:T(8,128)(2,1)S(1)}, u32[]{:S(2)}, u32[]{:S(2)}) collective-permute-start(bf16[128,1024]{1,0:T(8,128)(2,1)S(1)} %broadcast_select_fusion.3), channel_id=1, source_target_pairs={{4,6},{2,0},{5,7},{3,1},{12,14},{10,8},{13,15},{11,9},{20,22},{18,... | collective-permute-start | bytes 786440 | tf_op jit(solution)/shard_map/ppermute | solution.py:289
  76.4 26.8 %collective-permute-start.23 = (f32[4,128,128]{2,1,0:T(8,128)S(1)}, f32[4,128,128]{2,1,0:T(8,128)S(1)}, u32[]{:S(2)}, u32[]{:S(2)}) collective-permute-start(f32[4,128,128]{2,1,0:T(8,128)S(1)} %get-tuple-element.29), channel_id=1, source_target_pairs={{0,8},{8,0},{16,24},{24,16},{1,9},{9,1},{17,25},{25,17},{2,10},{10... | collective-permute-start | bytes 786440 | tf_op jit(solution)/shard_map/ppermute | solution.py:57
  104.0 9.3 %collective-permute-start.24 = (f32[4,128,128]{2,1,0:T(8,128)}, f32[4,128,128]{2,1,0:T(8,128)S(1)}, u32[]{:S(2)}, u32[]{:S(2)}) collective-permute-start(f32[4,128,128]{2,1,0:T(8,128)} %add.196), channel_id=1, source_target_pairs={{0,16},{8,24},{16,0},{24,8},{1,17},{9,25},{17,1},{25,9},{2,18},{10... | collective-permute-start | bytes 786440 | tf_op jit(solution)/shard_map/ppermute | solution.py:57
  106.1 17.5 %collective-permute-start.27 = (bf16[512,512]{1,0:T(8,128)(2,1)}, bf16[512,512]{1,0:T(8,128)(2,1)S(1)}, u32[]{:S(2)}, u32[]{:S(2)}) collective-permute-start(bf16[512,512]{1,0:T(8,128)(2,1)} %copy-done.41), channel_id=1, source_target_pairs={{0,8},{8,0},{16,24},{24,16},{1,9},{9,1},{17,25},{25,17},{2,10},{10... | collective-permute-start | bytes 1572872 | tf_op jit(solution)/shard_map/ppermute | solution.py:57
  106.4 14.8 %collective-permute-start.26 = (bf16[4,128,128]{2,1,0:T(8,128)(2,1)S(1)}, bf16[4,128,128]{2,1,0:T(8,128)(2,1)S(1)}, u32[]{:S(2)}, u32[]{:S(2)}) collective-permute-start(bf16[4,128,128]{2,1,0:T(8,128)(2,1)S(1)} %fusion.10), channel_id=1, source_target_pairs={{0,16},{8,24},{16,0},{24,8},{1,17},{9,25},{17,1},{25,9},{2,18},{10... | collective-permute-start | bytes 393224 | tf_op jit(solution)/shard_map/ppermute | solution.py:57
  113.4 11.1 %collective-permute-start.30 = (bf16[512,512]{1,0:T(8,128)(2,1)}, bf16[512,512]{1,0:T(8,128)(2,1)S(1)}, u32[]{:S(2)}, u32[]{:S(2)}) collective-permute-start(bf16[512,512]{1,0:T(8,128)(2,1)} %copy-done.42), channel_id=1, source_target_pairs={{0,8},{8,0},{16,24},{24,16},{1,9},{9,1},{17,25},{25,17},{2,10},{10... | collective-permute-start | bytes 1572872 | tf_op jit(solution)/shard_map/ppermute | solution.py:57
  113.4 12.8 %collective-permute-start.33 = (bf16[512,512]{1,0:T(8,128)(2,1)}, bf16[512,512]{1,0:T(8,128)(2,1)S(1)}, u32[]{:S(2)}, u32[]{:S(2)}) collective-permute-start(bf16[512,512]{1,0:T(8,128)(2,1)} %copy-done.43), channel_id=1, source_target_pairs={{0,8},{8,0},{16,24},{24,16},{1,9},{9,1},{17,25},{25,17},{2,10},{10... | collective-permute-start | bytes 1572872 | tf_op jit(solution)/shard_map/ppermute | solution.py:57
  113.9 13.5 %collective-permute-start.36 = (bf16[512,512]{1,0:T(8,128)(2,1)}, bf16[512,512]{1,0:T(8,128)(2,1)S(1)}, u32[]{:S(2)}, u32[]{:S(2)}) collective-permute-start(bf16[512,512]{1,0:T(8,128)(2,1)} %copy-done.44), channel_id=1, source_target_pairs={{0,8},{8,0},{16,24},{24,16},{1,9},{9,1},{17,25},{25,17},{2,10},{10... | collective-permute-start | bytes 1572872 | tf_op jit(solution)/shard_map/ppermute | solution.py:57
  123.9 9.2 %collective-permute-start.28 = (bf16[256,512]{1,0:T(8,128)(2,1)S(1)}, bf16[256,512]{1,0:T(8,128)(2,1)S(1)}, u32[]{:S(2)}, u32[]{:S(2)}) collective-permute-start(bf16[256,512]{1,0:T(8,128)(2,1)S(1)} %slice.63), channel_id=1, source_target_pairs={{0,16},{8,24},{16,0},{24,8},{1,17},{9,25},{17,1},{25,9},{2,18},{10... | collective-permute-start | bytes 786440 | tf_op jit(solution)/shard_map/ppermute | solution.py:57
  125.1 13.6 %collective-permute-start.31 = (bf16[256,512]{1,0:T(8,128)(2,1)S(1)}, bf16[256,512]{1,0:T(8,128)(2,1)S(1)}, u32[]{:S(2)}, u32[]{:S(2)}) collective-permute-start(bf16[256,512]{1,0:T(8,128)(2,1)S(1)} %slice.62), channel_id=1, source_target_pairs={{0,16},{8,24},{16,0},{24,8},{1,17},{9,25},{17,1},{25,9},{2,18},{10... | collective-permute-start | bytes 786440 | tf_op jit(solution)/shard_map/ppermute | solution.py:57
  126.5 17.8 %collective-permute-start.34 = (bf16[256,512]{1,0:T(8,128)(2,1)S(1)}, bf16[256,512]{1,0:T(8,128)(2,1)S(1)}, u32[]{:S(2)}, u32[]{:S(2)}) collective-permute-start(bf16[256,512]{1,0:T(8,128)(2,1)S(1)} %slice.61), channel_id=1, source_target_pairs={{0,16},{8,24},{16,0},{24,8},{1,17},{9,25},{17,1},{25,9},{2,18},{10... | collective-permute-start | bytes 786440 | tf_op jit(solution)/shard_map/ppermute | solution.py:57
  127.7 21.8 %collective-permute-start.37 = (bf16[256,512]{1,0:T(8,128)(2,1)S(1)}, bf16[256,512]{1,0:T(8,128)(2,1)S(1)}, u32[]{:S(2)}, u32[]{:S(2)}) collective-permute-start(bf16[256,512]{1,0:T(8,128)(2,1)S(1)} %slice.60), channel_id=1, source_target_pairs={{0,16},{8,24},{16,0},{24,8},{1,17},{9,25},{17,1},{25,9},{2,18},{10... | collective-permute-start | bytes 786440 | tf_op jit(solution)/shard_map/ppermute | solution.py:57
  133.1 18.0 %collective-permute-start.29 = (bf16[256,512]{1,0:T(8,128)(2,1)S(1)}, bf16[256,512]{1,0:T(8,128)(2,1)S(1)}, u32[]{:S(2)}, u32[]{:S(2)}) collective-permute-start(bf16[256,512]{1,0:T(8,128)(2,1)S(1)} %fusion.6), channel_id=1, source_target_pairs={{0,1},{1,0},{2,3},{3,2},{4,5},{5,4},{6,7},{7,6},{8,9},{9,8},{10,11... | collective-permute-start | bytes 786440 | tf_op jit(solution)/shard_map/ppermute | solution.py:318
  138.8 12.4 %collective-permute-start.32 = (bf16[256,512]{1,0:T(8,128)(2,1)S(1)}, bf16[256,512]{1,0:T(8,128)(2,1)S(1)}, u32[]{:S(2)}, u32[]{:S(2)}) collective-permute-start(bf16[256,512]{1,0:T(8,128)(2,1)S(1)} %fusion.5), channel_id=1, source_target_pairs={{0,1},{1,0},{2,3},{3,2},{4,5},{5,4},{6,7},{7,6},{8,9},{9,8},{10,11... | collective-permute-start | bytes 786440 | tf_op jit(solution)/shard_map/ppermute | solution.py:318
  (58 other events, 572.8 us)

commit v2 on v0

v2 whole, which is shorter than its diff:
```python
import functools
import math

import jax
import jax.numpy as jnp
from jax import lax
from jax.experimental import pallas as pl
from jax.experimental.pallas import tpu as pltpu
from jax.sharding import PartitionSpec as P

HEAD = 128
BLK = 64
EIGHTHS = (3, 2, 2, 1)
CORE_SENDS = (4, 4, 8, 1)
F32 = jnp.float32
BF16 = jnp.bfloat16
NT = (((1,), (1,)), ((), ()))
NN = (((1,), (0,)), ((), ()))
TN = (((0,), (0,)), ((), ()))
ANY = pl.BlockSpec(memory_space=pl.ANY)
SMEM = pl.BlockSpec(memory_space=pltpu.SMEM)
VMEM = pl.BlockSpec(memory_space=pltpu.VMEM)
HBM = pl.BlockSpec(memory_space=pltpu.HBM)


def mm(a, b, dims):
    return lax.dot_general(a, b, dims, preferred_element_type=F32)


def params(mebibytes=16):
    return pltpu.CompilerParams(vmem_limit_bytes=mebibytes * 1024 * 1024)


def bits_of(count):
    return [1 << b for b in range(count.bit_length() - 1)]


def reversed_order(count):
    width = count.bit_length() - 1
    return [int(format(p, "b").zfill(width)[::-1], 2) if width else 0 for p in range(count)]


def swap(array, axis, bit):
    count = lax.axis_size(axis)
    return lax.ppermute(array, axis, [(i, i ^ bit) for i in range(count)])


def in_hbm(*arrays):
    return [pltpu.with_memory_space_constraint(x, pltpu.HBM) for x in arrays]


def in_vmem(*arrays):
    return [pltpu.with_memory_space_constraint(x, pltpu.VMEM) for x in arrays]


def tie(array, *after):
    def kernel(*refs):
        pass

    return pl.pallas_call(
        kernel,
        in_specs=[ANY] * (1 + len(after)),
        out_specs=ANY,
        out_shape=jax.ShapeDtypeStruct(array.shape, array.dtype),
        input_output_aliases={0: 0},
        compiler_params=params(1),
        name="tie",
    )(array, *after)


def on_vmem(body, outs, arrays, after=(), name="on_vmem"):
    def kernel(*refs):
        body(*refs[:len(arrays)], *refs[len(arrays) + len(after):])

    return pl.pallas_call(
        kernel,
        in_specs=[VMEM] * len(arrays) + [ANY] * len(after),
        out_specs=[VMEM] * len(outs),
        out_shape=[pltpu.VMEM(shape, kind) for shape, kind in outs],
        compiler_params=params(),
        name=name,
    )(*in_vmem(*arrays), *after)


def load(pieces):
    count = len(pieces)

    def kernel(*refs):
        sources, targets, sems = refs[:count], refs[count:-1], refs[-1]
        copies = [
            pltpu.make_async_copy(source.at[pl.ds(first, rows)], target, sems.at[i])
            for i, (source, target, (_, first, rows)) in enumerate(zip(sources, targets, pieces))
        ]
        for copy in copies:
            copy.start()
        for copy in copies:
            copy.wait()

    return pl.pallas_call(
        kernel,
        in_specs=[HBM] * count,
        out_specs=[VMEM] * count,
        out_shape=[pltpu.VMEM((rows, x.shape[1]), x.dtype) for x, _, rows in pieces],
        scratch_shapes=[pltpu.SemaphoreType.DMA((count,))],
        compiler_params=params(1),
        name="load",
    )(*in_hbm(*[x for x, _, _ in pieces]))


def in_rows(array, count):
    rows = array.shape[0] // count

    def body(*refs):
        for i in range(count):
            refs[1 + i][...] = refs[0][i * rows:(i + 1) * rows, :]

    return on_vmem(body, [((rows, array.shape[1]), array.dtype)] * count, [array], name="in_rows")


def rows_of(refs, start, size):
    found, at = [], 0
    for ref in refs:
        low, high = max(start, at), min(start + size, at + ref.shape[0])
        if low < high:
            found.append(ref[low - at:high - at, :])
        at += ref.shape[0]
    return found[0] if len(found) == 1 else jnp.concatenate(found, axis=0)


def cut(whole, order, offsets, pieces):
    rows, model = whole.shape
    block = model // len(order)
    if pieces[-1] % 128:
        here = lax.axis_index("ctx")
        return [
            jnp.concatenate([lax.dynamic_slice(whole, (0, (here ^ j) * block + o), (rows, p)) for j in order], axis=1)
            for o, p in zip(offsets, pieces)
        ]

    def kernel(source, *refs):
        targets, sems = refs[:-1], refs[-1]
        here = lax.axis_index("ctx")
        for i, (offset, piece) in enumerate(zip(offsets, pieces)):
            for p, j in enumerate(order):
                at = pl.multiple_of((here ^ j) * block + offset, 128)
                pltpu.make_async_copy(
                    source.at[:, pl.ds(at, piece)], targets[i].at[:, pl.ds(p * piece, piece)], sems.at[i]
                ).start()
        for i, target in enumerate(targets):
            pltpu.make_async_copy(target, target, sems.at[i]).wait()

    return list(pl.pallas_call(
        kernel,
        in_specs=[HBM],
        out_specs=[VMEM] * len(pieces),
        out_shape=[pltpu.VMEM((rows, piece * len(order)), whole.dtype) for piece in pieces],
        scratch_shapes=[pltpu.SemaphoreType.DMA((len(pieces),))],
        compiler_params=params(1),
        name="cut",
    )(*in_hbm(whole)))


def scan_states(state, sc, later):
    shape = state.shape
    bits = bits_of(lax.axis_size("ctx"))
    total, came = state, []
    for bit in bits:
        if bit != bits[0]:
            total, = on_vmem(add_kernel, [(shape, total.dtype)], [total, came[-1]], name="add")
        came.append(swap(total, "ctx", bit))

    def body(*refs):
        here = lax.axis_index("ctx")
        sums = jnp.zeros(shape, F32)
        for bit, ref in zip(bits, refs):
            high = ((here & bit) != 0).astype(F32)
            sums = sums + ref[...].astype(F32) * ((1.0 - high) if later else high)
        refs[-1][...] = (sums * sc).astype(BF16)

    return on_vmem(body, [(shape, BF16)], came, name="states")[0], total


def add_kernel(a_ref, b_ref, out_ref):
    out_ref[...] = (a_ref[...].astype(F32) + b_ref[...].astype(F32)).astype(out_ref.dtype)


def spread(table, length):
    blocks = table.shape[0]
    row = lax.broadcasted_iota(jnp.int32, (length, blocks), 0) // BLK
    pick = (row == lax.broadcasted_iota(jnp.int32, (length, blocks), 1)).astype(BF16)
    chosen = mm(pick, (table == 1).astype(BF16), NN).astype(BF16)
    return mm(chosen, pick, NT)


def heads_of(ref):
    return [slice(h * HEAD, (h + 1) * HEAD) for h in range(ref.shape[1] // HEAD)]


def early(q, k, v, table, sc):
    length, width = q.shape
    heads = width // HEAD

    def body(table_ref, q_ref, k_ref, v_ref, mask_ref, s_ref, kv_ref):
        wide = spread(table_ref[...], length)
        row = lax.broadcasted_iota(jnp.int32, (length, length), 0)
        col = lax.broadcasted_iota(jnp.int32, (length, length), 1)
        inside = (row // BLK == col // BLK) & (row >= col)
        before = (row // BLK > col // BLK) & (wide > 0.5)
        mask_ref[...] = jnp.where(inside | before, sc, 0.0)
        for h, at in enumerate(heads_of(q_ref)):
            k_here = k_ref[:, at]
            s_ref[h] = (mm(q_ref[:, at], k_here, NT) * mask_ref[...]).astype(BF16)
            kv_ref[h] = mm(k_here, v_ref[:, at], TN)

    return on_vmem(
        body,
        [((length, length), F32), ((heads, length, length), BF16), ((heads, HEAD, HEAD), F32)],
        [table, q, k, v],
        name="early",
    )


def late_kernel(q_ref, k_ref, v_ref, g_ref, s_ref, prev_ref, mask_ref, *refs):
    dq_ref, dkp_ref, dvp_ref, dq, sem = refs[-5:]
    half = q_ref.shape[0] // 2
    lo, hi = slice(0, half), slice(half, 2 * half)
    for h, at in enumerate(heads_of(q_ref)):
        q, k, v, g = q_ref[:, at], k_ref[:, at], v_ref[:, at], g_ref[:, at]

        def weights(rows, cols):
            return (mm(g[rows], v[cols], NT) * mask_ref[rows, cols]).astype(BF16)

        m00, m10, m11 = weights(lo, lo), weights(hi, lo), weights(hi, hi)
        from_state = mm(g, prev_ref[h], NT)
        dq[lo, at] = (mm(m00, k[lo], NN) + from_state[lo]).astype(BF16)
        dq[hi, at] = (mm(m10, k[lo], NN) + mm(m11, k[hi], NN) + from_state[hi]).astype(BF16)
        dkp_ref[lo, at] = mm(m00, q[lo], TN) + mm(m10, q[hi], TN)
        dkp_ref[hi, at] = mm(m11, q[hi], TN)
        dvp_ref[lo, at] = mm(s_ref[h, :, lo], g, TN)
        dvp_ref[hi, at] = mm(s_ref[h, hi, hi], g[hi], TN)
    copy = pltpu.make_async_copy(dq, dq_ref, sem)
    copy.start()
    copy.wait()


def late(q, k, v, g, s, prev, mask, after):
    shape = q.shape
    return pl.pallas_call(
        late_kernel,
        in_specs=[VMEM] * 7 + [ANY] * len(after),
        out_specs=[HBM, VMEM, VMEM],
        out_shape=[pltpu.HBM(shape, BF16), pltpu.VMEM(shape, F32), pltpu.VMEM(shape, F32)],
        scratch_shapes=[pltpu.VMEM(shape, BF16), pltpu.SemaphoreType.DMA],
        compiler_params=params(),
        name="late",
    )(*in_vmem(q, k, v, g, s, prev, mask), *after)


def final_kernel(k_ref, v_ref, later_ref, dkp_ref, dvp_ref, *refs):
    dk_ref, dv_ref, dk, dv, sems = refs[-5:]
    for h, at in enumerate(heads_of(k_ref)):
        dk[:, at] = (dkp_ref[:, at] + mm(v_ref[:, at], later_ref[h], NT)).astype(BF16)
    copy_k = pltpu.make_async_copy(dk, dk_ref, sems.at[0])
    copy_k.start()
    for h, at in enumerate(heads_of(k_ref)):
        dv[:, at] = (dvp_ref[:, at] + mm(k_ref[:, at], later_ref[h], NN)).astype(BF16)
    copy_v = pltpu.make_async_copy(dv, dv_ref, sems.at[1])
    copy_v.start()
    copy_k.wait()
    copy_v.wait()


def final(k, v, later, dkp, dvp, after):
    shape = k.shape
    return pl.pallas_call(
        final_kernel,
        in_specs=[VMEM] * 5 + [ANY] * len(after),
        out_specs=[HBM, HBM],
        out_shape=[pltpu.HBM(shape, BF16)] * 2,
        scratch_shapes=[pltpu.VMEM(shape, BF16)] * 2 + [pltpu.SemaphoreType.DMA((2,))],
        compiler_params=params(),
        name="final",
    )(*in_vmem(k, v, later, dkp, dvp), *after)


def fold(blocks, opened, norm, ws, products, acc, q, sends, after=()):
    own, a, b1, c1, b2, c2 = blocks
    rows, wide = own.shape
    length, width = opened.shape
    half = wide // 2
    last, whole = q is not None, not products
    kept = [g for g, _ in products if g is not None]
    flat_ws = [x for w in ws for x in w] if products else []
    arrays = [own, a, b1, c1, b2, *c2, opened, *kept, *flat_ws]
    arrays += ([] if acc is None else [acc]) + ([q] if last else [])
    outs = [((half, width), F32)] + [((half // sends, width), BF16)] * sends
    if whole:
        outs.append(((length, wide), BF16))
    else:
        outs.append(((length, width), BF16 if last else F32))
    if last:
        outs.append(((width // HEAD, HEAD, HEAD), BF16))

    def kernel(*refs):
        refs = list(refs)
        own_ref, a_ref, b1_ref, c1_ref, b2_ref = [refs.pop(0) for _ in range(5)]
        c2_refs = [refs.pop(0) for _ in c2]
        opened_ref = refs.pop(0)
        kept_refs = [refs.pop(0) for _ in kept]
        w_refs = [[refs.pop(0) for _ in w] for w in ws] if products else []
        acc_ref = None if acc is None else refs.pop(0)
        q_ref = refs.pop(0) if last else None
        del refs[:len(after)]
        keep_ref = refs.pop(0)
        send_refs = [refs.pop(0) for _ in range(sends)]
        third_ref = refs.pop(0)
        qg_ref = refs.pop(0) if last else None
        grad = third_ref if whole else refs.pop(0)
        here = lax.axis_index("tsp")

        def place(ref, at, under=0):
            count = ref.shape[0]
            grad[pl.ds(pl.multiple_of(at * rows + under, count), count), :] = ref[...]

        at_end = (here == 0) | (here == 3)
        near, far = jnp.where(here < 2, 2, 1), jnp.where(here < 2, 3, 0)
        place(own_ref, here)
        place(a_ref, here ^ 1)

        @pl.when(at_end)
        def _():
            place(c1_ref, near)
            for i, ref in enumerate(c2_refs):
                place(ref, far, i * ref.shape[0])

        @pl.when(jnp.logical_not(at_end))
        def _():
            place(b1_ref, near)
            place(b2_ref, far)

        sent = (mm(grad[:, half:], opened_ref[...], TN) * norm).astype(BF16)
        for i, ref in enumerate(send_refs):
            ref[...] = sent[i * ref.shape[0]:(i + 1) * ref.shape[0], :]
        keep_ref[...] = mm(grad[:, :half], opened_ref[...], TN) * norm
        if whole:
            return
        total = None if acc is None else acc_ref[...]
        for g, start in products:
            source = grad if g is None else kept_refs.pop(0)
            piece = source.shape[1] // len(ws)
            rows_of_w = jnp.concatenate([rows_of(refs_here, start, piece) for refs_here in w_refs], axis=0)
            term = mm(source[...], rows_of_w, NN)
            total = term if total is None else total + term
        third_ref[...] = total.astype(third_ref.dtype)
        if last:
            for h, at in enumerate(heads_of(third_ref)):
                qg_ref[h] = mm(q_ref[:, at], third_ref[:, at], TN).astype(BF16)

    return pl.pallas_call(
        kernel,
        in_specs=[VMEM] * len(arrays) + [ANY] * len(after),
        out_specs=[VMEM] * len(outs),
        out_shape=[pltpu.VMEM(shape, kind) for shape, kind in outs],
        scratch_shapes=[] if whole else [pltpu.VMEM((length, wide), BF16)],
        compiler_params=params(),
        name="fold",
    )(*in_vmem(*arrays), *after)


def scatter_step(keep, sends, bit):
    came = [swap(x, "ctx", bit) for x in sends]
    half, width = keep.shape[0] // 2, keep.shape[1]

    def body(keep_ref, *refs):
        first_ref, second_ref = refs[-2:]
        came_refs = refs[:-2]
        first_ref[...] = keep_ref[:half, :] + rows_of(came_refs, 0, half).astype(F32)
        second_ref[...] = (keep_ref[half:, :] + rows_of(came_refs, half, half).astype(F32)).astype(BF16)

    return on_vmem(
        body, [((half, width), F32), ((half, width), BF16)], [keep, *came], name="split")


def finish(mine, came, offset, length, target):
    rows, width = mine.shape

    def kernel(*refs):
        mine_ref, came_ref = refs[:2]
        out_ref, total, sem = refs[-3:]
        total[...] = mine_ref[...].astype(F32) + came_ref[...].astype(F32)
        copy = pltpu.make_async_copy(total, out_ref.at[pl.ds(offset, rows)], sem)
        copy.start()
        copy.wait()

    extra = [] if target is None else [target]
    return pl.pallas_call(
        kernel,
        in_specs=[VMEM] * 2 + [HBM] * len(extra),
        out_specs=HBM,
        out_shape=pltpu.HBM((length, width), F32),
        input_output_aliases={} if target is None else {2: 0},
        scratch_shapes=[pltpu.VMEM((rows, width), F32), pltpu.SemaphoreType.DMA],
        compiler_params=params(),
        name="finish",
    )(*in_vmem(mine, came), *extra)


def shards(queries, keys, values, attn_out, out_grad, out_weight, block_mask):
    ctx = lax.axis_size("ctx")
    assert lax.axis_size("tsp") == 4 and lax.axis_size("dp") == 2
    _, group_len, width = queries.shape
    seq_len = group_len * ctx
    sc = 1.0 / math.sqrt(HEAD * seq_len)
    norm = 1.0 / math.sqrt(seq_len * lax.axis_size("dp"))
    grad = out_grad[0]
    order = reversed_order(ctx)
    block = grad.shape[1] // ctx
    count = len(EIGHTHS)
    pieces = [block * e // 8 for e in EIGHTHS]
    offsets = [sum(pieces[:i]) for i in range(count)]
    bits = bits_of(ctx)
    top = bits[-1]

    def outer(x):
        return lax.ppermute(x, "tsp", [(0, 1), (1, 0), (2, 3), (3, 2)])

    def inner(x):
        return lax.ppermute(x, "tsp", [(1, 2), (2, 1)])

    def to_ends(x):
        return lax.ppermute(x, "tsp", [(1, 0), (2, 3)])

    def other(x):
        return lax.ppermute(x, "dp", [(0, 1), (1, 0)])

    own = cut(grad, order, offsets, pieces)
    first = pieces[0]
    q, k, v, opened, w_here, w_low, w_high = load(
        [(x[0], 0, group_len) for x in (queries, keys, values, attn_out)]
        + [(out_weight, 0, block), (out_weight, 0, first), (out_weight, first, block - first)])
    a, b1, b2, c1, c2 = [[None] * count for _ in range(5)]

    def step_a(i, *after):
        if after:
            own[i] = tie(own[i], *after)
        a[i], b1[i] = outer(own[i]), inner(own[i])
        b2[i] = inner(a[i])

    def step_c1(i, *after):
        b1[i] = tie(b1[i], *after)
        c1[i] = to_ends(b1[i])

    def step_c2(i, *after, parts=1):
        b2[i] = tie(b2[i], *after)
        c2[i] = [to_ends(x) for x in (in_rows(b2[i], parts) if parts > 1 else [b2[i]])]

    step_a(0)
    step_a(1)

    held = {0: [w_here]}
    for bit in reversed(bits[1:]):
        for j in list(held):
            held[j | bit] = [swap(held[j][0], "ctx", bit)]
    for j in list(held):
        if j == 0:
            w_low = tie(w_low, a[1])
            held[j | bits[0]] = [swap(x, "ctx", bits[0]) for x in (w_low, w_high)]
        else:
            held[j | bits[0]] = [swap(x, "ctx", bits[0]) for x in in_rows(held[j][0], 4)]
    ws = [held[j] for j in order]

    mask, s, kv = early(q, k, v, block_mask[0, 0], sc)
    prev, _ = scan_states(kv, sc, False)

    step_c1(0, a[0])
    step_c2(0, a[1], held[bits[0]][0])
    step_a(2, c1[0])
    step_c1(1, *c2[0])
    step_c2(1, a[2], prev)
    step_a(3, c1[1])
    step_c1(2, *c2[1])
    step_c2(2, a[3])
    step_c1(3, c1[2])
    step_c2(3, *c2[2], parts=2)

    def add_top(keep, send, after=()):
        return on_vmem(
            add_kernel, [(keep.shape, BF16)], [keep, swap(send, "ctx", top)], after=after, name="mine")[0]

    keeps, sends, mine, theirs = [[None] * count for _ in range(4)]
    acc = kept = qg = None
    for i in range(count):
        last = i == count - 1
        products = [] if i == 0 else [(None, offsets[i])]
        if i == 1:
            products.insert(0, (kept, offsets[0]))
        keep, *rest = fold(
            (own[i], a[i], b1[i], c1[i], b2[i], c2[i]), opened, norm, ws, products, acc,
            q if last else None, CORE_SENDS[i])
        send, third, more = rest[:CORE_SENDS[i]], rest[CORE_SENDS[i]], rest[CORE_SENDS[i] + 1:]
        if i == 0:
            kept = third
        else:
            acc = third
        if last:
            qg = more[0]
        for bit in bits[:-1]:
            keep, send = scatter_step(keep, send, bit)
            send = [send]
        keeps[i], sends[i] = keep, send[0]
    og = acc
    for i in range(count - 2):
        mine[i] = add_top(keeps[i], sends[i])
        theirs[i] = other(mine[i])
    later, total_qg = scan_states(qg, sc, True)
    dq, dkp, dvp = late(q, k, v, og, s, prev, mask, (total_qg,))
    mine[-2] = add_top(keeps[-2], sends[-2], (dkp,))
    mine[-1] = add_top(keeps[-1], tie(sends[-1], *theirs[:-2]), (later,))
    theirs[-2], theirs[-1] = other(mine[-2]), other(mine[-1])
    dk, dv = final(k, v, later, dkp, dvp, ())
    grown = None
    for i in range(count):
        grown = finish(mine[i], theirs[i], offsets[i], block, grown)
    return dq[None], dk[None], dv[None], grown


def solution(mesh):
    placed = (
        P("dp", "ctx", "tsp"),
        P("dp", "ctx", "tsp"),
        P("dp", "ctx", "tsp"),
        P("dp", "ctx", "tsp"),
        P("dp", ("ctx", "tsp"), None),
        P("ctx", "tsp"),
        P("dp", "ctx", None, None),
    )
    return jax.shard_map(
        shards,
        mesh=mesh,
        in_specs=placed,
        out_specs=(
            P("dp", "ctx", "tsp"),
            P("dp", "ctx", "tsp"),
            P("dp", "ctx", "tsp"),
            P("ctx", "tsp"),
        ),
        check_vma=False,
    )
```

time: 315 us -> 131 us (0.42)
  waiting for transfers between devices: 249 us -> 55.1 us
  starting transfers between devices: 0.42 us -> 55.2 us
  matrix products: 27.1 us -> 0 us
  Pallas kernels: 0 us -> 18.7 us
  local copies, waits for them, and re-layouts: 14 us -> 0.01 us
  between operations: 14.4 us -> 1.35 us
  other arithmetic: 8.69 us -> 0 us
    all_gather x4 -> x0, waiting for transfers between devices: 132 us -> none  [the longest x1 80.7 us: shards(): gathered = lax.all_gather(out_grad, 'tsp', axis=1, tiled=True)]
    reduce_scatter x1 -> x0, waiting for transfers between devices: 63.7 us -> none  [shards(): lax.psum_scatter(product * norm_factor, 'ctx', scatter_dimension=0, tiled...]
    ppermute x0 -> x57, starting transfers between devices: none -> 55.2 us  [the longest x4 16.8 us: outer(): return lax.ppermute(x, 'tsp', [(0, 1), (1, 0), (2, 3), (3, 2)])]
    ppermute x0 -> x57, waiting for transfers between devices: none -> 55.1 us  [the longest x9 36.5 us: to_ends(): return lax.ppermute(x, 'tsp', [(1, 0), (2, 3)])]
    psum x1 -> x0, waiting for transfers between devices: 52.7 us -> none  [shards(): weight_grad = lax.psum(partial_grad, 'dp')]
    dot_general x11 -> x0, matrix products: 27.1 us -> none  [the longest x1 8.13 us: shards(): lax.dot_general(columns, opened, (((0,), (0,)), ((), ())), preferred_elem...]
    pallas_call x0 -> x39, Pallas kernels: none -> 18.7 us  [the longest x4 5.97 us: fold(): pl.pallas_call(kernel, in_specs=[VMEM] * len(arrays) + [ANY] * len(after)...]
    unnamed x32 -> x2, local copies, waits for them, and re-layouts: 9.6 us -> 0.01 us
  transfers between devices with their start and end apart: 6 -> 57, of which waited for: 6 -> 19; matrix products, arithmetic and copies ran while one was open for 14% -> 0% of each run, Pallas kernels for 0% -> 13%
where the time goes in v2:
time: 131 us; the launch traced here: 130 us
  starting transfers between devices  55.2 us (42%)
  waiting for transfers between devices  55.1 us (42%)
  Pallas kernels  18.7 us (14%)
  between operations  1.35 us (1%)
    ppermute x9, waiting for transfers between devices, to_ends(): return lax.ppermute(x, 'tsp', [(1, 0), (2, 3)])  36.5 us
    ppermute x4, starting transfers between devices, outer(): return lax.ppermute(x, 'tsp', [(0, 1), (1, 0), (2, 3), (3, 2)])  16.8 us
    ppermute x32, starting transfers between devices, swap(): return lax.ppermute(array, axis, [(i, i ^ bit) for i in range(count)])  15.6 us
    ppermute x9, starting transfers between devices, to_ends(): return lax.ppermute(x, 'tsp', [(1, 0), (2, 3)])  11.6 us
    ppermute x4, waiting for transfers between devices, outer(): return lax.ppermute(x, 'tsp', [(0, 1), (1, 0), (2, 3), (3, 2)])  8.87 us
    ppermute x32, waiting for transfers between devices, swap(): return lax.ppermute(array, axis, [(i, i ^ bit) for i in range(count)])  6.35 us
    pallas_call x4, Pallas kernels, fold(): pl.pallas_call(kernel, in_specs=[VMEM] * len(arrays) + [ANY] * len(after)...  5.97 us
    ppermute x4, starting transfers between devices, other(): return lax.ppermute(x, 'dp', [(0, 1), (1, 0)])  5.82 us
  transfers between devices with their start and end apart: 57, of which 19 were waited for; matrix products, arithmetic and copies ran while one was open for 0% of the time, Pallas kernels for 13%

profile of v2, /device:TPU:0, one launch (start us, length us, event | category | flops | bytes accessed | tf_op | source)
XLA Modules:
  0.0 130.3 jit_solution(10387604829893456735)
XLA Ops:
  1.9 3.1 %collective-permute-start.1 = (bf16[128,1536]{1,0:T(8,128)(2,1)S(1)}, bf16[128,1536]{1,0:T(8,128)(2,1)S(1)}, u32[]{:S(2)}, u32[]{:S(2)}) collective-permute-start(bf16[128,1536]{1,0:T(8,128)(2,1)S(1)} %get-tuple-element.68.refs_0_), channel_id=1, source_target_pairs={{0,2},{2,0},{4,6},{6,4},{1,3},{3,1},{5,7},{7,5},{8,10},{10,8},{12,... | collective-permute-start | bytes 1179656 | tf_op jit(solution)/shard_map/ppermute | solution.py:425
  5.7 4.4 %collective-permute-start.3 = (bf16[128,1024]{1,0:T(8,128)(2,1)S(1)}, bf16[128,1024]{1,0:T(8,128)(2,1)S(1)}, u32[]{:S(2)}, u32[]{:S(2)}) collective-permute-start(bf16[128,1024]{1,0:T(8,128)(2,1)S(1)} %get-tuple-element.67.refs_0_), channel_id=1, source_target_pairs={{0,2},{2,0},{4,6},{6,4},{1,3},{3,1},{5,7},{7,5},{8,10},{10,8},{12,... | collective-permute-start | bytes 786440 | tf_op jit(solution)/shard_map/ppermute | solution.py:425
  10.1 2.2 %load.1 = (bf16[512,512]{1,0:T(8,128)(2,1)S(1)}, bf16[512,512]{1,0:T(8,128)(2,1)S(1)}, bf16[512,512]{1,0:T(8,128)(2,1)S(1)}, bf16[512,512]{1,0:T(8,128)(2,1)S(1)...) custom-call(bf16[512,512]{1,0:T(8,128)(2,1)} %bitcast.11, ...), custom_call_target="tpu_custom_call" | custom-call | tf_op jit(solution)/shard_map/load/pallas_call | solution.py:99
  12.3 1.6 %collective-permute-start.24 = (bf16[1024,512]{1,0:T(8,128)(2,1)S(1)}, bf16[1024,512]{1,0:T(8,128)(2,1)S(1)}, u32[]{:S(2)}, u32[]{:S(2)}) collective-permute-start(bf16[1024,512]{1,0:T(8,128)(2,1)S(1)} %get-tuple-element.75.refs_8_.refs_7_), channel_id=1, source_target_pairs={{0,16},{8,24},{16,0},{24,8},{1,17},{9,25},{17,1},{25,9},{2,18},{10... | collective-permute-start | bytes 3145736 | tf_op jit(solution)/shard_map/ppermute | solution.py:45
  13.9 5.8 %collective-permute-done.3.refs_1_ = bf16[128,1024]{1,0:T(8,128)(2,1)S(1)} collective-permute-done((bf16[128,1024]{1,0:T(8,128)(2,1)S(1)}, bf16[128,1024]{1,0:T(8,128)(2,1)S(1)}, u32[]{:S(2)}, u32[]{:S(2)}) %collective-permute-start.3) | collective-permute-done | bytes 262176 | tf_op jit(solution)/shard_map/ppermute | solution.py:425
  19.7 1.3 collective-permute-start.10
  24.3 1.7 %collective-permute-start.15 = (f32[4,128,128]{2,1,0:T(8,128)S(1)}, f32[4,128,128]{2,1,0:T(8,128)S(1)}, u32[]{:S(2)}, u32[]{:S(2)}) collective-permute-start(f32[4,128,128]{2,1,0:T(8,128)S(1)} %add.2), channel_id=1, source_target_pairs={{0,16},{8,24},{16,0},{24,8},{1,17},{9,25},{17,1},{25,9},{2,18},{10... | collective-permute-start | bytes 786440 | tf_op jit(solution)/shard_map/ppermute | solution.py:45
  26.0 7.1 %collective-permute-done.10.refs_1_.refs_3_ = bf16[128,1536]{1,0:T(8,128)(2,1)S(1)} collective-permute-done((bf16[128,1536]{1,0:T(8,128)(2,1)S(1)}, bf16[128,1536]{1,0:T(8,128)(2,1)S(1)}, u32[]{:S(2)}, u32[]{:S(2)}) %collective-permute-start.10) | collective-permute-done | bytes 393248 | tf_op jit(solution)/shard_map/ppermute | solution.py:431
  33.8 5.9 %collective-permute-start.13 = (bf16[128,1024]{1,0:T(8,128)(2,1)S(1)}, bf16[128,1024]{1,0:T(8,128)(2,1)S(1)}, u32[]{:S(2)}, u32[]{:S(2)}) collective-permute-start(bf16[128,1024]{1,0:T(8,128)(2,1)S(1)} %tie.17.refs_0_), channel_id=1, source_target_pairs={{0,2},{2,0},{4,6},{6,4},{1,3},{3,1},{5,7},{7,5},{8,10},{10,8},{12,... | collective-permute-start | bytes 786440 | tf_op jit(solution)/shard_map/ppermute | solution.py:425
  39.7 2.4 %collective-permute-done.15.refs_1_ = f32[4,128,128]{2,1,0:T(8,128)S(1)} collective-permute-done((f32[4,128,128]{2,1,0:T(8,128)S(1)}, f32[4,128,128]{2,1,0:T(8,128)S(1)}, u32[]{:S(2)}, u32[]{:S(2)}) %collective-permute-start.15) | collective-permute-done | bytes 262176 | tf_op jit(solution)/shard_map/ppermute | solution.py:45
  44.1 2.6 %collective-permute-done.13.refs_1_ = bf16[128,1024]{1,0:T(8,128)(2,1)S(1)} collective-permute-done((bf16[128,1024]{1,0:T(8,128)(2,1)S(1)}, bf16[128,1024]{1,0:T(8,128)(2,1)S(1)}, u32[]{:S(2)}, u32[]{:S(2)}) %collective-permute-start.13) | collective-permute-done | bytes 262176 | tf_op jit(solution)/shard_map/ppermute | solution.py:425
  48.8 7.2 %collective-permute-done.5.refs_1_.refs_5_ = bf16[128,1536]{1,0:T(8,128)(2,1)S(1)} collective-permute-done((bf16[128,1536]{1,0:T(8,128)(2,1)S(1)}, bf16[128,1536]{1,0:T(8,128)(2,1)S(1)}, u32[]{:S(2)}, u32[]{:S(2)}) %collective-permute-start.5) | collective-permute-done | bytes 393248 | tf_op jit(solution)/shard_map/ppermute | solution.py:431
  56.0 3.7 %collective-permute-done.16.refs_1_.refs_5_ = bf16[128,1024]{1,0:T(8,128)(2,1)S(1)} collective-permute-done((bf16[128,1024]{1,0:T(8,128)(2,1)S(1)}, bf16[128,1024]{1,0:T(8,128)(2,1)S(1)}, u32[]{:S(2)}, u32[]{:S(2)}) %collective-permute-start.16) | collective-permute-done | bytes 262176 | tf_op jit(solution)/shard_map/ppermute | solution.py:431
  64.4 3.7 %collective-permute-done.6.refs_1_.refs_3_ = bf16[128,1024]{1,0:T(8,128)(2,1)S(1)} collective-permute-done((bf16[128,1024]{1,0:T(8,128)(2,1)S(1)}, bf16[128,1024]{1,0:T(8,128)(2,1)S(1)}, u32[]{:S(2)}, u32[]{:S(2)}) %collective-permute-start.6) | collective-permute-done | bytes 262176 | tf_op jit(solution)/shard_map/ppermute | solution.py:431
  68.1 2.2 %fold.5 = (f32[512,512]{1,0:T(8,128)S(1)}, bf16[128,512]{1,0:T(8,128)(2,1)S(1)}, bf16[128,512]{1,0:T(8,128)(2,1)S(1)}, bf16[128,512]{1,0:T(8,128)(2,1)S(1)}, bf1...) custom-call(bf16[128,1024]{1,0:T(8,128)(2,1)S(1)} %get-tuple-element.67.refs_0_, ...), custom_call_target="tpu_custom_call" | custom-call | tf_op jit(solution)/shard_map/fold/pallas_call | solution.py:359
  70.8 3.4 %collective-permute-start.7 = (bf16[128,512]{1,0:T(8,128)(2,1)S(1)}, bf16[128,512]{1,0:T(8,128)(2,1)S(1)}, u32[]{:S(2)}, u32[]{:S(2)}) collective-permute-start(bf16[128,512]{1,0:T(8,128)(2,1)S(1)} %tie.15.refs_0_), channel_id=1, source_target_pairs={{0,2},{2,0},{4,6},{6,4},{1,3},{3,1},{5,7},{7,5},{8,10},{10,8},{12,... | collective-permute-start | bytes 393224 | tf_op jit(solution)/shard_map/ppermute | solution.py:425
  74.4 1.6 %collective-permute-start.37 = (bf16[384,512]{1,0:T(8,128)(2,1)S(1)}, bf16[384,512]{1,0:T(8,128)(2,1)S(1)}, u32[]{:S(2)}, u32[]{:S(2)}) collective-permute-start(bf16[384,512]{1,0:T(8,128)(2,1)S(1)} %get-tuple-element.103), channel_id=1, source_target_pairs={{0,16},{8,24},{16,0},{24,8},{1,17},{9,25},{17,1},{25,9},{2,18},{10... | collective-permute-start | bytes 1179656 | tf_op jit(solution)/shard_map/ppermute | solution.py:45
  80.1 1.6 %collective-permute-start.43 = (bf16[256,512]{1,0:T(8,128)(2,1)S(1)}, bf16[256,512]{1,0:T(8,128)(2,1)S(1)}, u32[]{:S(2)}, u32[]{:S(2)}) collective-permute-start(bf16[256,512]{1,0:T(8,128)(2,1)S(1)} %get-tuple-element.110), channel_id=1, source_target_pairs={{0,16},{8,24},{16,0},{24,8},{1,17},{9,25},{17,1},{25,9},{2,18},{10... | collective-permute-start | bytes 786440 | tf_op jit(solution)/shard_map/ppermute | solution.py:45
  81.6 8.5 %collective-permute-done.17.refs_1_.refs_3_ = bf16[128,1024]{1,0:T(8,128)(2,1)S(1)} collective-permute-done((bf16[128,1024]{1,0:T(8,128)(2,1)S(1)}, bf16[128,1024]{1,0:T(8,128)(2,1)S(1)}, u32[]{:S(2)}, u32[]{:S(2)}) %collective-permute-start.17) | collective-permute-done | bytes 262176 | tf_op jit(solution)/shard_map/ppermute | solution.py:431
  92.1 3.4 %collective-permute-done.21.refs_1_.refs_5_ = bf16[128,1024]{1,0:T(8,128)(2,1)S(1)} collective-permute-done((bf16[128,1024]{1,0:T(8,128)(2,1)S(1)}, bf16[128,1024]{1,0:T(8,128)(2,1)S(1)}, u32[]{:S(2)}, u32[]{:S(2)}) %collective-permute-start.21) | collective-permute-done | bytes 262176 | tf_op jit(solution)/shard_map/ppermute | solution.py:431
  95.5 1.4 %fold.6 = (f32[512,512]{1,0:T(8,128)S(1)}, bf16[64,512]{1,0:T(8,128)(2,1)S(1)}, bf16[64,512]{1,0:T(8,128)(2,1)S(1)}, bf16[64,512]{1,0:T(8,128)(2,1)S(1)}, bf16[6...) custom-call(bf16[128,1024]{1,0:T(8,128)(2,1)S(1)} %tie.17.refs_0_, ...), custom_call_target="tpu_custom_call" | custom-call | tf_op jit(solution)/shard_map/fold/pallas_call | solution.py:359
  99.5 1.3 collective-permute-start.23
  100.8 1.6 %collective-permute-start.38 = (bf16[384,512]{1,0:T(8,128)(2,1)S(1)}, bf16[384,512]{1,0:T(8,128)(2,1)S(1)}, u32[]{:S(2)}, u32[]{:S(2)}) collective-permute-start(bf16[384,512]{1,0:T(8,128)(2,1)S(1)} %mine.4.refs_0_), channel_id=1, source_target_pairs={{0,1},{1,0},{2,3},{3,2},{4,5},{5,4},{6,7},{7,6},{8,9},{9,8},{10,11... | collective-permute-start | bytes 1179656 | tf_op jit(solution)/shard_map/ppermute | solution.py:434
  102.9 1.8 %collective-permute-done.22.refs_5_ = bf16[64,512]{1,0:T(8,128)(2,1)S(1)} collective-permute-done((bf16[64,512]{1,0:T(8,128)(2,1)S(1)}, bf16[64,512]{1,0:T(8,128)(2,1)S(1)}, u32[]{:S(2)}, u32[]{:S(2)}) %collective-permute-start.22) | collective-permute-done | bytes 65568 | tf_op jit(solution)/shard_map/ppermute | solution.py:431
  107.6 1.5 %collective-permute-start.44 = (bf16[256,512]{1,0:T(8,128)(2,1)S(1)}, bf16[256,512]{1,0:T(8,128)(2,1)S(1)}, u32[]{:S(2)}, u32[]{:S(2)}) collective-permute-start(bf16[256,512]{1,0:T(8,128)(2,1)S(1)} %mine.5.refs_0_), channel_id=1, source_target_pairs={{0,1},{1,0},{2,3},{3,2},{4,5},{5,4},{6,7},{7,6},{8,9},{9,8},{10,11... | collective-permute-start | bytes 786440 | tf_op jit(solution)/shard_map/ppermute | solution.py:434
  109.3 1.8 %collective-permute-start.55 = (bf16[256,512]{1,0:T(8,128)(2,1)S(1)}, bf16[256,512]{1,0:T(8,128)(2,1)S(1)}, u32[]{:S(2)}, u32[]{:S(2)}) collective-permute-start(bf16[256,512]{1,0:T(8,128)(2,1)S(1)} %get-tuple-element.121), channel_id=1, source_target_pairs={{0,16},{8,24},{16,0},{24,8},{1,17},{9,25},{17,1},{25,9},{2,18},{10... | collective-permute-start | bytes 786440 | tf_op jit(solution)/shard_map/ppermute | solution.py:45
  111.1 1.3 %collective-permute-done.30.refs_1_.refs_0_ = bf16[4,128,128]{2,1,0:T(8,128)(2,1)S(1)} collective-permute-done((bf16[4,128,128]{2,1,0:T(8,128)(2,1)S(1)}, bf16[4,128,128]{2,1,0:T(8,128)(2,1)S(1)}, u32[]{:S(2)}, u32[]{:S(2)}) %collective-permute-start.30) | collective-permute-done | bytes 131104 | tf_op jit(solution)/shard_map/ppermute | solution.py:45
  112.8 2.6 %late.1 = (bf16[512,512]{1,0:T(8,128)(2,1)}, f32[512,512]{1,0:T(8,128)S(1)}, f32[512,512]{1,0:T(8,128)S(1)}) custom-call(bf16[512,512]{1,0:T(8,128)(2,1)S(1)} %get-tuple-element.63.refs_1_.refs_17_.q_ref, bf16[512,512]{1,0:T(8,128)(2,1)S(1)} %get-tuple-element.64.refs_2_.k_ref, bf16[512,512]{1,0:T(8,128)(2,1)S(1)} %get-tuple-element.65.refs_3_.v_ref, ...), custom_call_target="tpu_custom_call" | custom-call | tf_op jit(solution)/shard_map/late/pallas_call | solution.py:248
  115.5 2.1 %collective-permute-done.44.refs_2_.refs_1_ = bf16[256,512]{1,0:T(8,128)(2,1)S(1)} collective-permute-done((bf16[256,512]{1,0:T(8,128)(2,1)S(1)}, bf16[256,512]{1,0:T(8,128)(2,1)S(1)}, u32[]{:S(2)}, u32[]{:S(2)}) %collective-permute-start.44) | collective-permute-done | bytes 262176 | tf_op jit(solution)/shard_map/ppermute | solution.py:434
  117.6 1.7 %collective-permute-start.45 = (bf16[128,512]{1,0:T(8,128)(2,1)S(1)}, bf16[128,512]{1,0:T(8,128)(2,1)S(1)}, u32[]{:S(2)}, u32[]{:S(2)}) collective-permute-start(bf16[128,512]{1,0:T(8,128)(2,1)S(1)} %tie.23), channel_id=1, source_target_pairs={{0,16},{8,24},{16,0},{24,8},{1,17},{9,25},{17,1},{25,9},{2,18},{10... | collective-permute-start | bytes 393224 | tf_op jit(solution)/shard_map/ppermute | solution.py:45
  119.4 1.6 %collective-permute-start.56 = (bf16[256,512]{1,0:T(8,128)(2,1)S(1)}, bf16[256,512]{1,0:T(8,128)(2,1)S(1)}, u32[]{:S(2)}, u32[]{:S(2)}) collective-permute-start(bf16[256,512]{1,0:T(8,128)(2,1)S(1)} %mine.7.refs_0_), channel_id=1, source_target_pairs={{0,1},{1,0},{2,3},{3,2},{4,5},{5,4},{6,7},{7,6},{8,9},{9,8},{10,11... | collective-permute-start | bytes 786440 | tf_op jit(solution)/shard_map/ppermute | solution.py:434
  121.0 1.9 %collective-permute-done.45.refs_1_ = bf16[128,512]{1,0:T(8,128)(2,1)S(1)} collective-permute-done((bf16[128,512]{1,0:T(8,128)(2,1)S(1)}, bf16[128,512]{1,0:T(8,128)(2,1)S(1)}, u32[]{:S(2)}, u32[]{:S(2)}) %collective-permute-start.45) | collective-permute-done | bytes 131104 | tf_op jit(solution)/shard_map/ppermute | solution.py:45
  (123 shorter events, 35.0 us)
Async XLA Ops:
  1.9 17.8 %collective-permute-start.1 = (bf16[128,1536]{1,0:T(8,128)(2,1)S(1)}, bf16[128,1536]{1,0:T(8,128)(2,1)S(1)}, u32[]{:S(2)}, u32[]{:S(2)}) collective-permute-start(bf16[128,1536]{1,0:T(8,128)(2,1)S(1)} %get-tuple-element.68.refs_0_), channel_id=1, source_target_pairs={{0,2},{2,0},{4,6},{6,4},{1,3},{3,1},{5,7},{7,5},{8,10},{10,8},{12,... | collective-permute-start | bytes 1179656 | tf_op jit(solution)/shard_map/ppermute | solution.py:425
  5.0 14.7 %collective-permute-start.9 = (bf16[128,1536]{1,0:T(8,128)(2,1)S(1)}, bf16[128,1536]{1,0:T(8,128)(2,1)S(1)}, u32[]{:S(2)}, u32[]{:S(2)}) collective-permute-start(bf16[128,1536]{1,0:T(8,128)(2,1)S(1)} %get-tuple-element.68.refs_0_), channel_id=1, source_target_pairs={{2,4},{4,2},{3,5},{5,3},{10,12},{12,10},{11,13},{13,11},{18,20},{2... | collective-permute-start | bytes 1179656 | tf_op jit(solution)/shard_map/ppermute | solution.py:428
  5.7 14.1 %collective-permute-start.3 = (bf16[128,1024]{1,0:T(8,128)(2,1)S(1)}, bf16[128,1024]{1,0:T(8,128)(2,1)S(1)}, u32[]{:S(2)}, u32[]{:S(2)}) collective-permute-start(bf16[128,1024]{1,0:T(8,128)(2,1)S(1)} %get-tuple-element.67.refs_0_), channel_id=1, source_target_pairs={{0,2},{2,0},{4,6},{6,4},{1,3},{3,1},{5,7},{7,5},{8,10},{10,8},{12,... | collective-permute-start | bytes 786440 | tf_op jit(solution)/shard_map/ppermute | solution.py:425
  12.3 35.7 %collective-permute-start.24 = (bf16[1024,512]{1,0:T(8,128)(2,1)S(1)}, bf16[1024,512]{1,0:T(8,128)(2,1)S(1)}, u32[]{:S(2)}, u32[]{:S(2)}) collective-permute-start(bf16[1024,512]{1,0:T(8,128)(2,1)S(1)} %get-tuple-element.75.refs_8_.refs_7_), channel_id=1, source_target_pairs={{0,16},{8,24},{16,0},{24,8},{1,17},{9,25},{17,1},{25,9},{2,18},{10... | collective-permute-start | bytes 3145736 | tf_op jit(solution)/shard_map/ppermute | solution.py:45
  19.7 13.4 %collective-permute-start.10 = (bf16[128,1536]{1,0:T(8,128)(2,1)S(1)}, bf16[128,1536]{1,0:T(8,128)(2,1)S(1)}, u32[]{:S(2)}, u32[]{:S(2)}) collective-permute-start(bf16[128,1536]{1,0:T(8,128)(2,1)S(1)} %tie.16.refs_2_), channel_id=1, source_target_pairs={{2,0},{4,6},{3,1},{5,7},{10,8},{12,14},{11,9},{13,15},{18,16},{20,... | collective-permute-start | bytes 1179656 | tf_op jit(solution)/shard_map/ppermute | solution.py:431
  22.7 11.1 %collective-permute-start.2 = (bf16[128,1536]{1,0:T(8,128)(2,1)S(1)}, bf16[128,1536]{1,0:T(8,128)(2,1)S(1)}, u32[]{:S(2)}, u32[]{:S(2)}) collective-permute-start(bf16[128,1536]{1,0:T(8,128)(2,1)S(1)} %collective-permute-done.1.refs_1_), channel_id=1, source_target_pairs={{2,4},{4,2},{3,5},{5,3},{10,12},{12,10},{11,13},{13,11},{18,20},{2... | collective-permute-start | bytes 1179656 | tf_op jit(solution)/shard_map/ppermute | solution.py:428
  23.9 24.8 %collective-permute-start.25 = (bf16[640,512]{1,0:T(8,128)(2,1)S(1)}, bf16[640,512]{1,0:T(8,128)(2,1)S(1)}, u32[]{:S(2)}, u32[]{:S(2)}) collective-permute-start(bf16[640,512]{1,0:T(8,128)(2,1)S(1)} %get-tuple-element.76), channel_id=1, source_target_pairs={{0,8},{8,0},{16,24},{24,16},{1,9},{9,1},{17,25},{25,17},{2,10},{10... | collective-permute-start | bytes 1966088 | tf_op jit(solution)/shard_map/ppermute | solution.py:45
  24.3 17.8 %collective-permute-start.15 = (f32[4,128,128]{2,1,0:T(8,128)S(1)}, f32[4,128,128]{2,1,0:T(8,128)S(1)}, u32[]{:S(2)}, u32[]{:S(2)}) collective-permute-start(f32[4,128,128]{2,1,0:T(8,128)S(1)} %add.2), channel_id=1, source_target_pairs={{0,16},{8,24},{16,0},{24,8},{1,17},{9,25},{17,1},{25,9},{2,18},{10... | collective-permute-start | bytes 786440 | tf_op jit(solution)/shard_map/ppermute | solution.py:45
  33.1 10.2 %collective-permute-start.12 = (bf16[128,1024]{1,0:T(8,128)(2,1)S(1)}, bf16[128,1024]{1,0:T(8,128)(2,1)S(1)}, u32[]{:S(2)}, u32[]{:S(2)}) collective-permute-start(bf16[128,1024]{1,0:T(8,128)(2,1)S(1)} %collective-permute-done.3.refs_1_), channel_id=1, source_target_pairs={{2,4},{4,2},{3,5},{5,3},{10,12},{12,10},{11,13},{13,11},{18,20},{2... | collective-permute-start | bytes 786440 | tf_op jit(solution)/shard_map/ppermute | solution.py:428
  33.8 12.9 %collective-permute-start.13 = (bf16[128,1024]{1,0:T(8,128)(2,1)S(1)}, bf16[128,1024]{1,0:T(8,128)(2,1)S(1)}, u32[]{:S(2)}, u32[]{:S(2)}) collective-permute-start(bf16[128,1024]{1,0:T(8,128)(2,1)S(1)} %tie.17.refs_0_), channel_id=1, source_target_pairs={{0,2},{2,0},{4,6},{6,4},{1,3},{3,1},{5,7},{7,5},{8,10},{10,8},{12,... | collective-permute-start | bytes 786440 | tf_op jit(solution)/shard_map/ppermute | solution.py:425
  42.1 13.9 %collective-permute-start.5 = (bf16[128,1536]{1,0:T(8,128)(2,1)S(1)}, bf16[128,1536]{1,0:T(8,128)(2,1)S(1)}, u32[]{:S(2)}, u32[]{:S(2)}) collective-permute-start(bf16[128,1536]{1,0:T(8,128)(2,1)S(1)} %tie.13.refs_4_), channel_id=1, source_target_pairs={{2,0},{4,6},{3,1},{5,7},{10,8},{12,14},{11,9},{13,15},{18,16},{20,... | collective-permute-start | bytes 1179656 | tf_op jit(solution)/shard_map/ppermute | solution.py:431
  46.7 13.0 %collective-permute-start.16 = (bf16[128,1024]{1,0:T(8,128)(2,1)S(1)}, bf16[128,1024]{1,0:T(8,128)(2,1)S(1)}, u32[]{:S(2)}, u32[]{:S(2)}) collective-permute-start(bf16[128,1024]{1,0:T(8,128)(2,1)S(1)} %tie.18.refs_4_), channel_id=1, source_target_pairs={{2,0},{4,6},{3,1},{5,7},{10,8},{12,14},{11,9},{13,15},{18,16},{20,... | collective-permute-start | bytes 786440 | tf_op jit(solution)/shard_map/ppermute | solution.py:431
  48.1 14.1 %collective-permute-start.26 = (bf16[256,512]{1,0:T(8,128)(2,1)S(1)}, bf16[256,512]{1,0:T(8,128)(2,1)S(1)}, u32[]{:S(2)}, u32[]{:S(2)}) collective-permute-start(bf16[256,512]{1,0:T(8,128)(2,1)S(1)} %get-tuple-element.77), channel_id=1, source_target_pairs={{0,8},{8,0},{16,24},{24,16},{1,9},{9,1},{17,25},{25,17},{2,10},{10... | collective-permute-start | bytes 786440 | tf_op jit(solution)/shard_map/ppermute | solution.py:45
  48.2 14.1 %collective-permute-start.27 = (bf16[256,512]{1,0:T(8,128)(2,1)S(1)}, bf16[256,512]{1,0:T(8,128)(2,1)S(1)}, u32[]{:S(2)}, u32[]{:S(2)}) collective-permute-start(bf16[256,512]{1,0:T(8,128)(2,1)S(1)} %get-tuple-element.78), channel_id=1, source_target_pairs={{0,8},{8,0},{16,24},{24,16},{1,9},{9,1},{17,25},{25,17},{2,10},{10... | collective-permute-start | bytes 786440 | tf_op jit(solution)/shard_map/ppermute | solution.py:45
  48.7 14.1 %collective-permute-start.28 = (bf16[256,512]{1,0:T(8,128)(2,1)S(1)}, bf16[256,512]{1,0:T(8,128)(2,1)S(1)}, u32[]{:S(2)}, u32[]{:S(2)}) collective-permute-start(bf16[256,512]{1,0:T(8,128)(2,1)S(1)} %get-tuple-element.79), channel_id=1, source_target_pairs={{0,8},{8,0},{16,24},{24,16},{1,9},{9,1},{17,25},{25,17},{2,10},{10... | collective-permute-start | bytes 786440 | tf_op jit(solution)/shard_map/ppermute | solution.py:45
  59.7 8.3 %collective-permute-start.6 = (bf16[128,1024]{1,0:T(8,128)(2,1)S(1)}, bf16[128,1024]{1,0:T(8,128)(2,1)S(1)}, u32[]{:S(2)}, u32[]{:S(2)}) collective-permute-start(bf16[128,1024]{1,0:T(8,128)(2,1)S(1)} %tie.14.refs_2_), channel_id=1, source_target_pairs={{2,0},{4,6},{3,1},{5,7},{10,8},{12,14},{11,9},{13,15},{18,16},{20,... | collective-permute-start | bytes 786440 | tf_op jit(solution)/shard_map/ppermute | solution.py:431
  62.3 8.0 %collective-permute-start.34 = (bf16[192,512]{1,0:T(8,128)(2,1)S(1)}, bf16[192,512]{1,0:T(8,128)(2,1)S(1)}, u32[]{:S(2)}, u32[]{:S(2)}) collective-permute-start(bf16[192,512]{1,0:T(8,128)(2,1)S(1)} %get-tuple-element.99), channel_id=1, source_target_pairs={{0,8},{8,0},{16,24},{24,16},{1,9},{9,1},{17,25},{25,17},{2,10},{10... | collective-permute-start | bytes 589832 | tf_op jit(solution)/shard_map/ppermute | solution.py:45
  62.8 8.1 %collective-permute-start.35 = (bf16[192,512]{1,0:T(8,128)(2,1)S(1)}, bf16[192,512]{1,0:T(8,128)(2,1)S(1)}, u32[]{:S(2)}, u32[]{:S(2)}) collective-permute-start(bf16[192,512]{1,0:T(8,128)(2,1)S(1)} %get-tuple-element.100), channel_id=1, source_target_pairs={{0,8},{8,0},{16,24},{24,16},{1,9},{9,1},{17,25},{25,17},{2,10},{10... | collective-permute-start | bytes 589832 | tf_op jit(solution)/shard_map/ppermute | solution.py:45
  62.9 11.5 %collective-permute-start.11 = (bf16[128,1024]{1,0:T(8,128)(2,1)S(1)}, bf16[128,1024]{1,0:T(8,128)(2,1)S(1)}, u32[]{:S(2)}, u32[]{:S(2)}) collective-permute-start(bf16[128,1024]{1,0:T(8,128)(2,1)S(1)} %tie.17.refs_0_), channel_id=1, source_target_pairs={{2,4},{4,2},{3,5},{5,3},{10,12},{12,10},{11,13},{13,11},{18,20},{2... | collective-permute-start | bytes 786440 | tf_op jit(solution)/shard_map/ppermute | solution.py:428
  63.7 12.2 %collective-permute-start.20 = (bf16[128,1024]{1,0:T(8,128)(2,1)S(1)}, bf16[128,1024]{1,0:T(8,128)(2,1)S(1)}, u32[]{:S(2)}, u32[]{:S(2)}) collective-permute-start(bf16[128,1024]{1,0:T(8,128)(2,1)S(1)} %collective-permute-done.13.refs_1_), channel_id=1, source_target_pairs={{2,4},{4,2},{3,5},{5,3},{10,12},{12,10},{11,13},{13,11},{18,20},{2... | collective-permute-start | bytes 786440 | tf_op jit(solution)/shard_map/ppermute | solution.py:428
  74.4 22.6 %collective-permute-start.37 = (bf16[384,512]{1,0:T(8,128)(2,1)S(1)}, bf16[384,512]{1,0:T(8,128)(2,1)S(1)}, u32[]{:S(2)}, u32[]{:S(2)}) collective-permute-start(bf16[384,512]{1,0:T(8,128)(2,1)S(1)} %get-tuple-element.103), channel_id=1, source_target_pairs={{0,16},{8,24},{16,0},{24,8},{1,17},{9,25},{17,1},{25,9},{2,18},{10... | collective-permute-start | bytes 1179656 | tf_op jit(solution)/shard_map/ppermute | solution.py:45
  75.9 14.2 %collective-permute-start.17 = (bf16[128,1024]{1,0:T(8,128)(2,1)S(1)}, bf16[128,1024]{1,0:T(8,128)(2,1)S(1)}, u32[]{:S(2)}, u32[]{:S(2)}) collective-permute-start(bf16[128,1024]{1,0:T(8,128)(2,1)S(1)} %tie.19.refs_2_), channel_id=1, source_target_pairs={{2,0},{4,6},{3,1},{5,7},{10,8},{12,14},{11,9},{13,15},{18,16},{20,... | collective-permute-start | bytes 786440 | tf_op jit(solution)/shard_map/ppermute | solution.py:431
  78.0 17.5 %collective-permute-start.21 = (bf16[128,1024]{1,0:T(8,128)(2,1)S(1)}, bf16[128,1024]{1,0:T(8,128)(2,1)S(1)}, u32[]{:S(2)}, u32[]{:S(2)}) collective-permute-start(bf16[128,1024]{1,0:T(8,128)(2,1)S(1)} %tie.21.refs_4_), channel_id=1, source_target_pairs={{2,0},{4,6},{3,1},{5,7},{10,8},{12,14},{11,9},{13,15},{18,16},{20,... | collective-permute-start | bytes 786440 | tf_op jit(solution)/shard_map/ppermute | solution.py:431
  79.3 11.5 %collective-permute-start.8 = (bf16[128,512]{1,0:T(8,128)(2,1)S(1)}, bf16[128,512]{1,0:T(8,128)(2,1)S(1)}, u32[]{:S(2)}, u32[]{:S(2)}) collective-permute-start(bf16[128,512]{1,0:T(8,128)(2,1)S(1)} %tie.15.refs_0_), channel_id=1, source_target_pairs={{2,4},{4,2},{3,5},{5,3},{10,12},{12,10},{11,13},{13,11},{18,20},{2... | collective-permute-start | bytes 393224 | tf_op jit(solution)/shard_map/ppermute | solution.py:428
  80.1 18.1 %collective-permute-start.43 = (bf16[256,512]{1,0:T(8,128)(2,1)S(1)}, bf16[256,512]{1,0:T(8,128)(2,1)S(1)}, u32[]{:S(2)}, u32[]{:S(2)}) collective-permute-start(bf16[256,512]{1,0:T(8,128)(2,1)S(1)} %get-tuple-element.110), channel_id=1, source_target_pairs={{0,16},{8,24},{16,0},{24,8},{1,17},{9,25},{17,1},{25,9},{2,18},{10... | collective-permute-start | bytes 786440 | tf_op jit(solution)/shard_map/ppermute | solution.py:45
  90.1 7.4 %collective-permute-start.19 = (bf16[128,512]{1,0:T(8,128)(2,1)S(1)}, bf16[128,512]{1,0:T(8,128)(2,1)S(1)}, u32[]{:S(2)}, u32[]{:S(2)}) collective-permute-start(bf16[128,512]{1,0:T(8,128)(2,1)S(1)} %collective-permute-done.7.refs_1_), channel_id=1, source_target_pairs={{2,4},{4,2},{3,5},{5,3},{10,12},{12,10},{11,13},{13,11},{18,20},{2... | collective-permute-start | bytes 393224 | tf_op jit(solution)/shard_map/ppermute | solution.py:428
  100.8 16.8 %collective-permute-start.38 = (bf16[384,512]{1,0:T(8,128)(2,1)S(1)}, bf16[384,512]{1,0:T(8,128)(2,1)S(1)}, u32[]{:S(2)}, u32[]{:S(2)}) collective-permute-start(bf16[384,512]{1,0:T(8,128)(2,1)S(1)} %mine.4.refs_0_), channel_id=1, source_target_pairs={{0,1},{1,0},{2,3},{3,2},{4,5},{5,4},{6,7},{7,6},{8,9},{9,8},{10,11... | collective-permute-start | bytes 1179656 | tf_op jit(solution)/shard_map/ppermute | solution.py:434
  107.1 8.3 %collective-permute-start.32 = (bf16[256,512]{1,0:T(8,128)(2,1)S(1)}, bf16[256,512]{1,0:T(8,128)(2,1)S(1)}, u32[]{:S(2)}, u32[]{:S(2)}) collective-permute-start(bf16[256,512]{1,0:T(8,128)(2,1)S(1)} %get-tuple-element.94), channel_id=1, source_target_pairs={{0,8},{8,0},{16,24},{24,16},{1,9},{9,1},{17,25},{25,17},{2,10},{10... | collective-permute-start | bytes 786440 | tf_op jit(solution)/shard_map/ppermute | solution.py:45
  107.6 9.9 %collective-permute-start.44 = (bf16[256,512]{1,0:T(8,128)(2,1)S(1)}, bf16[256,512]{1,0:T(8,128)(2,1)S(1)}, u32[]{:S(2)}, u32[]{:S(2)}) collective-permute-start(bf16[256,512]{1,0:T(8,128)(2,1)S(1)} %mine.5.refs_0_), channel_id=1, source_target_pairs={{0,1},{1,0},{2,3},{3,2},{4,5},{5,4},{6,7},{7,6},{8,9},{9,8},{10,11... | collective-permute-start | bytes 786440 | tf_op jit(solution)/shard_map/ppermute | solution.py:434
  109.3 10.1 %collective-permute-start.55 = (bf16[256,512]{1,0:T(8,128)(2,1)S(1)}, bf16[256,512]{1,0:T(8,128)(2,1)S(1)}, u32[]{:S(2)}, u32[]{:S(2)}) collective-permute-start(bf16[256,512]{1,0:T(8,128)(2,1)S(1)} %get-tuple-element.121), channel_id=1, source_target_pairs={{0,16},{8,24},{16,0},{24,8},{1,17},{9,25},{17,1},{25,9},{2,18},{10... | collective-permute-start | bytes 786440 | tf_op jit(solution)/shard_map/ppermute | solution.py:45
  112.5 8.5 %collective-permute-start.31 = (bf16[4,128,128]{2,1,0:T(8,128)(2,1)S(1)}, bf16[4,128,128]{2,1,0:T(8,128)(2,1)S(1)}, u32[]{:S(2)}, u32[]{:S(2)}) collective-permute-start(bf16[4,128,128]{2,1,0:T(8,128)(2,1)S(1)} %add.3.refs_0_), channel_id=1, source_target_pairs={{0,16},{8,24},{16,0},{24,8},{1,17},{9,25},{17,1},{25,9},{2,18},{10... | collective-permute-start | bytes 393224 | tf_op jit(solution)/shard_map/ppermute | solution.py:45
  119.4 8.6 %collective-permute-start.56 = (bf16[256,512]{1,0:T(8,128)(2,1)S(1)}, bf16[256,512]{1,0:T(8,128)(2,1)S(1)}, u32[]{:S(2)}, u32[]{:S(2)}) collective-permute-start(bf16[256,512]{1,0:T(8,128)(2,1)S(1)} %mine.7.refs_0_), channel_id=1, source_target_pairs={{0,1},{1,0},{2,3},{3,2},{4,5},{5,4},{6,7},{7,6},{8,9},{9,8},{10,11... | collective-permute-start | bytes 786440 | tf_op jit(solution)/shard_map/ppermute | solution.py:434
  (26 other events, 122.9 us)

commit v3 on v2

--- a/solution.py
+++ b/solution.py
@@ -11,7 +11,21 @@
 HEAD = 128
 BLK = 64
 EIGHTHS = (3, 2, 2, 1)
-CORE_SENDS = (4, 4, 8, 1)
+GROUPS = ((0,), (1, 2, 3))
+CORE_SENDS = (4, 4, 4, 2)
+TOP_SENDS = (2, 1, 1, 1)
+LAST_SENDS = (1, 1, 1, 1)
+AFTER = {
+    'cut': ('wcore',),
+    'b2_1': ('c1_0',),
+    'c1_1': ('b2_0',),
+    'c2_2': ('prev',),
+    'send_3': ('last_0', 'mine_1'),
+    'late': ('qg',),
+    'mine_3': ('later', 'late'),
+    'fold_2': ('c2_3',),
+    'fold_3': ('last_0',),
+}
 F32 = jnp.float32
 BF16 = jnp.bfloat16
 NT = (((1,), (1,)), ((), ()))
@@ -82,29 +96,37 @@
     )(*in_vmem(*arrays), *after)
 
 
-def load(pieces):
-    count = len(pieces)
+def load(pieces, cuts=()):
+    sources = [x for x, _, _ in pieces] + [x for x, _ in cuts]
+    shapes = [(rows, x.shape[1]) for x, _, rows in pieces]
+    shapes += [(x.shape[0], sum(width for _, width in columns(0))) for x, columns in cuts]
+    count = len(sources)
 
     def kernel(*refs):
-        sources, targets, sems = refs[:count], refs[count:-1], refs[-1]
-        copies = [
-            pltpu.make_async_copy(source.at[pl.ds(first, rows)], target, sems.at[i])
-            for i, (source, target, (_, first, rows)) in enumerate(zip(sources, targets, pieces))
-        ]
-        for copy in copies:
-            copy.start()
-        for copy in copies:
-            copy.wait()
+        refs, targets, sems = refs[:count], refs[count:-1], refs[-1]
+        for i, (_, first, rows) in enumerate(pieces):
+            pltpu.make_async_copy(refs[i].at[pl.ds(first, rows)], targets[i], sems.at[i]).start()
+        here = lax.axis_index("ctx")
+        for i, (_, columns) in enumerate(cuts, len(pieces)):
+            at = 0
+            for start, width in columns(here):
+                pltpu.make_async_copy(
+                    refs[i].at[:, pl.ds(pl.multiple_of(start, 128), width)],
+                    targets[i].at[:, pl.ds(at, width)], sems.at[i]
+                ).start()
+                at += width
+        for i, target in enumerate(targets):
+            pltpu.make_async_copy(target, target, sems.at[i]).wait()
 
     return pl.pallas_call(
         kernel,
         in_specs=[HBM] * count,
         out_specs=[VMEM] * count,
-        out_shape=[pltpu.VMEM((rows, x.shape[1]), x.dtype) for x, _, rows in pieces],
+        out_shape=[pltpu.VMEM(shape, x.dtype) for shape, x in zip(shapes, sources)],
         scratch_shapes=[pltpu.SemaphoreType.DMA((count,))],
         compiler_params=params(1),
         name="load",
-    )(*in_hbm(*[x for x, _, _ in pieces]))
+    )(*in_hbm(*sources))
 
 
 def in_rows(array, count):
@@ -127,37 +149,32 @@
     return found[0] if len(found) == 1 else jnp.concatenate(found, axis=0)
 
 
-def cut(whole, order, offsets, pieces):
+def columns_of(group, order, block):
+    return lambda here: [((here ^ j) * block + offset, piece) for offset, piece in group for j in order]
+
+
+def cut(whole, order, groups, after=()):
     rows, model = whole.shape
     block = model // len(order)
-    if pieces[-1] % 128:
+    widths = [sum(piece for _, piece in group) * len(order) for group in groups]
+    if any(piece % 128 for group in groups for _, piece in group):
         here = lax.axis_index("ctx")
         return [
-            jnp.concatenate([lax.dynamic_slice(whole, (0, (here ^ j) * block + o), (rows, p)) for j in order], axis=1)
-            for o, p in zip(offsets, pieces)
+            jnp.concatenate([
+                lax.dynamic_slice(whole, (0, at), (rows, piece)) for at, piece in columns_of(group, order, block)(here)
+            ], axis=1)
+            for group in groups
         ]
 
-    def kernel(source, *refs):
-        targets, sems = refs[:-1], refs[-1]
+    def body(source, *targets):
         here = lax.axis_index("ctx")
-        for i, (offset, piece) in enumerate(zip(offsets, pieces)):
-            for p, j in enumerate(order):
-                at = pl.multiple_of((here ^ j) * block + offset, 128)
-                pltpu.make_async_copy(
-                    source.at[:, pl.ds(at, piece)], targets[i].at[:, pl.ds(p * piece, piece)], sems.at[i]
-                ).start()
-        for i, target in enumerate(targets):
-            pltpu.make_async_copy(target, target, sems.at[i]).wait()
-
-    return list(pl.pallas_call(
-        kernel,
-        in_specs=[HBM],
-        out_specs=[VMEM] * len(pieces),
-        out_shape=[pltpu.VMEM((rows, piece * len(order)), whole.dtype) for piece in pieces],
-        scratch_shapes=[pltpu.SemaphoreType.DMA((len(pieces),))],
-        compiler_params=params(1),
-        name="cut",
-    )(*in_hbm(whole)))
+        for target, group in zip(targets, groups):
+            column = 0
+            for at, piece in columns_of(group, order, block)(here):
+                target[:, column:column + piece] = source[:, pl.ds(pl.multiple_of(at, 128), piece)]
+                column += piece
+
+    return on_vmem(body, [((rows, width), whole.dtype) for width in widths], [whole], after=after, name="cut")
 
 
 def scan_states(state, sc, later):
@@ -210,11 +227,11 @@
         for h, at in enumerate(heads_of(q_ref)):
             k_here = k_ref[:, at]
             s_ref[h] = (mm(q_ref[:, at], k_here, NT) * mask_ref[...]).astype(BF16)
-            kv_ref[h] = mm(k_here, v_ref[:, at], TN)
+            kv_ref[h] = mm(k_here, v_ref[:, at], TN).astype(BF16)
 
     return on_vmem(
         body,
-        [((length, length), F32), ((heads, length, length), BF16), ((heads, HEAD, HEAD), F32)],
+        [((length, length), F32), ((heads, length, length), BF16), ((heads, HEAD, HEAD), BF16)],
         [table, q, k, v],
         name="early",
     )
@@ -284,7 +301,7 @@
 
 
 def fold(blocks, opened, norm, ws, products, acc, q, sends, after=()):
-    own, a, b1, c1, b2, c2 = blocks
+    own, a, (b1, b1_at), (c1, c1_at), b2, c2 = blocks
     rows, wide = own.shape
     length, width = opened.shape
     half = wide // 2
@@ -318,9 +335,9 @@
         grad = third_ref if whole else refs.pop(0)
         here = lax.axis_index("tsp")
 
-        def place(ref, at, under=0):
+        def place(ref, at, under=0, column=0):
             count = ref.shape[0]
-            grad[pl.ds(pl.multiple_of(at * rows + under, count), count), :] = ref[...]
+            grad[pl.ds(pl.multiple_of(at * rows + under, count), count), :] = ref[:, column:column + wide]
 
         at_end = (here == 0) | (here == 3)
         near, far = jnp.where(here < 2, 2, 1), jnp.where(here < 2, 3, 0)
@@ -329,13 +346,13 @@
 
         @pl.when(at_end)
         def _():
-            place(c1_ref, near)
+            place(c1_ref, near, 0, c1_at)
             for i, ref in enumerate(c2_refs):
                 place(ref, far, i * ref.shape[0])
 
         @pl.when(jnp.logical_not(at_end))
         def _():
-            place(b1_ref, near)
+            place(b1_ref, near, 0, b1_at)
             place(b2_ref, far)
 
         sent = (mm(grad[:, half:], opened_ref[...], TN) * norm).astype(BF16)
@@ -367,27 +384,31 @@
     )(*in_vmem(*arrays), *after)
 
 
-def scatter_step(keep, sends, bit):
+def scatter_step(keep, sends, bit, parts=1):
     came = [swap(x, "ctx", bit) for x in sends]
     half, width = keep.shape[0] // 2, keep.shape[1]
 
     def body(keep_ref, *refs):
-        first_ref, second_ref = refs[-2:]
-        came_refs = refs[:-2]
+        came_refs, first_ref, second_refs = refs[:len(came)], refs[len(came)], refs[len(came) + 1:]
         first_ref[...] = keep_ref[:half, :] + rows_of(came_refs, 0, half).astype(F32)
-        second_ref[...] = (keep_ref[half:, :] + rows_of(came_refs, half, half).astype(F32)).astype(BF16)
-
-    return on_vmem(
-        body, [((half, width), F32), ((half, width), BF16)], [keep, *came], name="split")
+        rows = half // parts
+        for i, ref in enumerate(second_refs):
+            at = half + i * rows
+            ref[...] = (keep_ref[at:at + rows, :] + rows_of(came_refs, at, rows).astype(F32)).astype(BF16)
+
+    got = on_vmem(
+        body, [((half, width), F32)] + [((half // parts, width), BF16)] * parts, [keep, *came], name="split")
+    return got[0], got[1:]
 
 
 def finish(mine, came, offset, length, target):
-    rows, width = mine.shape
+    rows, width = sum(x.shape[0] for x in mine), mine[0].shape[1]
+    arrays = [*mine, *came]
 
     def kernel(*refs):
-        mine_ref, came_ref = refs[:2]
         out_ref, total, sem = refs[-3:]
-        total[...] = mine_ref[...].astype(F32) + came_ref[...].astype(F32)
+        ours = rows_of(refs[:len(mine)], 0, rows).astype(F32)
+        total[...] = ours + rows_of(refs[len(mine):len(arrays)], 0, rows).astype(F32)
         copy = pltpu.make_async_copy(total, out_ref.at[pl.ds(offset, rows)], sem)
         copy.start()
         copy.wait()
@@ -395,14 +416,14 @@
     extra = [] if target is None else [target]
     return pl.pallas_call(
         kernel,
-        in_specs=[VMEM] * 2 + [HBM] * len(extra),
+        in_specs=[VMEM] * len(arrays) + [HBM] * len(extra),
         out_specs=HBM,
         out_shape=pltpu.HBM((length, width), F32),
-        input_output_aliases={} if target is None else {2: 0},
+        input_output_aliases={} if target is None else {len(arrays): 0},
         scratch_shapes=[pltpu.VMEM((rows, width), F32), pltpu.SemaphoreType.DMA],
         compiler_params=params(),
         name="finish",
-    )(*in_vmem(mine, came), *extra)
+    )(*in_vmem(*arrays), *extra)
 
 
 def shards(queries, keys, values, attn_out, out_grad, out_weight, block_mask):
@@ -433,94 +454,132 @@
     def other(x):
         return lax.ppermute(x, "dp", [(0, 1), (1, 0)])
 
-    own = cut(grad, order, offsets, pieces)
-    first = pieces[0]
-    q, k, v, opened, w_here, w_low, w_high = load(
+    a_all, b_all = outer(grad), inner(grad)
+    parts = list(zip(offsets, pieces))
+    single = [[part] for part in parts]
+    aligned = all(piece % 128 == 0 for piece in pieces)
+    q, k, v, opened, w_here, w_low, w_high, *own = load(
         [(x[0], 0, group_len) for x in (queries, keys, values, attn_out)]
-        + [(out_weight, 0, block), (out_weight, 0, first), (out_weight, first, block - first)])
-    a, b1, b2, c1, c2 = [[None] * count for _ in range(5)]
-
-    def step_a(i, *after):
-        if after:
-            own[i] = tie(own[i], *after)
-        a[i], b1[i] = outer(own[i]), inner(own[i])
-        b2[i] = inner(a[i])
-
-    def step_c1(i, *after):
-        b1[i] = tie(b1[i], *after)
-        c1[i] = to_ends(b1[i])
-
-    def step_c2(i, *after, parts=1):
-        b2[i] = tie(b2[i], *after)
-        c2[i] = [to_ends(x) for x in (in_rows(b2[i], parts) if parts > 1 else [b2[i]])]
-
-    step_a(0)
-    step_a(1)
+        + [(out_weight, 0, block), (out_weight, 0, block // 2), (out_weight, block // 2, block // 2)],
+        [(grad, columns_of(group, order, block)) for group in single] if aligned else [])
+    if not aligned:
+        own = cut(grad, order, single)
 
     held = {0: [w_here]}
     for bit in reversed(bits[1:]):
         for j in list(held):
-            held[j | bit] = [swap(held[j][0], "ctx", bit)]
+            held[j | bit] = [swap(held[j][0] if j else out_weight, "ctx", bit)]
     for j in list(held):
-        if j == 0:
-            w_low = tie(w_low, a[1])
-            held[j | bits[0]] = [swap(x, "ctx", bits[0]) for x in (w_low, w_high)]
-        else:
-            held[j | bits[0]] = [swap(x, "ctx", bits[0]) for x in in_rows(held[j][0], 4)]
+        rows_here = in_rows(held[j][0], 4) if j else (w_low, w_high)
+        held[j | bits[0]] = [swap(x, "ctx", bits[0]) for x in rows_here]
     ws = [held[j] for j in order]
 
-    mask, s, kv = early(q, k, v, block_mask[0, 0], sc)
-    prev, _ = scan_states(kv, sc, False)
-
-    step_c1(0, a[0])
-    step_c2(0, a[1], held[bits[0]][0])
-    step_a(2, c1[0])
-    step_c1(1, *c2[0])
-    step_c2(1, a[2], prev)
-    step_a(3, c1[1])
-    step_c1(2, *c2[1])
-    step_c2(2, a[3])
-    step_c1(3, c1[2])
-    step_c2(3, *c2[2], parts=2)
-
-    def add_top(keep, send, after=()):
-        return on_vmem(
-            add_kernel, [(keep.shape, BF16)], [keep, swap(send, "ctx", top)], after=after, name="mine")[0]
-
-    keeps, sends, mine, theirs = [[None] * count for _ in range(4)]
-    acc = kept = qg = None
-    for i in range(count):
+    made, final_form = {"wcore": held[bits[0]]}, {}
+
+    def get(name):
+        if name not in made:
+            kind, _, number = name.partition("_")
+            made[name] = builders[kind](*([int(number)] if number else []))
+        return made[name]
+
+    def after(name):
+        found = []
+        for other_name in AFTER.get(name, ()):
+            got = get(other_name)
+            found += [got] if isinstance(got, jax.Array) else list(got)
+        return found
+
+    def tied(name, array):
+        waits = after(name)
+        final_form[name] = tie(array, *waits) if waits else array
+        return final_form[name]
+
+    def build_cut():
+        waits = after("cut")
+        return cut(b_all, order, [[parts[i] for i in group] for group in GROUPS], waits), cut(
+            a_all, order, single, waits)
+
+    def group_of(i):
+        return next(g for g, group in enumerate(GROUPS) if i in group)
+
+    def build_c1(g):
+        return to_ends(tied(f"c1_{g}", get("cut")[0][g]))
+
+    def build_b2(i):
+        return inner(tied(f"b2_{i}", get("cut")[1][i]))
+
+    def build_c2(i):
+        return to_ends(tied(f"c2_{i}", get(f"b2_{i}")))
+
+    def build_early():
+        return early(q, k, v, block_mask[0, 0], sc)
+
+    def build_prev():
+        return scan_states(get("early")[2], sc, False)[0]
+
+    def build_fold(i):
         last = i == count - 1
+        g = group_of(i)
+        c2 = get(f"c2_{i}")
+        c1 = get(f"c1_{g}")
+        at = (offsets[i] - offsets[GROUPS[g][0]]) * ctx
+        blocks = (
+            own[i], final_form[f"b2_{i}"], (final_form[f"c1_{g}"], at), (c1, at), final_form[f"c2_{i}"], [c2])
         products = [] if i == 0 else [(None, offsets[i])]
         if i == 1:
-            products.insert(0, (kept, offsets[0]))
-        keep, *rest = fold(
-            (own[i], a[i], b1[i], c1[i], b2[i], c2[i]), opened, norm, ws, products, acc,
-            q if last else None, CORE_SENDS[i])
-        send, third, more = rest[:CORE_SENDS[i]], rest[CORE_SENDS[i]], rest[CORE_SENDS[i] + 1:]
-        if i == 0:
-            kept = third
-        else:
-            acc = third
-        if last:
-            qg = more[0]
+            products.insert(0, (get("fold_0")[-1], offsets[0]))
+        acc = get(f"fold_{i - 1}")[CORE_SENDS[i - 1] + 1] if i > 1 else None
+        return fold(
+            blocks, opened, norm, ws, products, acc, q if last else None, CORE_SENDS[i], after(f"fold_{i}"))
+
+    def build_send(i):
+        got = get(f"fold_{i}")
+        keep, sends = got[0], got[1:1 + CORE_SENDS[i]]
         for bit in bits[:-1]:
-            keep, send = scatter_step(keep, send, bit)
-            send = [send]
-        keeps[i], sends[i] = keep, send[0]
-    og = acc
-    for i in range(count - 2):
-        mine[i] = add_top(keeps[i], sends[i])
-        theirs[i] = other(mine[i])
-    later, total_qg = scan_states(qg, sc, True)
-    dq, dkp, dvp = late(q, k, v, og, s, prev, mask, (total_qg,))
-    mine[-2] = add_top(keeps[-2], sends[-2], (dkp,))
-    mine[-1] = add_top(keeps[-1], tie(sends[-1], *theirs[:-2]), (later,))
-    theirs[-2], theirs[-1] = other(mine[-2]), other(mine[-1])
-    dk, dv = final(k, v, later, dkp, dvp, ())
+            keep, sends = scatter_step(keep, sends, bit, TOP_SENDS[i] if bit == bits[-2] else 1)
+        keeps[i] = keep
+        waits = after(f"send_{i}")
+        return [tie(x, *waits) for x in sends] if waits else sends
+
+    def build_mine(i):
+        sends = get(f"send_{i}")
+        keep, came = keeps[i], [swap(x, "ctx", top) for x in sends]
+        rows = keep.shape[0] // LAST_SENDS[i]
+
+        def body(keep_ref, *refs):
+            for n, ref in enumerate(refs[len(came):]):
+                here = rows_of([keep_ref], n * rows, rows) + rows_of(refs[:len(came)], n * rows, rows).astype(F32)
+                ref[...] = here.astype(BF16)
+
+        return on_vmem(
+            body, [((rows, width), BF16)] * LAST_SENDS[i], [keep, *came], after=after(f"mine_{i}"), name="mine")
+
+    def build_last(i):
+        return [other(x) for x in get(f"mine_{i}")]
+
+    def build_later():
+        return scan_states(get(f"fold_{count - 1}")[-1], sc, True)
+
+    def build_late():
+        mask, s, _ = get("early")
+        og = get(f"fold_{count - 1}")[-2]
+        return late(q, k, v, og, s, get("prev"), mask, after("late"))
+
+    def build_final():
+        _, dkp, dvp = get("late")
+        return final(k, v, get("later")[0], dkp, dvp, after("final"))
+
+    keeps = [None] * count
+    builders = {
+        "cut": build_cut, "c1": build_c1, "b2": build_b2, "c2": build_c2, "early": build_early, "prev": build_prev,
+        "fold": build_fold, "send": build_send, "mine": build_mine, "last": build_last, "later": build_later,
+        "qg": lambda: get("later")[1], "late": build_late, "final": build_final,
+    }
     grown = None
     for i in range(count):
-        grown = finish(mine[i], theirs[i], offsets[i], block, grown)
+        grown = finish(get(f"mine_{i}"), get(f"last_{i}"), offsets[i], block, grown)
+    dq = get("late")[0]
+    dk, dv = get("final")
     return dq[None], dk[None], dv[None], grown
 
 

time: 131 us -> 115 us (0.88)
  starting transfers between devices: 55.2 us -> 35.2 us
  waiting for transfers between devices: 55.1 us -> 58.5 us
    ppermute x4 -> x1, starting transfers between devices: 16.8 us -> 3.09 us  [outer(): return lax.ppermute(x, 'tsp', [(0, 1), (1, 0), (2, 3), (3, 2)])]
    ppermute x4 -> x1, waiting for transfers between devices: 8.87 us -> 17.3 us  [outer(): return lax.ppermute(x, 'tsp', [(0, 1), (1, 0), (2, 3), (3, 2)])]
    ppermute x9 -> x6, waiting for transfers between devices: 36.5 us -> 28.8 us  [to_ends(): return lax.ppermute(x, 'tsp', [(1, 0), (2, 3)])]
    ppermute x9 -> x6, starting transfers between devices: 11.6 us -> 7.72 us  [to_ends(): return lax.ppermute(x, 'tsp', [(1, 0), (2, 3)])]
    ppermute x32 -> x30, waiting for transfers between devices: 6.35 us -> 9.49 us  [swap(): return lax.ppermute(array, axis, [(i, i ^ bit) for i in range(count)])]
    ppermute x8 -> x5, starting transfers between devices: 5.35 us -> 3.4 us  [inner(): return lax.ppermute(x, 'tsp', [(1, 2), (2, 1)])]
    pallas_call x5 -> x4, Pallas kernels: 4.66 us -> 3.42 us  [finish(): pl.pallas_call(kernel, in_specs=[VMEM] * len(arrays) + [HBM] * len(extra)...]
    ppermute x32 -> x30, starting transfers between devices: 15.6 us -> 14.7 us  [swap(): return lax.ppermute(array, axis, [(i, i ^ bit) for i in range(count)])]
  transfers between devices with their start and end apart: 57 -> 46, of which waited for: 19 -> 14; matrix products, arithmetic and copies ran while one was open for 0% -> 0% of each run, Pallas kernels for 13% -> 15%
where the time goes in v3:
time: 115 us; the launch traced here: 114 us
  waiting for transfers between devices  58.5 us (51%)
  starting transfers between devices  35.2 us (31%)
  Pallas kernels  18.1 us (16%)
  between operations  1.3 us (1%)
    ppermute x6, waiting for transfers between devices, to_ends(): return lax.ppermute(x, 'tsp', [(1, 0), (2, 3)])  28.8 us
    ppermute x1, waiting for transfers between devices, outer(): return lax.ppermute(x, 'tsp', [(0, 1), (1, 0), (2, 3), (3, 2)])  17.3 us
    ppermute x30, starting transfers between devices, swap(): return lax.ppermute(array, axis, [(i, i ^ bit) for i in range(count)])  14.7 us
    ppermute x30, waiting for transfers between devices, swap(): return lax.ppermute(array, axis, [(i, i ^ bit) for i in range(count)])  9.49 us
    ppermute x6, starting transfers between devices, to_ends(): return lax.ppermute(x, 'tsp', [(1, 0), (2, 3)])  7.72 us
    ppermute x4, starting transfers between devices, other(): return lax.ppermute(x, 'dp', [(0, 1), (1, 0)])  6.34 us
    pallas_call x4, Pallas kernels, fold(): pl.pallas_call(kernel, in_specs=[VMEM] * len(arrays) + [ANY] * len(after)...  5.96 us
    pallas_call x4, Pallas kernels, finish(): pl.pallas_call(kernel, in_specs=[VMEM] * len(arrays) + [HBM] * len(extra)...  3.42 us
  transfers between devices with their start and end apart: 46, of which 14 were waited for; matrix products, arithmetic and copies ran while one was open for 0% of the time, Pallas kernels for 15%

profile of v3, /device:TPU:0, one launch (start us, length us, event | category | flops | bytes accessed | tf_op | source)
XLA Modules:
  0.0 114.2 jit_solution(3538569939884649555)
XLA Ops:
  0.6 3.1 %collective-permute-start = (bf16[128,4096]{1,0:T(8,128)(2,1)}, bf16[128,4096]{1,0:T(8,128)(2,1)S(1)}, u32[]{:S(2)}, u32[]{:S(2)}) collective-permute-start(bf16[128,4096]{1,0:T(8,128)(2,1)} %bitcast.11), channel_id=1, source_target_pairs={{0,2},{2,0},{4,6},{6,4},{1,3},{3,1},{5,7},{7,5},{8,10},{10,8},{12,... | collective-permute-start | bytes 3145736 | tf_op jit(solution)/shard_map/ppermute | solution.py:446
  4.5 2.6 %load.1 = (bf16[512,512]{1,0:T(8,128)(2,1)S(1)}, bf16[512,512]{1,0:T(8,128)(2,1)S(1)}, bf16[512,512]{1,0:T(8,128)(2,1)S(1)}, bf16[512,512]{1,0:T(8,128)(2,1)S(1)...) custom-call(bf16[512,512]{1,0:T(8,128)(2,1)} %bitcast.17, ...), custom_call_target="tpu_custom_call" | custom-call | tf_op jit(solution)/shard_map/load/pallas_call | solution.py:121
  7.6 1.5 %collective-permute-start.8 = (bf16[1024,512]{1,0:T(8,128)(2,1)S(1)}, bf16[1024,512]{1,0:T(8,128)(2,1)S(1)}, u32[]{:S(2)}, u32[]{:S(2)}) collective-permute-start(bf16[1024,512]{1,0:T(8,128)(2,1)S(1)} %copy-done.2), channel_id=1, source_target_pairs={{0,16},{8,24},{16,0},{24,8},{1,17},{9,25},{17,1},{25,9},{2,18},{10... | collective-permute-start | bytes 3145736 | tf_op jit(solution)/shard_map/ppermute | solution.py:59
  9.7 17.3 %collective-permute-done.refs_0_ = bf16[128,4096]{1,0:T(8,128)(2,1)S(1)} collective-permute-done((bf16[128,4096]{1,0:T(8,128)(2,1)}, bf16[128,4096]{1,0:T(8,128)(2,1)S(1)}, u32[]{:S(2)}, u32[]{:S(2)}) %collective-permute-start) | collective-permute-done | bytes 1048608 | tf_op jit(solution)/shard_map/ppermute | solution.py:446
  28.1 1.3 %collective-permute-start.17 = (bf16[128,1536]{1,0:T(8,128)(2,1)S(1)}, bf16[128,1536]{1,0:T(8,128)(2,1)S(1)}, u32[]{:S(2)}, u32[]{:S(2)}) collective-permute-start(bf16[128,1536]{1,0:T(8,128)(2,1)S(1)} %get-tuple-element.85.refs_2_), channel_id=1, source_target_pairs={{2,0},{4,6},{3,1},{5,7},{10,8},{12,14},{11,9},{13,15},{18,16},{20,... | collective-permute-start | bytes 1179656 | tf_op jit(solution)/shard_map/ppermute | solution.py:452
  30.6 1.3 %collective-permute-start.20 = (bf16[128,1536]{1,0:T(8,128)(2,1)S(1)}, bf16[128,1536]{1,0:T(8,128)(2,1)S(1)}, u32[]{:S(2)}, u32[]{:S(2)}) collective-permute-start(bf16[128,1536]{1,0:T(8,128)(2,1)S(1)} %collective-permute-done.4.refs_1_.refs_4_), channel_id=1, source_target_pairs={{2,0},{4,6},{3,1},{5,7},{10,8},{12,14},{11,9},{13,15},{18,16},{20,... | collective-permute-start | bytes 1179656 | tf_op jit(solution)/shard_map/ppermute | solution.py:452
  32.0 1.7 %collective-permute-start.15 = (bf16[4,128,128]{2,1,0:T(8,128)(2,1)S(1)}, bf16[4,128,128]{2,1,0:T(8,128)(2,1)S(1)}, u32[]{:S(2)}, u32[]{:S(2)}) collective-permute-start(bf16[4,128,128]{2,1,0:T(8,128)(2,1)S(1)} %add.2), channel_id=1, source_target_pairs={{0,16},{8,24},{16,0},{24,8},{1,17},{9,25},{17,1},{25,9},{2,18},{10... | collective-permute-start | bytes 393224 | tf_op jit(solution)/shard_map/ppermute | solution.py:59
  34.4 3.6 %collective-permute-done.15.refs_1_ = bf16[4,128,128]{2,1,0:T(8,128)(2,1)S(1)} collective-permute-done((bf16[4,128,128]{2,1,0:T(8,128)(2,1)S(1)}, bf16[4,128,128]{2,1,0:T(8,128)(2,1)S(1)}, u32[]{:S(2)}, u32[]{:S(2)}) %collective-permute-start.15) | collective-permute-done | bytes 131104 | tf_op jit(solution)/shard_map/ppermute | solution.py:59
  38.6 4.1 %collective-permute-done.17.refs_1_.refs_3_ = bf16[128,1536]{1,0:T(8,128)(2,1)S(1)} collective-permute-done((bf16[128,1536]{1,0:T(8,128)(2,1)S(1)}, bf16[128,1536]{1,0:T(8,128)(2,1)S(1)}, u32[]{:S(2)}, u32[]{:S(2)}) %collective-permute-start.17) | collective-permute-done | bytes 393248 | tf_op jit(solution)/shard_map/ppermute | solution.py:452
  44.1 6.2 %collective-permute-done.20.refs_5_ = bf16[128,1536]{1,0:T(8,128)(2,1)S(1)} collective-permute-done((bf16[128,1536]{1,0:T(8,128)(2,1)S(1)}, bf16[128,1536]{1,0:T(8,128)(2,1)S(1)}, u32[]{:S(2)}, u32[]{:S(2)}) %collective-permute-start.20) | collective-permute-done | bytes 393248 | tf_op jit(solution)/shard_map/ppermute | solution.py:452
  50.3 1.3 %collective-permute-start.5 = (bf16[128,2560]{1,0:T(8,128)(2,1)S(1)}, bf16[128,2560]{1,0:T(8,128)(2,1)S(1)}, u32[]{:S(2)}, u32[]{:S(2)}) collective-permute-start(bf16[128,2560]{1,0:T(8,128)(2,1)S(1)} %tie.4.refs_2_), channel_id=1, source_target_pairs={{2,0},{4,6},{3,1},{5,7},{10,8},{12,14},{11,9},{13,15},{18,16},{20,... | collective-permute-start | bytes 1966088 | tf_op jit(solution)/shard_map/ppermute | solution.py:452
  51.6 1.1 fold.4
  54.8 1.3 %collective-permute-start.19 = (bf16[128,1024]{1,0:T(8,128)(2,1)S(1)}, bf16[128,1024]{1,0:T(8,128)(2,1)S(1)}, u32[]{:S(2)}, u32[]{:S(2)}) collective-permute-start(bf16[128,1024]{1,0:T(8,128)(2,1)S(1)} %collective-permute-done.18.refs_4_), channel_id=1, source_target_pairs={{2,0},{4,6},{3,1},{5,7},{10,8},{12,14},{11,9},{13,15},{18,16},{20,... | collective-permute-start | bytes 786440 | tf_op jit(solution)/shard_map/ppermute | solution.py:452
  56.2 1.3 %collective-permute-start.16 = (bf16[128,1024]{1,0:T(8,128)(2,1)S(1)}, bf16[128,1024]{1,0:T(8,128)(2,1)S(1)}, u32[]{:S(2)}, u32[]{:S(2)}) collective-permute-start(bf16[128,1024]{1,0:T(8,128)(2,1)S(1)} %tie.5.refs_4_), channel_id=1, source_target_pairs={{2,0},{4,6},{3,1},{5,7},{10,8},{12,14},{11,9},{13,15},{18,16},{20,... | collective-permute-start | bytes 786440 | tf_op jit(solution)/shard_map/ppermute | solution.py:452
  57.7 1.6 %collective-permute-start.25 = (bf16[192,512]{1,0:T(8,128)(2,1)S(1)}, bf16[192,512]{1,0:T(8,128)(2,1)S(1)}, u32[]{:S(2)}, u32[]{:S(2)}) collective-permute-start(bf16[192,512]{1,0:T(8,128)(2,1)S(1)} %get-tuple-element.96), channel_id=1, source_target_pairs={{0,16},{8,24},{16,0},{24,8},{1,17},{9,25},{17,1},{25,9},{2,18},{10... | collective-permute-start | bytes 589832 | tf_op jit(solution)/shard_map/ppermute | solution.py:59
  59.8 17.0 %collective-permute-done.19.refs_5_ = bf16[128,1024]{1,0:T(8,128)(2,1)S(1)} collective-permute-done((bf16[128,1024]{1,0:T(8,128)(2,1)S(1)}, bf16[128,1024]{1,0:T(8,128)(2,1)S(1)}, u32[]{:S(2)}, u32[]{:S(2)}) %collective-permute-start.19) | collective-permute-done | bytes 262176 | tf_op jit(solution)/shard_map/ppermute | solution.py:452
  76.8 1.3 %collective-permute-start.7 = (bf16[128,512]{1,0:T(8,128)(2,1)S(1)}, bf16[128,512]{1,0:T(8,128)(2,1)S(1)}, u32[]{:S(2)}, u32[]{:S(2)}) collective-permute-start(bf16[128,512]{1,0:T(8,128)(2,1)S(1)} %collective-permute-done.6.refs_4_), channel_id=1, source_target_pairs={{2,0},{4,6},{3,1},{5,7},{10,8},{12,14},{11,9},{13,15},{18,16},{20,... | collective-permute-start | bytes 393224 | tf_op jit(solution)/shard_map/ppermute | solution.py:452
  78.1 2.2 %fold.5 = (f32[512,512]{1,0:T(8,128)S(1)}, bf16[128,512]{1,0:T(8,128)(2,1)S(1)}, bf16[128,512]{1,0:T(8,128)(2,1)S(1)}, bf16[128,512]{1,0:T(8,128)(2,1)S(1)}, bf1...) custom-call(bf16[128,1024]{1,0:T(8,128)(2,1)S(1)} %get-tuple-element.83.refs_0_, bf16[128,1024]{1,0:T(8,128)(2,1)S(1)} %tie.6.refs_1_, ...), custom_call_target="tpu_custom_call" | custom-call | tf_op jit(solution)/shard_map/fold/pallas_call | solution.py:376
  80.4 1.6 %collective-permute-start.27 = (bf16[384,512]{1,0:T(8,128)(2,1)S(1)}, bf16[384,512]{1,0:T(8,128)(2,1)S(1)}, u32[]{:S(2)}, u32[]{:S(2)}) collective-permute-start(bf16[384,512]{1,0:T(8,128)(2,1)S(1)} %mine.4.refs_0_), channel_id=1, source_target_pairs={{0,1},{1,0},{2,3},{3,2},{4,5},{5,4},{6,7},{7,6},{8,9},{9,8},{10,11... | collective-permute-start | bytes 1179656 | tf_op jit(solution)/shard_map/ppermute | solution.py:455
  82.2 1.4 %collective-permute-done.7.refs_16_.refs_5_ = bf16[128,512]{1,0:T(8,128)(2,1)S(1)} collective-permute-done((bf16[128,512]{1,0:T(8,128)(2,1)S(1)}, bf16[128,512]{1,0:T(8,128)(2,1)S(1)}, u32[]{:S(2)}, u32[]{:S(2)}) %collective-permute-start.7) | collective-permute-done | bytes 131104 | tf_op jit(solution)/shard_map/ppermute | solution.py:452
  84.2 1.4 %fold.6 = (f32[512,512]{1,0:T(8,128)S(1)}, bf16[128,512]{1,0:T(8,128)(2,1)S(1)}, bf16[128,512]{1,0:T(8,128)(2,1)S(1)}, bf16[128,512]{1,0:T(8,128)(2,1)S(1)}, bf1...) custom-call(bf16[128,1024]{1,0:T(8,128)(2,1)S(1)} %get-tuple-element.80.refs_0_, ...), custom_call_target="tpu_custom_call" | custom-call | tf_op jit(solution)/shard_map/fold/pallas_call | solution.py:376
  87.0 1.1 collective-permute-start.36
  89.2 2.8 %collective-permute-done.27.refs_17_.refs_1_ = bf16[384,512]{1,0:T(8,128)(2,1)S(1)} collective-permute-done((bf16[384,512]{1,0:T(8,128)(2,1)S(1)}, bf16[384,512]{1,0:T(8,128)(2,1)S(1)}, u32[]{:S(2)}, u32[]{:S(2)}) %collective-permute-start.27) | collective-permute-done | bytes 393248 | tf_op jit(solution)/shard_map/ppermute | solution.py:455
  92.0 1.3 %fold.7 = (f32[256,512]{1,0:T(8,128)S(1)}, bf16[128,512]{1,0:T(8,128)(2,1)S(1)}, bf16[128,512]{1,0:T(8,128)(2,1)S(1)}, bf16[512,512]{1,0:T(8,128)(2,1)S(1)}, bf16[4,128,128]{2,1,0:T(8,128)(2,1)S(1)}) custom-call(bf16[128,512]{1,0:T(8,128)(2,1)S(1)} %get-tuple-element.68.refs_0_, bf16[128,512]{1,0:T(8,128)(2,1)S(1)} %get-tuple-element.71.refs_1_, ...), custom_call_target="tpu_custom_call" | custom-call | tf_op jit(solution)/shard_map/fold/pallas_call | solution.py:376
  93.9 2.2 %collective-permute-done.36.refs_1_ = bf16[256,512]{1,0:T(8,128)(2,1)S(1)} collective-permute-done((bf16[256,512]{1,0:T(8,128)(2,1)S(1)}, bf16[256,512]{1,0:T(8,128)(2,1)S(1)}, u32[]{:S(2)}, u32[]{:S(2)}) %collective-permute-start.36) | collective-permute-done | bytes 262176 | tf_op jit(solution)/shard_map/ppermute | solution.py:59
  96.2 1.6 %collective-permute-start.45 = (bf16[256,512]{1,0:T(8,128)(2,1)S(1)}, bf16[256,512]{1,0:T(8,128)(2,1)S(1)}, u32[]{:S(2)}, u32[]{:S(2)}) collective-permute-start(bf16[256,512]{1,0:T(8,128)(2,1)S(1)} %mine.5.refs_2_.refs_0_), channel_id=1, source_target_pairs={{0,1},{1,0},{2,3},{3,2},{4,5},{5,4},{6,7},{7,6},{8,9},{9,8},{10,11... | collective-permute-start | bytes 786440 | tf_op jit(solution)/shard_map/ppermute | solution.py:455
  97.8 1.2 %collective-permute-start.29 = (bf16[4,128,128]{2,1,0:T(8,128)(2,1)S(1)}, bf16[4,128,128]{2,1,0:T(8,128)(2,1)S(1)}, u32[]{:S(2)}, u32[]{:S(2)}) collective-permute-start(bf16[4,128,128]{2,1,0:T(8,128)(2,1)S(1)} %add.3.refs_0_.refs_3_), channel_id=1, source_target_pairs={{0,16},{8,24},{16,0},{24,8},{1,17},{9,25},{17,1},{25,9},{2,18},{10... | collective-permute-start | bytes 393224 | tf_op jit(solution)/shard_map/ppermute | solution.py:59
  100.0 1.7 %collective-permute-done.43.refs_1_ = bf16[256,512]{1,0:T(8,128)(2,1)S(1)} collective-permute-done((bf16[256,512]{1,0:T(8,128)(2,1)S(1)}, bf16[256,512]{1,0:T(8,128)(2,1)S(1)}, u32[]{:S(2)}, u32[]{:S(2)}) %collective-permute-start.43) | collective-permute-done | bytes 262176 | tf_op jit(solution)/shard_map/ppermute | solution.py:59
  101.8 1.6 %collective-permute-start.44 = (bf16[256,512]{1,0:T(8,128)(2,1)S(1)}, bf16[256,512]{1,0:T(8,128)(2,1)S(1)}, u32[]{:S(2)}, u32[]{:S(2)}) collective-permute-start(bf16[256,512]{1,0:T(8,128)(2,1)S(1)} %mine.7.refs_0_), channel_id=1, source_target_pairs={{0,1},{1,0},{2,3},{3,2},{4,5},{5,4},{6,7},{7,6},{8,9},{9,8},{10,11... | collective-permute-start | bytes 786440 | tf_op jit(solution)/shard_map/ppermute | solution.py:455
  103.4 2.6 %late.1 = (bf16[512,512]{1,0:T(8,128)(2,1)}, f32[512,512]{1,0:T(8,128)S(1)}, f32[512,512]{1,0:T(8,128)S(1)}) custom-call(bf16[512,512]{1,0:T(8,128)(2,1)S(1)} %get-tuple-element.65.refs_1_.refs_16_.q_ref, bf16[512,512]{1,0:T(8,128)(2,1)S(1)} %get-tuple-element.66.refs_2_.k_ref, bf16[512,512]{1,0:T(8,128)(2,1)S(1)} %get-tuple-element.67.refs_3_.v_ref, ...), custom_call_target="tpu_custom_call" | custom-call | tf_op jit(solution)/shard_map/late/pallas_call | solution.py:265
  107.6 1.6 %collective-permute-start.38 = (bf16[128,512]{1,0:T(8,128)(2,1)S(1)}, bf16[128,512]{1,0:T(8,128)(2,1)S(1)}, u32[]{:S(2)}, u32[]{:S(2)}) collective-permute-start(bf16[128,512]{1,0:T(8,128)(2,1)S(1)} %mine.6.refs_0_), channel_id=1, source_target_pairs={{0,1},{1,0},{2,3},{3,2},{4,5},{5,4},{6,7},{7,6},{8,9},{9,8},{10,11... | collective-permute-start | bytes 393224 | tf_op jit(solution)/shard_map/ppermute | solution.py:455
  112.0 1.3 %final.1 = (bf16[512,512]{1,0:T(8,128)(2,1)}, bf16[512,512]{1,0:T(8,128)(2,1)}) custom-call(bf16[512,512]{1,0:T(8,128)(2,1)S(1)} %get-tuple-element.66.refs_2_.k_ref, bf16[512,512]{1,0:T(8,128)(2,1)S(1)} %get-tuple-element.67.refs_3_.v_ref, bf16[4,128,128]{2,1,0:T(8,128)(2,1)S(1)} %states.3.later_ref.refs_2_, ...), custom_call_target="tpu_custom_call" | custom-call | tf_op jit(solution)/shard_map/final/pallas_call | solution.py:292
  (97 shorter events, 19.8 us)
Async XLA Ops:
  0.6 26.5 %collective-permute-start = (bf16[128,4096]{1,0:T(8,128)(2,1)}, bf16[128,4096]{1,0:T(8,128)(2,1)S(1)}, u32[]{:S(2)}, u32[]{:S(2)}) collective-permute-start(bf16[128,4096]{1,0:T(8,128)(2,1)} %bitcast.11), channel_id=1, source_target_pairs={{0,2},{2,0},{4,6},{6,4},{1,3},{3,1},{5,7},{7,5},{8,10},{10,8},{12,... | collective-permute-start | bytes 3145736 | tf_op jit(solution)/shard_map/ppermute | solution.py:446
  3.7 24.2 %collective-permute-start.3 = (bf16[128,4096]{1,0:T(8,128)(2,1)}, bf16[128,4096]{1,0:T(8,128)(2,1)S(1)}, u32[]{:S(2)}, u32[]{:S(2)}) collective-permute-start(bf16[128,4096]{1,0:T(8,128)(2,1)} %bitcast.12), channel_id=1, source_target_pairs={{2,4},{4,2},{3,5},{5,3},{10,12},{12,10},{11,13},{13,11},{18,20},{2... | collective-permute-start | bytes 3145736 | tf_op jit(solution)/shard_map/ppermute | solution.py:449
  7.6 26.1 %collective-permute-start.8 = (bf16[1024,512]{1,0:T(8,128)(2,1)S(1)}, bf16[1024,512]{1,0:T(8,128)(2,1)S(1)}, u32[]{:S(2)}, u32[]{:S(2)}) collective-permute-start(bf16[1024,512]{1,0:T(8,128)(2,1)S(1)} %copy-done.2), channel_id=1, source_target_pairs={{0,16},{8,24},{16,0},{24,8},{1,17},{9,25},{17,1},{25,9},{2,18},{10... | collective-permute-start | bytes 3145736 | tf_op jit(solution)/shard_map/ppermute | solution.py:59
  28.1 14.6 %collective-permute-start.17 = (bf16[128,1536]{1,0:T(8,128)(2,1)S(1)}, bf16[128,1536]{1,0:T(8,128)(2,1)S(1)}, u32[]{:S(2)}, u32[]{:S(2)}) collective-permute-start(bf16[128,1536]{1,0:T(8,128)(2,1)S(1)} %get-tuple-element.85.refs_2_), channel_id=1, source_target_pairs={{2,0},{4,6},{3,1},{5,7},{10,8},{12,14},{11,9},{13,15},{18,16},{20,... | collective-permute-start | bytes 1179656 | tf_op jit(solution)/shard_map/ppermute | solution.py:452
  30.6 19.7 %collective-permute-start.20 = (bf16[128,1536]{1,0:T(8,128)(2,1)S(1)}, bf16[128,1536]{1,0:T(8,128)(2,1)S(1)}, u32[]{:S(2)}, u32[]{:S(2)}) collective-permute-start(bf16[128,1536]{1,0:T(8,128)(2,1)S(1)} %collective-permute-done.4.refs_1_.refs_4_), channel_id=1, source_target_pairs={{2,0},{4,6},{3,1},{5,7},{10,8},{12,14},{11,9},{13,15},{18,16},{20,... | collective-permute-start | bytes 1179656 | tf_op jit(solution)/shard_map/ppermute | solution.py:452
  32.0 5.9 %collective-permute-start.15 = (bf16[4,128,128]{2,1,0:T(8,128)(2,1)S(1)}, bf16[4,128,128]{2,1,0:T(8,128)(2,1)S(1)}, u32[]{:S(2)}, u32[]{:S(2)}) collective-permute-start(bf16[4,128,128]{2,1,0:T(8,128)(2,1)S(1)} %add.2), channel_id=1, source_target_pairs={{0,16},{8,24},{16,0},{24,8},{1,17},{9,25},{17,1},{25,9},{2,18},{10... | collective-permute-start | bytes 393224 | tf_op jit(solution)/shard_map/ppermute | solution.py:59
  33.8 19.0 %collective-permute-start.9 = (bf16[256,512]{1,0:T(8,128)(2,1)S(1)}, bf16[256,512]{1,0:T(8,128)(2,1)S(1)}, u32[]{:S(2)}, u32[]{:S(2)}) collective-permute-start(bf16[256,512]{1,0:T(8,128)(2,1)S(1)} %get-tuple-element.76), channel_id=1, source_target_pairs={{0,8},{8,0},{16,24},{24,16},{1,9},{9,1},{17,25},{25,17},{2,10},{10... | collective-permute-start | bytes 786440 | tf_op jit(solution)/shard_map/ppermute | solution.py:59
  34.0 18.8 %collective-permute-start.10 = (bf16[256,512]{1,0:T(8,128)(2,1)S(1)}, bf16[256,512]{1,0:T(8,128)(2,1)S(1)}, u32[]{:S(2)}, u32[]{:S(2)}) collective-permute-start(bf16[256,512]{1,0:T(8,128)(2,1)S(1)} %get-tuple-element.77), channel_id=1, source_target_pairs={{0,8},{8,0},{16,24},{24,16},{1,9},{9,1},{17,25},{25,17},{2,10},{10... | collective-permute-start | bytes 786440 | tf_op jit(solution)/shard_map/ppermute | solution.py:59
  37.9 5.5 %collective-permute-start.6 = (bf16[128,512]{1,0:T(8,128)(2,1)S(1)}, bf16[128,512]{1,0:T(8,128)(2,1)S(1)}, u32[]{:S(2)}, u32[]{:S(2)}) collective-permute-start(bf16[128,512]{1,0:T(8,128)(2,1)S(1)} %get-tuple-element.71.refs_1_), channel_id=1, source_target_pairs={{2,4},{4,2},{3,5},{5,3},{10,12},{12,10},{11,13},{13,11},{18,20},{2... | collective-permute-start | bytes 393224 | tf_op jit(solution)/shard_map/ppermute | solution.py:449
  42.7 10.7 %collective-permute-start.13 = (bf16[128,1024]{1,0:T(8,128)(2,1)S(1)}, bf16[128,1024]{1,0:T(8,128)(2,1)S(1)}, u32[]{:S(2)}, u32[]{:S(2)}) collective-permute-start(bf16[128,1024]{1,0:T(8,128)(2,1)S(1)} %get-tuple-element.81.refs_1_), channel_id=1, source_target_pairs={{2,4},{4,2},{3,5},{5,3},{10,12},{12,10},{11,13},{13,11},{18,20},{2... | collective-permute-start | bytes 786440 | tf_op jit(solution)/shard_map/ppermute | solution.py:449
  43.4 10.0 %collective-permute-start.18 = (bf16[128,1024]{1,0:T(8,128)(2,1)S(1)}, bf16[128,1024]{1,0:T(8,128)(2,1)S(1)}, u32[]{:S(2)}, u32[]{:S(2)}) collective-permute-start(bf16[128,1024]{1,0:T(8,128)(2,1)S(1)} %tie.6.refs_1_), channel_id=1, source_target_pairs={{2,4},{4,2},{3,5},{5,3},{10,12},{12,10},{11,13},{13,11},{18,20},{2... | collective-permute-start | bytes 786440 | tf_op jit(solution)/shard_map/ppermute | solution.py:449
  50.3 27.7 %collective-permute-start.5 = (bf16[128,2560]{1,0:T(8,128)(2,1)S(1)}, bf16[128,2560]{1,0:T(8,128)(2,1)S(1)}, u32[]{:S(2)}, u32[]{:S(2)}) collective-permute-start(bf16[128,2560]{1,0:T(8,128)(2,1)S(1)} %tie.4.refs_2_), channel_id=1, source_target_pairs={{2,0},{4,6},{3,1},{5,7},{10,8},{12,14},{11,9},{13,15},{18,16},{20,... | collective-permute-start | bytes 1966088 | tf_op jit(solution)/shard_map/ppermute | solution.py:452
  53.4 4.2 %collective-permute-start.11 = (bf16[256,512]{1,0:T(8,128)(2,1)S(1)}, bf16[256,512]{1,0:T(8,128)(2,1)S(1)}, u32[]{:S(2)}, u32[]{:S(2)}) collective-permute-start(bf16[256,512]{1,0:T(8,128)(2,1)S(1)} %get-tuple-element.78), channel_id=1, source_target_pairs={{0,8},{8,0},{16,24},{24,16},{1,9},{9,1},{17,25},{25,17},{2,10},{10... | collective-permute-start | bytes 786440 | tf_op jit(solution)/shard_map/ppermute | solution.py:59
  54.3 5.0 %collective-permute-start.12 = (bf16[256,512]{1,0:T(8,128)(2,1)S(1)}, bf16[256,512]{1,0:T(8,128)(2,1)S(1)}, u32[]{:S(2)}, u32[]{:S(2)}) collective-permute-start(bf16[256,512]{1,0:T(8,128)(2,1)S(1)} %get-tuple-element.79), channel_id=1, source_target_pairs={{0,8},{8,0},{16,24},{24,16},{1,9},{9,1},{17,25},{25,17},{2,10},{10... | collective-permute-start | bytes 786440 | tf_op jit(solution)/shard_map/ppermute | solution.py:59
  54.8 21.9 %collective-permute-start.19 = (bf16[128,1024]{1,0:T(8,128)(2,1)S(1)}, bf16[128,1024]{1,0:T(8,128)(2,1)S(1)}, u32[]{:S(2)}, u32[]{:S(2)}) collective-permute-start(bf16[128,1024]{1,0:T(8,128)(2,1)S(1)} %collective-permute-done.18.refs_4_), channel_id=1, source_target_pairs={{2,0},{4,6},{3,1},{5,7},{10,8},{12,14},{11,9},{13,15},{18,16},{20,... | collective-permute-start | bytes 786440 | tf_op jit(solution)/shard_map/ppermute | solution.py:452
  56.2 27.4 %collective-permute-start.16 = (bf16[128,1024]{1,0:T(8,128)(2,1)S(1)}, bf16[128,1024]{1,0:T(8,128)(2,1)S(1)}, u32[]{:S(2)}, u32[]{:S(2)}) collective-permute-start(bf16[128,1024]{1,0:T(8,128)(2,1)S(1)} %tie.5.refs_4_), channel_id=1, source_target_pairs={{2,0},{4,6},{3,1},{5,7},{10,8},{12,14},{11,9},{13,15},{18,16},{20,... | collective-permute-start | bytes 786440 | tf_op jit(solution)/shard_map/ppermute | solution.py:452
  57.7 22.7 %collective-permute-start.25 = (bf16[192,512]{1,0:T(8,128)(2,1)S(1)}, bf16[192,512]{1,0:T(8,128)(2,1)S(1)}, u32[]{:S(2)}, u32[]{:S(2)}) collective-permute-start(bf16[192,512]{1,0:T(8,128)(2,1)S(1)} %get-tuple-element.96), channel_id=1, source_target_pairs={{0,16},{8,24},{16,0},{24,8},{1,17},{9,25},{17,1},{25,9},{2,18},{10... | collective-permute-start | bytes 589832 | tf_op jit(solution)/shard_map/ppermute | solution.py:59
  59.2 21.1 %collective-permute-start.26 = (bf16[192,512]{1,0:T(8,128)(2,1)S(1)}, bf16[192,512]{1,0:T(8,128)(2,1)S(1)}, u32[]{:S(2)}, u32[]{:S(2)}) collective-permute-start(bf16[192,512]{1,0:T(8,128)(2,1)S(1)} %get-tuple-element.97), channel_id=1, source_target_pairs={{0,16},{8,24},{16,0},{24,8},{1,17},{9,25},{17,1},{25,9},{2,18},{10... | collective-permute-start | bytes 589832 | tf_op jit(solution)/shard_map/ppermute | solution.py:59
  76.8 6.9 %collective-permute-start.7 = (bf16[128,512]{1,0:T(8,128)(2,1)S(1)}, bf16[128,512]{1,0:T(8,128)(2,1)S(1)}, u32[]{:S(2)}, u32[]{:S(2)}) collective-permute-start(bf16[128,512]{1,0:T(8,128)(2,1)S(1)} %collective-permute-done.6.refs_4_), channel_id=1, source_target_pairs={{2,0},{4,6},{3,1},{5,7},{10,8},{12,14},{11,9},{13,15},{18,16},{20,... | collective-permute-start | bytes 393224 | tf_op jit(solution)/shard_map/ppermute | solution.py:452
  80.3 5.3 %collective-permute-start.32 = (bf16[128,512]{1,0:T(8,128)(2,1)S(1)}, bf16[128,512]{1,0:T(8,128)(2,1)S(1)}, u32[]{:S(2)}, u32[]{:S(2)}) collective-permute-start(bf16[128,512]{1,0:T(8,128)(2,1)S(1)} %get-tuple-element.113), channel_id=1, source_target_pairs={{0,8},{8,0},{16,24},{24,16},{1,9},{9,1},{17,25},{25,17},{2,10},{10... | collective-permute-start | bytes 393224 | tf_op jit(solution)/shard_map/ppermute | solution.py:59
  80.4 11.6 %collective-permute-start.27 = (bf16[384,512]{1,0:T(8,128)(2,1)S(1)}, bf16[384,512]{1,0:T(8,128)(2,1)S(1)}, u32[]{:S(2)}, u32[]{:S(2)}) collective-permute-start(bf16[384,512]{1,0:T(8,128)(2,1)S(1)} %mine.4.refs_0_), channel_id=1, source_target_pairs={{0,1},{1,0},{2,3},{3,2},{4,5},{5,4},{6,7},{7,6},{8,9},{9,8},{10,11... | collective-permute-start | bytes 1179656 | tf_op jit(solution)/shard_map/ppermute | solution.py:455
  82.0 3.6 %collective-permute-start.33 = (bf16[128,512]{1,0:T(8,128)(2,1)S(1)}, bf16[128,512]{1,0:T(8,128)(2,1)S(1)}, u32[]{:S(2)}, u32[]{:S(2)}) collective-permute-start(bf16[128,512]{1,0:T(8,128)(2,1)S(1)} %get-tuple-element.114), channel_id=1, source_target_pairs={{0,8},{8,0},{16,24},{24,16},{1,9},{9,1},{17,25},{25,17},{2,10},{10... | collective-permute-start | bytes 393224 | tf_op jit(solution)/shard_map/ppermute | solution.py:59
  87.0 9.1 %collective-permute-start.36 = (bf16[256,512]{1,0:T(8,128)(2,1)S(1)}, bf16[256,512]{1,0:T(8,128)(2,1)S(1)}, u32[]{:S(2)}, u32[]{:S(2)}) collective-permute-start(bf16[256,512]{1,0:T(8,128)(2,1)S(1)} %get-tuple-element.118), channel_id=1, source_target_pairs={{0,16},{8,24},{16,0},{24,8},{1,17},{9,25},{17,1},{25,9},{2,18},{10... | collective-permute-start | bytes 786440 | tf_op jit(solution)/shard_map/ppermute | solution.py:59
  88.2 13.5 %collective-permute-start.43 = (bf16[256,512]{1,0:T(8,128)(2,1)S(1)}, bf16[256,512]{1,0:T(8,128)(2,1)S(1)}, u32[]{:S(2)}, u32[]{:S(2)}) collective-permute-start(bf16[256,512]{1,0:T(8,128)(2,1)S(1)} %get-tuple-element.125), channel_id=1, source_target_pairs={{0,16},{8,24},{16,0},{24,8},{1,17},{9,25},{17,1},{25,9},{2,18},{10... | collective-permute-start | bytes 786440 | tf_op jit(solution)/shard_map/ppermute | solution.py:59
  93.3 4.5 %collective-permute-start.28 = (bf16[4,128,128]{2,1,0:T(8,128)(2,1)S(1)}, bf16[4,128,128]{2,1,0:T(8,128)(2,1)S(1)}, u32[]{:S(2)}, u32[]{:S(2)}) collective-permute-start(bf16[4,128,128]{2,1,0:T(8,128)(2,1)S(1)} %get-tuple-element.101.refs_0_), channel_id=1, source_target_pairs={{0,8},{8,0},{16,24},{24,16},{1,9},{9,1},{17,25},{25,17},{2,10},{10... | collective-permute-start | bytes 393224 | tf_op jit(solution)/shard_map/ppermute | solution.py:59
  93.3 5.6 %collective-permute-start.30 = (bf16[128,512]{1,0:T(8,128)(2,1)S(1)}, bf16[128,512]{1,0:T(8,128)(2,1)S(1)}, u32[]{:S(2)}, u32[]{:S(2)}) collective-permute-start(bf16[128,512]{1,0:T(8,128)(2,1)S(1)} %get-tuple-element.108), channel_id=1, source_target_pairs={{0,8},{8,0},{16,24},{24,16},{1,9},{9,1},{17,25},{25,17},{2,10},{10... | collective-permute-start | bytes 393224 | tf_op jit(solution)/shard_map/ppermute | solution.py:59
  93.8 5.2 %collective-permute-start.31 = (bf16[128,512]{1,0:T(8,128)(2,1)S(1)}, bf16[128,512]{1,0:T(8,128)(2,1)S(1)}, u32[]{:S(2)}, u32[]{:S(2)}) collective-permute-start(bf16[128,512]{1,0:T(8,128)(2,1)S(1)} %get-tuple-element.109), channel_id=1, source_target_pairs={{0,8},{8,0},{16,24},{24,16},{1,9},{9,1},{17,25},{25,17},{2,10},{10... | collective-permute-start | bytes 393224 | tf_op jit(solution)/shard_map/ppermute | solution.py:59
  96.2 14.0 %collective-permute-start.45 = (bf16[256,512]{1,0:T(8,128)(2,1)S(1)}, bf16[256,512]{1,0:T(8,128)(2,1)S(1)}, u32[]{:S(2)}, u32[]{:S(2)}) collective-permute-start(bf16[256,512]{1,0:T(8,128)(2,1)S(1)} %mine.5.refs_2_.refs_0_), channel_id=1, source_target_pairs={{0,1},{1,0},{2,3},{3,2},{4,5},{5,4},{6,7},{7,6},{8,9},{9,8},{10,11... | collective-permute-start | bytes 786440 | tf_op jit(solution)/shard_map/ppermute | solution.py:455
  97.8 8.2 %collective-permute-start.29 = (bf16[4,128,128]{2,1,0:T(8,128)(2,1)S(1)}, bf16[4,128,128]{2,1,0:T(8,128)(2,1)S(1)}, u32[]{:S(2)}, u32[]{:S(2)}) collective-permute-start(bf16[4,128,128]{2,1,0:T(8,128)(2,1)S(1)} %add.3.refs_0_.refs_3_), channel_id=1, source_target_pairs={{0,16},{8,24},{16,0},{24,8},{1,17},{9,25},{17,1},{25,9},{2,18},{10... | collective-permute-start | bytes 393224 | tf_op jit(solution)/shard_map/ppermute | solution.py:59
  99.1 7.5 %collective-permute-start.37 = (bf16[128,512]{1,0:T(8,128)(2,1)S(1)}, bf16[128,512]{1,0:T(8,128)(2,1)S(1)}, u32[]{:S(2)}, u32[]{:S(2)}) collective-permute-start(bf16[128,512]{1,0:T(8,128)(2,1)S(1)} %tie.7), channel_id=1, source_target_pairs={{0,16},{8,24},{16,0},{24,8},{1,17},{9,25},{17,1},{25,9},{2,18},{10... | collective-permute-start | bytes 393224 | tf_op jit(solution)/shard_map/ppermute | solution.py:59
  101.8 9.3 %collective-permute-start.44 = (bf16[256,512]{1,0:T(8,128)(2,1)S(1)}, bf16[256,512]{1,0:T(8,128)(2,1)S(1)}, u32[]{:S(2)}, u32[]{:S(2)}) collective-permute-start(bf16[256,512]{1,0:T(8,128)(2,1)S(1)} %mine.7.refs_0_), channel_id=1, source_target_pairs={{0,1},{1,0},{2,3},{3,2},{4,5},{5,4},{6,7},{7,6},{8,9},{9,8},{10,11... | collective-permute-start | bytes 786440 | tf_op jit(solution)/shard_map/ppermute | solution.py:455
  107.6 5.6 %collective-permute-start.38 = (bf16[128,512]{1,0:T(8,128)(2,1)S(1)}, bf16[128,512]{1,0:T(8,128)(2,1)S(1)}, u32[]{:S(2)}, u32[]{:S(2)}) collective-permute-start(bf16[128,512]{1,0:T(8,128)(2,1)S(1)} %mine.6.refs_0_), channel_id=1, source_target_pairs={{0,1},{1,0},{2,3},{3,2},{4,5},{5,4},{6,7},{7,6},{8,9},{9,8},{10,11... | collective-permute-start | bytes 393224 | tf_op jit(solution)/shard_map/ppermute | solution.py:455
  (17 other events, 55.1 us)

commit v4 on v3

--- a/solution.py
+++ b/solution.py
@@ -12,19 +12,17 @@
 BLK = 64
 EIGHTHS = (3, 2, 2, 1)
 GROUPS = ((0,), (1, 2, 3))
-CORE_SENDS = (4, 4, 4, 2)
 TOP_SENDS = (2, 1, 1, 1)
 LAST_SENDS = (1, 1, 1, 1)
+OG_SENDS = 4
 AFTER = {
-    'cut': ('wcore',),
-    'b2_1': ('c1_0',),
-    'c1_1': ('b2_0',),
-    'c2_2': ('prev',),
-    'send_3': ('last_0', 'mine_1'),
-    'late': ('qg',),
-    'mine_3': ('later', 'late'),
-    'fold_2': ('c2_3',),
-    'fold_3': ('last_0',),
+    "cut": ("opened",),
+    "c1_1": ("b2_1", "c1_0"),
+    "late": ("qg",),
+    "mine_2": ("late", "last_1"),
+    "fold_1": ("prev",),
+    "fold_2": ("c2_3",),
+    "fold_3": ("last_0", "mine_1"),
 }
 F32 = jnp.float32
 BF16 = jnp.bfloat16
@@ -96,14 +94,14 @@
     )(*in_vmem(*arrays), *after)
 
 
-def load(pieces, cuts=()):
+def load(pieces, cuts=(), after=()):
     sources = [x for x, _, _ in pieces] + [x for x, _ in cuts]
     shapes = [(rows, x.shape[1]) for x, _, rows in pieces]
     shapes += [(x.shape[0], sum(width for _, width in columns(0))) for x, columns in cuts]
     count = len(sources)
 
     def kernel(*refs):
-        refs, targets, sems = refs[:count], refs[count:-1], refs[-1]
+        refs, targets, sems = refs[:count], refs[count + len(after):-1], refs[-1]
         for i, (_, first, rows) in enumerate(pieces):
             pltpu.make_async_copy(refs[i].at[pl.ds(first, rows)], targets[i], sems.at[i]).start()
         here = lax.axis_index("ctx")
@@ -120,23 +118,13 @@
 
     return pl.pallas_call(
         kernel,
-        in_specs=[HBM] * count,
+        in_specs=[HBM] * count + [ANY] * len(after),
         out_specs=[VMEM] * count,
         out_shape=[pltpu.VMEM(shape, x.dtype) for shape, x in zip(shapes, sources)],
         scratch_shapes=[pltpu.SemaphoreType.DMA((count,))],
         compiler_params=params(1),
         name="load",
-    )(*in_hbm(*sources))
-
-
-def in_rows(array, count):
-    rows = array.shape[0] // count
-
-    def body(*refs):
-        for i in range(count):
-            refs[1 + i][...] = refs[0][i * rows:(i + 1) * rows, :]
-
-    return on_vmem(body, [((rows, array.shape[1]), array.dtype)] * count, [array], name="in_rows")
+    )(*in_hbm(*sources), *after)
 
 
 def rows_of(refs, start, size):
@@ -149,32 +137,37 @@
     return found[0] if len(found) == 1 else jnp.concatenate(found, axis=0)
 
 
-def columns_of(group, order, block):
-    return lambda here: [((here ^ j) * block + offset, piece) for offset, piece in group for j in order]
-
-
-def cut(whole, order, groups, after=()):
+def halves(whole, order, parts):
     rows, model = whole.shape
-    block = model // len(order)
-    widths = [sum(piece for _, piece in group) * len(order) for group in groups]
-    if any(piece % 128 for group in groups for _, piece in group):
-        here = lax.axis_index("ctx")
-        return [
-            jnp.concatenate([
-                lax.dynamic_slice(whole, (0, at), (rows, piece)) for at, piece in columns_of(group, order, block)(here)
-            ], axis=1)
-            for group in groups
-        ]
-
-    def body(source, *targets):
-        here = lax.axis_index("ctx")
-        for target, group in zip(targets, groups):
-            column = 0
-            for at, piece in columns_of(group, order, block)(here):
-                target[:, column:column + piece] = source[:, pl.ds(pl.multiple_of(at, 128), piece)]
-                column += piece
-
-    return on_vmem(body, [((rows, width), whole.dtype) for width in widths], [whole], after=after, name="cut")
+    block = model // (2 * len(order))
+
+    def columns(flip):
+        return lambda here: [((here ^ flip ^ j) * block + offset, piece) for offset, piece in parts for j in order]
+
+    if all(piece % 128 == 0 for _, piece in parts):
+        return load([], [(whole, columns(0)), (whole, columns(1))])
+    here = lax.axis_index("ctx")
+    return [
+        jnp.concatenate([lax.dynamic_slice(whole, (0, at), (rows, piece)) for at, piece in columns(flip)(here)], axis=1)
+        for flip in (0, 1)
+    ]
+
+
+def stack(pairs, widths, after=()):
+    outs = [((2 * x.shape[0], width), x.dtype) for (x, _), cuts in zip(pairs, widths) for width in cuts]
+
+    def body(*refs):
+        targets = list(refs[2 * len(pairs):])
+        for i, cuts in enumerate(widths):
+            rows, column = refs[2 * i].shape[0], 0
+            for width in cuts:
+                target = targets.pop(0)
+                target[:rows, :] = refs[2 * i][:, column:column + width]
+                target[rows:, :] = refs[2 * i + 1][:, column:column + width]
+                column += width
+
+    got = list(on_vmem(body, outs, [x for pair in pairs for x in pair], after=after, name="stack"))
+    return [[got.pop(0) for _ in cuts] for cuts in widths]
 
 
 def scan_states(state, sc, later):
@@ -300,44 +293,34 @@
     )(*in_vmem(k, v, later, dkp, dvp), *after)
 
 
-def fold(blocks, opened, norm, ws, products, acc, q, sends, after=()):
+def fold(blocks, opened, norm, ws, start, acc, sends, og_sends, after=()):
     own, a, (b1, b1_at), (c1, c1_at), b2, c2 = blocks
-    rows, wide = own.shape
+    rows, wide = own.shape[0] // 2, own.shape[1]
     length, width = opened.shape
-    half = wide // 2
-    last, whole = q is not None, not products
-    kept = [g for g, _ in products if g is not None]
-    flat_ws = [x for w in ws for x in w] if products else []
-    arrays = [own, a, b1, c1, b2, *c2, opened, *kept, *flat_ws]
-    arrays += ([] if acc is None else [acc]) + ([q] if last else [])
+    half, group = wide // 2, length // 2
+    last = og_sends > 0
+    arrays = [own, a, b1, c1, b2, c2, opened, *ws] + ([] if acc is None else [acc])
     outs = [((half, width), F32)] + [((half // sends, width), BF16)] * sends
-    if whole:
-        outs.append(((length, wide), BF16))
+    if last:
+        outs += [((group, width), F32)] + [((group // og_sends, width), BF16)] * og_sends
     else:
-        outs.append(((length, width), BF16 if last else F32))
-    if last:
-        outs.append(((width // HEAD, HEAD, HEAD), BF16))
+        outs.append(((length, width), F32))
 
     def kernel(*refs):
         refs = list(refs)
-        own_ref, a_ref, b1_ref, c1_ref, b2_ref = [refs.pop(0) for _ in range(5)]
-        c2_refs = [refs.pop(0) for _ in c2]
-        opened_ref = refs.pop(0)
-        kept_refs = [refs.pop(0) for _ in kept]
-        w_refs = [[refs.pop(0) for _ in w] for w in ws] if products else []
+        own_ref, a_ref, b1_ref, c1_ref, b2_ref, c2_ref, opened_ref = [refs.pop(0) for _ in range(7)]
+        w_refs = [refs.pop(0) for _ in ws]
         acc_ref = None if acc is None else refs.pop(0)
-        q_ref = refs.pop(0) if last else None
         del refs[:len(after)]
         keep_ref = refs.pop(0)
         send_refs = [refs.pop(0) for _ in range(sends)]
-        third_ref = refs.pop(0)
-        qg_ref = refs.pop(0) if last else None
-        grad = third_ref if whole else refs.pop(0)
+        og_ref, *og_refs, grad = refs
         here = lax.axis_index("tsp")
 
-        def place(ref, at, under=0, column=0):
-            count = ref.shape[0]
-            grad[pl.ds(pl.multiple_of(at * rows + under, count), count), :] = ref[:, column:column + wide]
+        def place(ref, at, column=0):
+            for core in range(2):
+                to = pl.ds(pl.multiple_of(core * group + at * rows, rows), rows)
+                grad[to, :] = ref[core * rows:(core + 1) * rows, column:column + wide]
 
         at_end = (here == 0) | (here == 3)
         near, far = jnp.where(here < 2, 2, 1), jnp.where(here < 2, 3, 0)
@@ -346,42 +329,53 @@
 
         @pl.when(at_end)
         def _():
-            place(c1_ref, near, 0, c1_at)
-            for i, ref in enumerate(c2_refs):
-                place(ref, far, i * ref.shape[0])
+            place(c1_ref, near, c1_at)
+            place(c2_ref, far)
 
         @pl.when(jnp.logical_not(at_end))
         def _():
-            place(b1_ref, near, 0, b1_at)
+            place(b1_ref, near, b1_at)
             place(b2_ref, far)
 
         sent = (mm(grad[:, half:], opened_ref[...], TN) * norm).astype(BF16)
         for i, ref in enumerate(send_refs):
             ref[...] = sent[i * ref.shape[0]:(i + 1) * ref.shape[0], :]
         keep_ref[...] = mm(grad[:, :half], opened_ref[...], TN) * norm
-        if whole:
-            return
-        total = None if acc is None else acc_ref[...]
-        for g, start in products:
-            source = grad if g is None else kept_refs.pop(0)
-            piece = source.shape[1] // len(ws)
-            rows_of_w = jnp.concatenate([rows_of(refs_here, start, piece) for refs_here in w_refs], axis=0)
-            term = mm(source[...], rows_of_w, NN)
-            total = term if total is None else total + term
-        third_ref[...] = total.astype(third_ref.dtype)
+        piece = wide // len(ws)
+        rows_of_w = jnp.concatenate([ref[start:start + piece, :] for ref in w_refs], axis=0)
+        total = mm(grad[...], rows_of_w, NN)
+        if acc is not None:
+            total = total + acc_ref[...]
         if last:
-            for h, at in enumerate(heads_of(third_ref)):
-                qg_ref[h] = mm(q_ref[:, at], third_ref[:, at], TN).astype(BF16)
+            og_ref[...] = total[:group]
+            for i, ref in enumerate(og_refs):
+                at = group + i * ref.shape[0]
+                ref[...] = total[at:at + ref.shape[0]].astype(BF16)
+        else:
+            og_ref[...] = total
 
     return pl.pallas_call(
         kernel,
         in_specs=[VMEM] * len(arrays) + [ANY] * len(after),
         out_specs=[VMEM] * len(outs),
         out_shape=[pltpu.VMEM(shape, kind) for shape, kind in outs],
-        scratch_shapes=[] if whole else [pltpu.VMEM((length, wide), BF16)],
+        scratch_shapes=[pltpu.VMEM((length, wide), BF16)],
         compiler_params=params(),
         name="fold",
     )(*in_vmem(*arrays), *after)
+
+
+def join(kept, came, q, after):
+    length, width = kept.shape
+
+    def body(kept_ref, *refs):
+        came_refs, q_ref, og_ref, qg_ref = refs[:len(came)], refs[-3], refs[-2], refs[-1]
+        og_ref[...] = (kept_ref[...] + rows_of(came_refs, 0, length).astype(F32)).astype(BF16)
+        for h, at in enumerate(heads_of(og_ref)):
+            qg_ref[h] = mm(q_ref[:, at], og_ref[:, at], TN).astype(BF16)
+
+    return on_vmem(
+        body, [((length, width), BF16), ((width // HEAD, HEAD, HEAD), BF16)], [kept, *came, q], after=after, name="join")
 
 
 def scatter_step(keep, sends, bit, parts=1):
@@ -434,47 +428,48 @@
     sc = 1.0 / math.sqrt(HEAD * seq_len)
     norm = 1.0 / math.sqrt(seq_len * lax.axis_size("dp"))
     grad = out_grad[0]
-    order = reversed_order(ctx)
+    order = [2 * r for r in reversed_order(ctx // 2)]
     block = grad.shape[1] // ctx
     count = len(EIGHTHS)
     pieces = [block * e // 8 for e in EIGHTHS]
     offsets = [sum(pieces[:i]) for i in range(count)]
+    wides = [piece * len(order) for piece in pieces]
     bits = bits_of(ctx)
-    top = bits[-1]
+    core, top = bits[0], bits[-1]
+
+    OUTER, INNER = ((0, 1), (1, 0), (2, 3), (3, 2)), ((1, 2), (2, 1))
 
     def outer(x):
-        return lax.ppermute(x, "tsp", [(0, 1), (1, 0), (2, 3), (3, 2)])
+        return lax.ppermute(x, "tsp", OUTER)
 
     def inner(x):
-        return lax.ppermute(x, "tsp", [(1, 2), (2, 1)])
+        return lax.ppermute(x, "tsp", INNER)
 
     def to_ends(x):
         return lax.ppermute(x, "tsp", [(1, 0), (2, 3)])
 
+    def to_other_core(x, pairs):
+        return lax.ppermute(
+            x, ("ctx", "tsp"), [(t * 4 + i, (t ^ core) * 4 + j) for t in range(ctx) for i, j in pairs])
+
     def other(x):
         return lax.ppermute(x, "dp", [(0, 1), (1, 0)])
 
-    a_all, b_all = outer(grad), inner(grad)
-    parts = list(zip(offsets, pieces))
-    single = [[part] for part in parts]
-    aligned = all(piece % 128 == 0 for piece in pieces)
-    q, k, v, opened, w_here, w_low, w_high, *own = load(
-        [(x[0], 0, group_len) for x in (queries, keys, values, attn_out)]
-        + [(out_weight, 0, block), (out_weight, 0, block // 2), (out_weight, block // 2, block // 2)],
-        [(grad, columns_of(group, order, block)) for group in single] if aligned else [])
-    if not aligned:
-        own = cut(grad, order, single)
-
-    held = {0: [w_here]}
+    same, cross = halves(grad, order, list(zip(offsets, pieces)))
+    a_pair = outer(same), to_other_core(cross, OUTER)
+    b_pair = inner(same), to_other_core(cross, INNER)
+    own_pair = same, swap(cross, "ctx", core)
+    q, k, v, opened_here, w_here = load(
+        [(x[0], 0, group_len) for x in (queries, keys, values, attn_out)] + [(out_weight, 0, block)], after=own_pair[1:])
+    opened_there = swap(opened_here, "ctx", core)
+
+    held = {0: w_here}
     for bit in reversed(bits[1:]):
         for j in list(held):
-            held[j | bit] = [swap(held[j][0] if j else out_weight, "ctx", bit)]
-    for j in list(held):
-        rows_here = in_rows(held[j][0], 4) if j else (w_low, w_high)
-        held[j | bits[0]] = [swap(x, "ctx", bits[0]) for x in rows_here]
+            held[j | bit] = swap(held[j] if j else out_weight, "ctx", bit)
     ws = [held[j] for j in order]
 
-    made, final_form = {"wcore": held[bits[0]]}, {}
+    made, final_form = {"opened": opened_there}, {}
 
     def get(name):
         if name not in made:
@@ -496,8 +491,10 @@
 
     def build_cut():
         waits = after("cut")
-        return cut(b_all, order, [[parts[i] for i in group] for group in GROUPS], waits), cut(
-            a_all, order, single, waits)
+        (opened,), own = stack([(opened_here, opened_there), own_pair], [[width], wides], waits)
+        b1, = stack([b_pair], [[sum(wides[i] for i in group) for group in GROUPS]], waits)
+        a, = stack([a_pair], [wides], waits)
+        return b1, a, own, opened
 
     def group_of(i):
         return next(g for g, group in enumerate(GROUPS) if i in group)
@@ -518,25 +515,25 @@
         return scan_states(get("early")[2], sc, False)[0]
 
     def build_fold(i):
-        last = i == count - 1
         g = group_of(i)
-        c2 = get(f"c2_{i}")
-        c1 = get(f"c1_{g}")
-        at = (offsets[i] - offsets[GROUPS[g][0]]) * ctx
-        blocks = (
-            own[i], final_form[f"b2_{i}"], (final_form[f"c1_{g}"], at), (c1, at), final_form[f"c2_{i}"], [c2])
-        products = [] if i == 0 else [(None, offsets[i])]
-        if i == 1:
-            products.insert(0, (get("fold_0")[-1], offsets[0]))
-        acc = get(f"fold_{i - 1}")[CORE_SENDS[i - 1] + 1] if i > 1 else None
+        c2, c1 = get(f"c2_{i}"), get(f"c1_{g}")
+        at = (offsets[i] - offsets[GROUPS[g][0]]) * len(order)
+        _, _, own, opened = get("cut")
+        blocks = own[i], final_form[f"b2_{i}"], (final_form[f"c1_{g}"], at), (c1, at), final_form[f"c2_{i}"], c2
+        acc = get(f"fold_{i - 1}")[1 + TOP_SENDS[i - 1]] if i else None
         return fold(
-            blocks, opened, norm, ws, products, acc, q if last else None, CORE_SENDS[i], after(f"fold_{i}"))
+            blocks, opened, norm, ws, offsets[i], acc, TOP_SENDS[i], OG_SENDS if i == count - 1 else 0,
+            after(f"fold_{i}"))
+
+    def build_join():
+        kept, *sends = get(f"fold_{count - 1}")[1 + TOP_SENDS[-1]:]
+        return join(kept, [swap(x, "ctx", core) for x in sends], q, after("join"))
 
     def build_send(i):
         got = get(f"fold_{i}")
-        keep, sends = got[0], got[1:1 + CORE_SENDS[i]]
-        for bit in bits[:-1]:
-            keep, sends = scatter_step(keep, sends, bit, TOP_SENDS[i] if bit == bits[-2] else 1)
+        keep, sends = got[0], got[1:1 + TOP_SENDS[i]]
+        for bit in bits[1:-1]:
+            keep, sends = scatter_step(keep, sends, bit)
         keeps[i] = keep
         waits = after(f"send_{i}")
         return [tie(x, *waits) for x in sends] if waits else sends
@@ -558,11 +555,11 @@
         return [other(x) for x in get(f"mine_{i}")]
 
     def build_later():
-        return scan_states(get(f"fold_{count - 1}")[-1], sc, True)
+        return scan_states(get("join")[1], sc, True)
 
     def build_late():
         mask, s, _ = get("early")
-        og = get(f"fold_{count - 1}")[-2]
+        og = get("join")[0]
         return late(q, k, v, og, s, get("prev"), mask, after("late"))
 
     def build_final():
@@ -572,7 +569,7 @@
     keeps = [None] * count
     builders = {
         "cut": build_cut, "c1": build_c1, "b2": build_b2, "c2": build_c2, "early": build_early, "prev": build_prev,
-        "fold": build_fold, "send": build_send, "mine": build_mine, "last": build_last, "later": build_later,
+        "fold": build_fold, "join": build_join, "send": build_send, "mine": build_mine, "last": build_last, "later": build_later,
         "qg": lambda: get("later")[1], "late": build_late, "final": build_final,
     }
     grown = None

time: 115 us -> 111 us (0.965)
  starting transfers between devices: 35.2 us -> 31.8 us
    ppermute x30 -> x16, starting transfers between devices: 14.7 us -> 12.1 us  [swap(): return lax.ppermute(array, axis, [(i, i ^ bit) for i in range(count)])]
    ppermute x4, waiting for transfers between devices: 2.82 us -> 0.91 us  [other(): return lax.ppermute(x, 'dp', [(0, 1), (1, 0)])]
    ppermute x6 -> x8, waiting for transfers between devices: 17.4 us -> 18.1 us  [the longest x1 9.19 us: outer(): return lax.ppermute(x, 'tsp', OUTER)]
    pallas_call x1 -> x2, Pallas kernels: 2.56 us -> 3.15 us  [load(): pl.pallas_call(kernel, in_specs=[HBM] * count + [ANY] * len(after), out_s...]
    ppermute x6 -> x8, starting transfers between devices: 6.49 us -> 6.79 us  [the longest x5 3.38 us: inner(): return lax.ppermute(x, 'tsp', INNER)]
    ppermute x30 -> x16, waiting for transfers between devices: 9.49 us -> 9.58 us  [swap(): return lax.ppermute(array, axis, [(i, i ^ bit) for i in range(count)])]
  transfers between devices with their start and end apart: 46 -> 34, of which waited for: 14 -> 13; matrix products, arithmetic and copies ran while one was open for 0% -> 0% of each run, Pallas kernels for 15% -> 14%
where the time goes in v4:
time: 111 us
  waiting for transfers between devices  58.1 us (52%)
  starting transfers between devices  31.8 us (29%)
  Pallas kernels  18.4 us (17%)
  between operations  1.17 us (1%)
    ppermute x6, waiting for transfers between devices, to_ends(): return lax.ppermute(x, 'tsp', [(1, 0), (2, 3)])  29.6 us
    ppermute x16, starting transfers between devices, swap(): return lax.ppermute(array, axis, [(i, i ^ bit) for i in range(count)])  12.1 us
    ppermute x16, waiting for transfers between devices, swap(): return lax.ppermute(array, axis, [(i, i ^ bit) for i in range(count)])  9.58 us
    ppermute x1, waiting for transfers between devices, outer(): return lax.ppermute(x, 'tsp', OUTER)  9.19 us
    ppermute x2, waiting for transfers between devices, to_other_core(): lax.ppermute(x, ('ctx', 'tsp'), [(t * 4 + i, (t ^ core) * 4 + j) for t in...  8.85 us
    ppermute x6, starting transfers between devices, to_ends(): return lax.ppermute(x, 'tsp', [(1, 0), (2, 3)])  7.73 us
    pallas_call x4, Pallas kernels, fold(): pl.pallas_call(kernel, in_specs=[VMEM] * len(arrays) + [ANY] * len(after)...  5.63 us
    ppermute x4, starting transfers between devices, other(): return lax.ppermute(x, 'dp', [(0, 1), (1, 0)])  5.26 us
  transfers between devices with their start and end apart: 34, of which 13 were waited for; matrix products, arithmetic and copies ran while one was open for 0% of the time, Pallas kernels for 14%

profile of v4, /device:TPU:0, one launch (start us, length us, event | category | flops | bytes accessed | tf_op | source)
XLA Modules:
  0.0 110.6 jit_solution(7841651669095843730)
XLA Ops:
  0.6 1.2 %load.2 = (bf16[128,2048]{1,0:T(8,128)(2,1)S(1)}, bf16[128,2048]{1,0:T(8,128)(2,1)S(1)}) custom-call(bf16[128,4096]{1,0:T(8,128)(2,1)} %bitcast.11, bf16[128,4096]{1,0:T(8,128)(2,1)} %bitcast.12), custom_call_target="tpu_custom_call" | custom-call | tf_op jit(solution)/shard_map/load/pallas_call | solution.py:119
  2.4 2.6 %collective-permute-start.2 = (bf16[128,2048]{1,0:T(8,128)(2,1)S(1)}, bf16[128,2048]{1,0:T(8,128)(2,1)S(1)}, u32[]{:S(2)}, u32[]{:S(2)}) collective-permute-start(bf16[128,2048]{1,0:T(8,128)(2,1)S(1)} %get-tuple-element.54.refs_2_), channel_id=1, source_target_pairs={{0,2},{2,0},{4,6},{6,4},{1,3},{3,1},{5,7},{7,5},{8,10},{10,8},{12,... | collective-permute-start | bytes 1572872 | tf_op jit(solution)/shard_map/ppermute | solution.py:443
  5.1 1.9 %load.3 = (bf16[512,512]{1,0:T(8,128)(2,1)S(1)}, bf16[512,512]{1,0:T(8,128)(2,1)S(1)}, bf16[512,512]{1,0:T(8,128)(2,1)S(1)}, bf16[512,512]{1,0:T(8,128)(2,1)S(1)}, bf16[1024,512]{1,0:T(8,128)(2,1)S(1)}) custom-call(bf16[512,512]{1,0:T(8,128)(2,1)} %bitcast.13, bf16[512,512]{1,0:T(8,128)(2,1)} %bitcast.14, bf16[512,512]{1,0:T(8,128)(2,1)} %bitcast.15, ...), custom_call_target="tpu_custom_call" | custom-call | tf_op jit(solution)/shard_map/load/pallas_call | solution.py:119
  8.6 9.2 %collective-permute-done.2.refs_0_ = bf16[128,2048]{1,0:T(8,128)(2,1)S(1)} collective-permute-done((bf16[128,2048]{1,0:T(8,128)(2,1)S(1)}, bf16[128,2048]{1,0:T(8,128)(2,1)S(1)}, u32[]{:S(2)}, u32[]{:S(2)}) %collective-permute-start.2) | collective-permute-done | bytes 524320 | tf_op jit(solution)/shard_map/ppermute | solution.py:443
  17.8 1.9 %collective-permute-start.11 = (bf16[1024,512]{1,0:T(8,128)(2,1)S(1)}, bf16[1024,512]{1,0:T(8,128)(2,1)S(1)}, u32[]{:S(2)}, u32[]{:S(2)}) collective-permute-start(bf16[1024,512]{1,0:T(8,128)(2,1)S(1)} %copy-done.2), channel_id=1, source_target_pairs={{0,16},{8,24},{16,0},{24,8},{1,17},{9,25},{17,1},{25,9},{2,18},{10... | collective-permute-start | bytes 3145736 | tf_op jit(solution)/shard_map/ppermute | solution.py:57
  19.7 8.8 %collective-permute-done.3.refs_1_ = bf16[128,2048]{1,0:T(8,128)(2,1)S(1)} collective-permute-done((bf16[128,2048]{1,0:T(8,128)(2,1)S(1)}, bf16[128,2048]{1,0:T(8,128)(2,1)S(1)}, u32[]{:S(2)}, u32[]{:S(2)}) %collective-permute-start.3) | collective-permute-done | bytes 524320 | tf_op jit(solution)/shard_map/ppermute | solution.py:452
  29.5 1.3 %collective-permute-start.7 = (bf16[256,768]{1,0:T(8,128)(2,1)S(1)}, bf16[256,768]{1,0:T(8,128)(2,1)S(1)}, u32[]{:S(2)}, u32[]{:S(2)}) collective-permute-start(bf16[256,768]{1,0:T(8,128)(2,1)S(1)} %get-tuple-element.59.refs_2_), channel_id=1, source_target_pairs={{2,0},{4,6},{3,1},{5,7},{10,8},{12,14},{11,9},{13,15},{18,16},{20,... | collective-permute-start | bytes 1179656 | tf_op jit(solution)/shard_map/ppermute | solution.py:449
  31.4 1.3 %collective-permute-start.16 = (bf16[256,768]{1,0:T(8,128)(2,1)S(1)}, bf16[256,768]{1,0:T(8,128)(2,1)S(1)}, u32[]{:S(2)}, u32[]{:S(2)}) collective-permute-start(bf16[256,768]{1,0:T(8,128)(2,1)S(1)} %collective-permute-done.15.refs_4_), channel_id=1, source_target_pairs={{2,0},{4,6},{3,1},{5,7},{10,8},{12,14},{11,9},{13,15},{18,16},{20,... | collective-permute-start | bytes 1179656 | tf_op jit(solution)/shard_map/ppermute | solution.py:449
  32.8 14.4 %collective-permute-done.7.refs_2_.refs_3_ = bf16[256,768]{1,0:T(8,128)(2,1)S(1)} collective-permute-done((bf16[256,768]{1,0:T(8,128)(2,1)S(1)}, bf16[256,768]{1,0:T(8,128)(2,1)S(1)}, u32[]{:S(2)}, u32[]{:S(2)}) %collective-permute-start.7) | collective-permute-done | bytes 393248 | tf_op jit(solution)/shard_map/ppermute | solution.py:449
  47.2 1.3 %collective-permute-start.8 = (bf16[256,1280]{1,0:T(8,128)(2,1)S(1)}, bf16[256,1280]{1,0:T(8,128)(2,1)S(1)}, u32[]{:S(2)}, u32[]{:S(2)}) collective-permute-start(bf16[256,1280]{1,0:T(8,128)(2,1)S(1)} %tie.1.refs_2_), channel_id=1, source_target_pairs={{2,0},{4,6},{3,1},{5,7},{10,8},{12,14},{11,9},{13,15},{18,16},{20,... | collective-permute-start | bytes 1966088 | tf_op jit(solution)/shard_map/ppermute | solution.py:449
  49.9 6.9 %collective-permute-done.16.refs_5_ = bf16[256,768]{1,0:T(8,128)(2,1)S(1)} collective-permute-done((bf16[256,768]{1,0:T(8,128)(2,1)S(1)}, bf16[256,768]{1,0:T(8,128)(2,1)S(1)}, u32[]{:S(2)}, u32[]{:S(2)}) %collective-permute-start.16) | collective-permute-done | bytes 393248 | tf_op jit(solution)/shard_map/ppermute | solution.py:449
  56.8 1.9 %fold.4 = (f32[384,512]{1,0:T(8,128)S(1)}, bf16[192,512]{1,0:T(8,128)(2,1)S(1)}, bf16[192,512]{1,0:T(8,128)(2,1)S(1)}, f32[1024,512]{1,0:T(8,128)S(1)}) custom-call(bf16[256,768]{1,0:T(8,128)(2,1)S(1)} %get-tuple-element.65.refs_0_, bf16[256,768]{1,0:T(8,128)(2,1)S(1)} %get-tuple-element.66.refs_1_, bf16[256,768]{1,0:T(8,128)(2,1)S(1)} %get-tuple-element.59.refs_2_, ...), custom_call_target="tpu_custom_call" | custom-call | tf_op jit(solution)/shard_map/fold/pallas_call | solution.py:357
  58.7 1.6 %collective-permute-start.19 = (bf16[192,512]{1,0:T(8,128)(2,1)S(1)}, bf16[192,512]{1,0:T(8,128)(2,1)S(1)}, u32[]{:S(2)}, u32[]{:S(2)}) collective-permute-start(bf16[192,512]{1,0:T(8,128)(2,1)S(1)} %get-tuple-element.72), channel_id=1, source_target_pairs={{0,16},{8,24},{16,0},{24,8},{1,17},{9,25},{17,1},{25,9},{2,18},{10... | collective-permute-start | bytes 589832 | tf_op jit(solution)/shard_map/ppermute | solution.py:57
  61.5 1.3 %collective-permute-start.14 = (bf16[256,512]{1,0:T(8,128)(2,1)S(1)}, bf16[256,512]{1,0:T(8,128)(2,1)S(1)}, u32[]{:S(2)}, u32[]{:S(2)}) collective-permute-start(bf16[256,512]{1,0:T(8,128)(2,1)S(1)} %collective-permute-done.6.refs_1_.refs_4_), channel_id=1, source_target_pairs={{2,0},{4,6},{3,1},{5,7},{10,8},{12,14},{11,9},{13,15},{18,16},{20,... | collective-permute-start | bytes 786440 | tf_op jit(solution)/shard_map/ppermute | solution.py:449
  62.8 3.8 %collective-permute-done.19.refs_1_ = bf16[192,512]{1,0:T(8,128)(2,1)S(1)} collective-permute-done((bf16[192,512]{1,0:T(8,128)(2,1)S(1)}, bf16[192,512]{1,0:T(8,128)(2,1)S(1)}, u32[]{:S(2)}, u32[]{:S(2)}) %collective-permute-start.19) | collective-permute-done | bytes 196640 | tf_op jit(solution)/shard_map/ppermute | solution.py:57
  66.6 1.5 %collective-permute-start.18 = (bf16[4,128,128]{2,1,0:T(8,128)(2,1)S(1)}, bf16[4,128,128]{2,1,0:T(8,128)(2,1)S(1)}, u32[]{:S(2)}, u32[]{:S(2)}) collective-permute-start(bf16[4,128,128]{2,1,0:T(8,128)(2,1)S(1)} %add.2), channel_id=1, source_target_pairs={{0,16},{8,24},{16,0},{24,8},{1,17},{9,25},{17,1},{25,9},{2,18},{10... | collective-permute-start | bytes 393224 | tf_op jit(solution)/shard_map/ppermute | solution.py:57
  68.1 1.4 %collective-permute-done.20.refs_2_ = bf16[192,512]{1,0:T(8,128)(2,1)S(1)} collective-permute-done((bf16[192,512]{1,0:T(8,128)(2,1)S(1)}, bf16[192,512]{1,0:T(8,128)(2,1)S(1)}, u32[]{:S(2)}, u32[]{:S(2)}) %collective-permute-start.20) | collective-permute-done | bytes 196640 | tf_op jit(solution)/shard_map/ppermute | solution.py:57
  69.6 1.6 %collective-permute-start.21 = (bf16[384,512]{1,0:T(8,128)(2,1)S(1)}, bf16[384,512]{1,0:T(8,128)(2,1)S(1)}, u32[]{:S(2)}, u32[]{:S(2)}) collective-permute-start(bf16[384,512]{1,0:T(8,128)(2,1)S(1)} %mine.4.refs_0_), channel_id=1, source_target_pairs={{0,1},{1,0},{2,3},{3,2},{4,5},{5,4},{6,7},{7,6},{8,9},{9,8},{10,11... | collective-permute-start | bytes 1179656 | tf_op jit(solution)/shard_map/ppermute | solution.py:456
  72.4 1.3 %collective-permute-start.13 = (bf16[256,512]{1,0:T(8,128)(2,1)S(1)}, bf16[256,512]{1,0:T(8,128)(2,1)S(1)}, u32[]{:S(2)}, u32[]{:S(2)}) collective-permute-start(bf16[256,512]{1,0:T(8,128)(2,1)S(1)} %collective-permute-done.12.refs_4_), channel_id=1, source_target_pairs={{2,0},{4,6},{3,1},{5,7},{10,8},{12,14},{11,9},{13,15},{18,16},{20,... | collective-permute-start | bytes 786440 | tf_op jit(solution)/shard_map/ppermute | solution.py:449
  73.7 2.8 %collective-permute-done.14.refs_5_ = bf16[256,512]{1,0:T(8,128)(2,1)S(1)} collective-permute-done((bf16[256,512]{1,0:T(8,128)(2,1)S(1)}, bf16[256,512]{1,0:T(8,128)(2,1)S(1)}, u32[]{:S(2)}, u32[]{:S(2)}) %collective-permute-start.14) | collective-permute-done | bytes 262176 | tf_op jit(solution)/shard_map/ppermute | solution.py:449
  76.5 1.4 %fold.5 = (f32[256,512]{1,0:T(8,128)S(1)}, bf16[256,512]{1,0:T(8,128)(2,1)S(1)}, f32[1024,512]{1,0:T(8,128)S(1)}) custom-call(bf16[256,512]{1,0:T(8,128)(2,1)S(1)} %get-tuple-element.64.refs_0_, bf16[256,512]{1,0:T(8,128)(2,1)S(1)} %get-tuple-element.58.refs_1_, bf16[256,1280]{1,0:T(8,128)(2,1)S(1)} %tie.1.refs_2_, ...), custom_call_target="tpu_custom_call" | custom-call | tf_op jit(solution)/shard_map/fold/pallas_call | solution.py:357
  77.8 1.6 %collective-permute-start.22 = (bf16[256,512]{1,0:T(8,128)(2,1)S(1)}, bf16[256,512]{1,0:T(8,128)(2,1)S(1)}, u32[]{:S(2)}, u32[]{:S(2)}) collective-permute-start(bf16[256,512]{1,0:T(8,128)(2,1)S(1)} %get-tuple-element.75), channel_id=1, source_target_pairs={{0,16},{8,24},{16,0},{24,8},{1,17},{9,25},{17,1},{25,9},{2,18},{10... | collective-permute-start | bytes 786440 | tf_op jit(solution)/shard_map/ppermute | solution.py:57
  79.4 1.3 %collective-permute-start.10 = (bf16[256,256]{1,0:T(8,128)(2,1)S(1)}, bf16[256,256]{1,0:T(8,128)(2,1)S(1)}, u32[]{:S(2)}, u32[]{:S(2)}) collective-permute-start(bf16[256,256]{1,0:T(8,128)(2,1)S(1)} %collective-permute-done.9.refs_4_), channel_id=1, source_target_pairs={{2,0},{4,6},{3,1},{5,7},{10,8},{12,14},{11,9},{13,15},{18,16},{20,... | collective-permute-start | bytes 393224 | tf_op jit(solution)/shard_map/ppermute | solution.py:449
  80.7 5.6 %collective-permute-done.10.refs_10_.refs_5_ = bf16[256,256]{1,0:T(8,128)(2,1)S(1)} collective-permute-done((bf16[256,256]{1,0:T(8,128)(2,1)S(1)}, bf16[256,256]{1,0:T(8,128)(2,1)S(1)}, u32[]{:S(2)}, u32[]{:S(2)}) %collective-permute-start.10) | collective-permute-done | bytes 131104 | tf_op jit(solution)/shard_map/ppermute | solution.py:449
  86.2 1.4 %fold.6 = (f32[256,512]{1,0:T(8,128)S(1)}, bf16[256,512]{1,0:T(8,128)(2,1)S(1)}, f32[1024,512]{1,0:T(8,128)S(1)}) custom-call(bf16[256,512]{1,0:T(8,128)(2,1)S(1)} %get-tuple-element.62.refs_0_, bf16[256,512]{1,0:T(8,128)(2,1)S(1)} %get-tuple-element.63.refs_1_, bf16[256,1280]{1,0:T(8,128)(2,1)S(1)} %tie.1.refs_2_, ...), custom_call_target="tpu_custom_call" | custom-call | tf_op jit(solution)/shard_map/fold/pallas_call | solution.py:357
  90.3 1.5 %collective-permute-start.32 = (bf16[256,512]{1,0:T(8,128)(2,1)S(1)}, bf16[256,512]{1,0:T(8,128)(2,1)S(1)}, u32[]{:S(2)}, u32[]{:S(2)}) collective-permute-start(bf16[256,512]{1,0:T(8,128)(2,1)S(1)} %mine.5.refs_11_.refs_0_), channel_id=1, source_target_pairs={{0,1},{1,0},{2,3},{3,2},{4,5},{5,4},{6,7},{7,6},{8,9},{9,8},{10,11... | collective-permute-start | bytes 786440 | tf_op jit(solution)/shard_map/ppermute | solution.py:456
  92.4 1.6 %collective-permute-start.29 = (bf16[128,512]{1,0:T(8,128)(2,1)S(1)}, bf16[128,512]{1,0:T(8,128)(2,1)S(1)}, u32[]{:S(2)}, u32[]{:S(2)}) collective-permute-start(bf16[128,512]{1,0:T(8,128)(2,1)S(1)} %get-tuple-element.91), channel_id=1, source_target_pairs={{0,16},{8,24},{16,0},{24,8},{1,17},{9,25},{17,1},{25,9},{2,18},{10... | collective-permute-start | bytes 393224 | tf_op jit(solution)/shard_map/ppermute | solution.py:57
  94.0 2.6 %late.1 = (bf16[512,512]{1,0:T(8,128)(2,1)}, f32[512,512]{1,0:T(8,128)S(1)}, f32[512,512]{1,0:T(8,128)S(1)}) custom-call(bf16[512,512]{1,0:T(8,128)(2,1)S(1)} %get-tuple-element.50.refs_1_.refs_5_.q_ref, bf16[512,512]{1,0:T(8,128)(2,1)S(1)} %get-tuple-element.51.refs_2_.k_ref, bf16[512,512]{1,0:T(8,128)(2,1)S(1)} %get-tuple-element.52.refs_3_.v_ref, ...), custom_call_target="tpu_custom_call" | custom-call | tf_op jit(solution)/shard_map/late/pallas_call | solution.py:258
  96.6 2.3 %collective-permute-done.31.refs_1_ = bf16[256,512]{1,0:T(8,128)(2,1)S(1)} collective-permute-done((bf16[256,512]{1,0:T(8,128)(2,1)S(1)}, bf16[256,512]{1,0:T(8,128)(2,1)S(1)}, u32[]{:S(2)}, u32[]{:S(2)}) %collective-permute-start.31) | collective-permute-done | bytes 262176 | tf_op jit(solution)/shard_map/ppermute | solution.py:57
  100.0 1.6 %collective-permute-start.33 = (bf16[256,512]{1,0:T(8,128)(2,1)S(1)}, bf16[256,512]{1,0:T(8,128)(2,1)S(1)}, u32[]{:S(2)}, u32[]{:S(2)}) collective-permute-start(bf16[256,512]{1,0:T(8,128)(2,1)S(1)} %mine.7.refs_0_), channel_id=1, source_target_pairs={{0,1},{1,0},{2,3},{3,2},{4,5},{5,4},{6,7},{7,6},{8,9},{9,8},{10,11... | collective-permute-start | bytes 786440 | tf_op jit(solution)/shard_map/ppermute | solution.py:456
  104.9 1.7 %collective-permute-done.28.refs_1_ = bf16[4,128,128]{2,1,0:T(8,128)(2,1)S(1)} collective-permute-done((bf16[4,128,128]{2,1,0:T(8,128)(2,1)S(1)}, bf16[4,128,128]{2,1,0:T(8,128)(2,1)S(1)}, u32[]{:S(2)}, u32[]{:S(2)}) %collective-permute-start.28) | collective-permute-done | bytes 131104 | tf_op jit(solution)/shard_map/ppermute | solution.py:57
  106.6 1.3 %final.1 = (bf16[512,512]{1,0:T(8,128)(2,1)}, bf16[512,512]{1,0:T(8,128)(2,1)}) custom-call(bf16[512,512]{1,0:T(8,128)(2,1)S(1)} %get-tuple-element.51.refs_2_.k_ref, bf16[512,512]{1,0:T(8,128)(2,1)S(1)} %get-tuple-element.52.refs_3_.v_ref, bf16[4,128,128]{2,1,0:T(8,128)(2,1)S(1)} %states.3.later_ref, f32[512,512]{1,0:T(8,128)S(1)} %get-tuple-element.86.dkp_ref.refs_3_, ...), custom_call_target="tpu_custom_call" | custom-call | tf_op jit(solution)/shard_map/final/pallas_call | solution.py:285
  (68 shorter events, 17.8 us)
Async XLA Ops:
  1.9 3.2 %collective-permute-start = (bf16[128,2048]{1,0:T(8,128)(2,1)S(1)}, bf16[128,2048]{1,0:T(8,128)(2,1)S(1)}, u32[]{:S(2)}, u32[]{:S(2)}) collective-permute-start(bf16[128,2048]{1,0:T(8,128)(2,1)S(1)} %get-tuple-element.49), channel_id=1, source_target_pairs={{0,8},{8,0},{16,24},{24,16},{1,9},{9,1},{17,25},{25,17},{2,10},{10... | collective-permute-start | bytes 1572872 | tf_op jit(solution)/shard_map/ppermute | solution.py:57
  2.4 15.4 %collective-permute-start.2 = (bf16[128,2048]{1,0:T(8,128)(2,1)S(1)}, bf16[128,2048]{1,0:T(8,128)(2,1)S(1)}, u32[]{:S(2)}, u32[]{:S(2)}) collective-permute-start(bf16[128,2048]{1,0:T(8,128)(2,1)S(1)} %get-tuple-element.54.refs_2_), channel_id=1, source_target_pairs={{0,2},{2,0},{4,6},{6,4},{1,3},{3,1},{5,7},{7,5},{8,10},{10,8},{12,... | collective-permute-start | bytes 1572872 | tf_op jit(solution)/shard_map/ppermute | solution.py:443
  5.1 23.5 %collective-permute-start.3 = (bf16[128,2048]{1,0:T(8,128)(2,1)S(1)}, bf16[128,2048]{1,0:T(8,128)(2,1)S(1)}, u32[]{:S(2)}, u32[]{:S(2)}) collective-permute-start(bf16[128,2048]{1,0:T(8,128)(2,1)S(1)} %get-tuple-element.49), channel_id=1, source_target_pairs={{0,10},{2,8},{4,14},{6,12},{8,2},{10,0},{12,6},{14,4},{16,26},{18,... | collective-permute-start | bytes 1572872 | tf_op jit(solution)/shard_map/ppermute | solution.py:452
  7.1 21.5 %collective-permute-start.1 = (bf16[512,512]{1,0:T(8,128)(2,1)S(1)}, bf16[512,512]{1,0:T(8,128)(2,1)S(1)}, u32[]{:S(2)}, u32[]{:S(2)}) collective-permute-start(bf16[512,512]{1,0:T(8,128)(2,1)S(1)} %get-tuple-element.53.refs_0_), channel_id=1, source_target_pairs={{0,8},{8,0},{16,24},{24,16},{1,9},{9,1},{17,25},{25,17},{2,10},{10... | collective-permute-start | bytes 1572872 | tf_op jit(solution)/shard_map/ppermute | solution.py:57
  7.3 22.1 %collective-permute-start.4 = (bf16[128,2048]{1,0:T(8,128)(2,1)S(1)}, bf16[128,2048]{1,0:T(8,128)(2,1)S(1)}, u32[]{:S(2)}, u32[]{:S(2)}) collective-permute-start(bf16[128,2048]{1,0:T(8,128)(2,1)S(1)} %get-tuple-element.54.refs_2_), channel_id=1, source_target_pairs={{2,4},{4,2},{3,5},{5,3},{10,12},{12,10},{11,13},{13,11},{18,20},{2... | collective-permute-start | bytes 1572872 | tf_op jit(solution)/shard_map/ppermute | solution.py:446
  7.9 21.4 %collective-permute-start.5 = (bf16[128,2048]{1,0:T(8,128)(2,1)S(1)}, bf16[128,2048]{1,0:T(8,128)(2,1)S(1)}, u32[]{:S(2)}, u32[]{:S(2)}) collective-permute-start(bf16[128,2048]{1,0:T(8,128)(2,1)S(1)} %get-tuple-element.49), channel_id=1, source_target_pairs={{2,12},{4,10},{10,4},{12,2},{18,28},{20,26},{26,20},{28,18},{3,13}... | collective-permute-start | bytes 1572872 | tf_op jit(solution)/shard_map/ppermute | solution.py:452
  17.8 32.1 %collective-permute-start.11 = (bf16[1024,512]{1,0:T(8,128)(2,1)S(1)}, bf16[1024,512]{1,0:T(8,128)(2,1)S(1)}, u32[]{:S(2)}, u32[]{:S(2)}) collective-permute-start(bf16[1024,512]{1,0:T(8,128)(2,1)S(1)} %copy-done.2), channel_id=1, source_target_pairs={{0,16},{8,24},{16,0},{24,8},{1,17},{9,25},{17,1},{25,9},{2,18},{10... | collective-permute-start | bytes 3145736 | tf_op jit(solution)/shard_map/ppermute | solution.py:57
  28.7 2.8 %collective-permute-start.15 = (bf16[256,768]{1,0:T(8,128)(2,1)S(1)}, bf16[256,768]{1,0:T(8,128)(2,1)S(1)}, u32[]{:S(2)}, u32[]{:S(2)}) collective-permute-start(bf16[256,768]{1,0:T(8,128)(2,1)S(1)} %get-tuple-element.66.refs_1_), channel_id=1, source_target_pairs={{2,4},{4,2},{3,5},{5,3},{10,12},{12,10},{11,13},{13,11},{18,20},{2... | collective-permute-start | bytes 1179656 | tf_op jit(solution)/shard_map/ppermute | solution.py:446
  29.5 17.7 %collective-permute-start.7 = (bf16[256,768]{1,0:T(8,128)(2,1)S(1)}, bf16[256,768]{1,0:T(8,128)(2,1)S(1)}, u32[]{:S(2)}, u32[]{:S(2)}) collective-permute-start(bf16[256,768]{1,0:T(8,128)(2,1)S(1)} %get-tuple-element.59.refs_2_), channel_id=1, source_target_pairs={{2,0},{4,6},{3,1},{5,7},{10,8},{12,14},{11,9},{13,15},{18,16},{20,... | collective-permute-start | bytes 1179656 | tf_op jit(solution)/shard_map/ppermute | solution.py:449
  30.8 2.0 %collective-permute-start.6 = (bf16[256,512]{1,0:T(8,128)(2,1)S(1)}, bf16[256,512]{1,0:T(8,128)(2,1)S(1)}, u32[]{:S(2)}, u32[]{:S(2)}) collective-permute-start(bf16[256,512]{1,0:T(8,128)(2,1)S(1)} %get-tuple-element.58.refs_1_), channel_id=1, source_target_pairs={{2,4},{4,2},{3,5},{5,3},{10,12},{12,10},{11,13},{13,11},{18,20},{2... | collective-permute-start | bytes 786440 | tf_op jit(solution)/shard_map/ppermute | solution.py:446
  31.4 25.3 %collective-permute-start.16 = (bf16[256,768]{1,0:T(8,128)(2,1)S(1)}, bf16[256,768]{1,0:T(8,128)(2,1)S(1)}, u32[]{:S(2)}, u32[]{:S(2)}) collective-permute-start(bf16[256,768]{1,0:T(8,128)(2,1)S(1)} %collective-permute-done.15.refs_4_), channel_id=1, source_target_pairs={{2,0},{4,6},{3,1},{5,7},{10,8},{12,14},{11,9},{13,15},{18,16},{20,... | collective-permute-start | bytes 1179656 | tf_op jit(solution)/shard_map/ppermute | solution.py:449
  47.2 29.3 %collective-permute-start.8 = (bf16[256,1280]{1,0:T(8,128)(2,1)S(1)}, bf16[256,1280]{1,0:T(8,128)(2,1)S(1)}, u32[]{:S(2)}, u32[]{:S(2)}) collective-permute-start(bf16[256,1280]{1,0:T(8,128)(2,1)S(1)} %tie.1.refs_2_), channel_id=1, source_target_pairs={{2,0},{4,6},{3,1},{5,7},{10,8},{12,14},{11,9},{13,15},{18,16},{20,... | collective-permute-start | bytes 1966088 | tf_op jit(solution)/shard_map/ppermute | solution.py:449
  49.6 11.9 %collective-permute-start.17 = (bf16[4,128,128]{2,1,0:T(8,128)(2,1)S(1)}, bf16[4,128,128]{2,1,0:T(8,128)(2,1)S(1)}, u32[]{:S(2)}, u32[]{:S(2)}) collective-permute-start(bf16[4,128,128]{2,1,0:T(8,128)(2,1)S(1)} %get-tuple-element.68.refs_0_), channel_id=1, source_target_pairs={{0,8},{8,0},{16,24},{24,16},{1,9},{9,1},{17,25},{25,17},{2,10},{10... | collective-permute-start | bytes 393224 | tf_op jit(solution)/shard_map/ppermute | solution.py:57
  58.7 7.9 %collective-permute-start.19 = (bf16[192,512]{1,0:T(8,128)(2,1)S(1)}, bf16[192,512]{1,0:T(8,128)(2,1)S(1)}, u32[]{:S(2)}, u32[]{:S(2)}) collective-permute-start(bf16[192,512]{1,0:T(8,128)(2,1)S(1)} %get-tuple-element.72), channel_id=1, source_target_pairs={{0,16},{8,24},{16,0},{24,8},{1,17},{9,25},{17,1},{25,9},{2,18},{10... | collective-permute-start | bytes 589832 | tf_op jit(solution)/shard_map/ppermute | solution.py:57
  60.3 9.3 %collective-permute-start.20 = (bf16[192,512]{1,0:T(8,128)(2,1)S(1)}, bf16[192,512]{1,0:T(8,128)(2,1)S(1)}, u32[]{:S(2)}, u32[]{:S(2)}) collective-permute-start(bf16[192,512]{1,0:T(8,128)(2,1)S(1)} %get-tuple-element.73), channel_id=1, source_target_pairs={{0,16},{8,24},{16,0},{24,8},{1,17},{9,25},{17,1},{25,9},{2,18},{10... | collective-permute-start | bytes 589832 | tf_op jit(solution)/shard_map/ppermute | solution.py:57
  60.8 11.5 %collective-permute-start.12 = (bf16[256,512]{1,0:T(8,128)(2,1)S(1)}, bf16[256,512]{1,0:T(8,128)(2,1)S(1)}, u32[]{:S(2)}, u32[]{:S(2)}) collective-permute-start(bf16[256,512]{1,0:T(8,128)(2,1)S(1)} %get-tuple-element.63.refs_1_), channel_id=1, source_target_pairs={{2,4},{4,2},{3,5},{5,3},{10,12},{12,10},{11,13},{13,11},{18,20},{2... | collective-permute-start | bytes 786440 | tf_op jit(solution)/shard_map/ppermute | solution.py:446
  61.5 15.0 %collective-permute-start.14 = (bf16[256,512]{1,0:T(8,128)(2,1)S(1)}, bf16[256,512]{1,0:T(8,128)(2,1)S(1)}, u32[]{:S(2)}, u32[]{:S(2)}) collective-permute-start(bf16[256,512]{1,0:T(8,128)(2,1)S(1)} %collective-permute-done.6.refs_1_.refs_4_), channel_id=1, source_target_pairs={{2,0},{4,6},{3,1},{5,7},{10,8},{12,14},{11,9},{13,15},{18,16},{20,... | collective-permute-start | bytes 786440 | tf_op jit(solution)/shard_map/ppermute | solution.py:449
  66.6 5.0 %collective-permute-start.18 = (bf16[4,128,128]{2,1,0:T(8,128)(2,1)S(1)}, bf16[4,128,128]{2,1,0:T(8,128)(2,1)S(1)}, u32[]{:S(2)}, u32[]{:S(2)}) collective-permute-start(bf16[4,128,128]{2,1,0:T(8,128)(2,1)S(1)} %add.2), channel_id=1, source_target_pairs={{0,16},{8,24},{16,0},{24,8},{1,17},{9,25},{17,1},{25,9},{2,18},{10... | collective-permute-start | bytes 393224 | tf_op jit(solution)/shard_map/ppermute | solution.py:57
  69.6 18.1 %collective-permute-start.21 = (bf16[384,512]{1,0:T(8,128)(2,1)S(1)}, bf16[384,512]{1,0:T(8,128)(2,1)S(1)}, u32[]{:S(2)}, u32[]{:S(2)}) collective-permute-start(bf16[384,512]{1,0:T(8,128)(2,1)S(1)} %mine.4.refs_0_), channel_id=1, source_target_pairs={{0,1},{1,0},{2,3},{3,2},{4,5},{5,4},{6,7},{7,6},{8,9},{9,8},{10,11... | collective-permute-start | bytes 1179656 | tf_op jit(solution)/shard_map/ppermute | solution.py:456
  71.7 7.7 %collective-permute-start.9 = (bf16[256,256]{1,0:T(8,128)(2,1)S(1)}, bf16[256,256]{1,0:T(8,128)(2,1)S(1)}, u32[]{:S(2)}, u32[]{:S(2)}) collective-permute-start(bf16[256,256]{1,0:T(8,128)(2,1)S(1)} %get-tuple-element.56.refs_1_), channel_id=1, source_target_pairs={{2,4},{4,2},{3,5},{5,3},{10,12},{12,10},{11,13},{13,11},{18,20},{2... | collective-permute-start | bytes 393224 | tf_op jit(solution)/shard_map/ppermute | solution.py:446
  72.4 13.9 %collective-permute-start.13 = (bf16[256,512]{1,0:T(8,128)(2,1)S(1)}, bf16[256,512]{1,0:T(8,128)(2,1)S(1)}, u32[]{:S(2)}, u32[]{:S(2)}) collective-permute-start(bf16[256,512]{1,0:T(8,128)(2,1)S(1)} %collective-permute-done.12.refs_4_), channel_id=1, source_target_pairs={{2,0},{4,6},{3,1},{5,7},{10,8},{12,14},{11,9},{13,15},{18,16},{20,... | collective-permute-start | bytes 786440 | tf_op jit(solution)/shard_map/ppermute | solution.py:449
  77.8 9.8 %collective-permute-start.22 = (bf16[256,512]{1,0:T(8,128)(2,1)S(1)}, bf16[256,512]{1,0:T(8,128)(2,1)S(1)}, u32[]{:S(2)}, u32[]{:S(2)}) collective-permute-start(bf16[256,512]{1,0:T(8,128)(2,1)S(1)} %get-tuple-element.75), channel_id=1, source_target_pairs={{0,16},{8,24},{16,0},{24,8},{1,17},{9,25},{17,1},{25,9},{2,18},{10... | collective-permute-start | bytes 786440 | tf_op jit(solution)/shard_map/ppermute | solution.py:57
  79.4 6.9 %collective-permute-start.10 = (bf16[256,256]{1,0:T(8,128)(2,1)S(1)}, bf16[256,256]{1,0:T(8,128)(2,1)S(1)}, u32[]{:S(2)}, u32[]{:S(2)}) collective-permute-start(bf16[256,256]{1,0:T(8,128)(2,1)S(1)} %collective-permute-done.9.refs_4_), channel_id=1, source_target_pairs={{2,0},{4,6},{3,1},{5,7},{10,8},{12,14},{11,9},{13,15},{18,16},{20,... | collective-permute-start | bytes 393224 | tf_op jit(solution)/shard_map/ppermute | solution.py:449
  88.7 3.1 %collective-permute-start.24 = (bf16[128,512]{1,0:T(8,128)(2,1)S(1)}, bf16[128,512]{1,0:T(8,128)(2,1)S(1)}, u32[]{:S(2)}, u32[]{:S(2)}) collective-permute-start(bf16[128,512]{1,0:T(8,128)(2,1)S(1)} %get-tuple-element.78), channel_id=1, source_target_pairs={{0,8},{8,0},{16,24},{24,16},{1,9},{9,1},{17,25},{25,17},{2,10},{10... | collective-permute-start | bytes 393224 | tf_op jit(solution)/shard_map/ppermute | solution.py:57
  89.2 2.6 %collective-permute-start.25 = (bf16[128,512]{1,0:T(8,128)(2,1)S(1)}, bf16[128,512]{1,0:T(8,128)(2,1)S(1)}, u32[]{:S(2)}, u32[]{:S(2)}) collective-permute-start(bf16[128,512]{1,0:T(8,128)(2,1)S(1)} %get-tuple-element.79), channel_id=1, source_target_pairs={{0,8},{8,0},{16,24},{24,16},{1,9},{9,1},{17,25},{25,17},{2,10},{10... | collective-permute-start | bytes 393224 | tf_op jit(solution)/shard_map/ppermute | solution.py:57
  89.3 2.5 %collective-permute-start.26 = (bf16[128,512]{1,0:T(8,128)(2,1)S(1)}, bf16[128,512]{1,0:T(8,128)(2,1)S(1)}, u32[]{:S(2)}, u32[]{:S(2)}) collective-permute-start(bf16[128,512]{1,0:T(8,128)(2,1)S(1)} %get-tuple-element.80), channel_id=1, source_target_pairs={{0,8},{8,0},{16,24},{24,16},{1,9},{9,1},{17,25},{25,17},{2,10},{10... | collective-permute-start | bytes 393224 | tf_op jit(solution)/shard_map/ppermute | solution.py:57
  89.8 9.2 %collective-permute-start.31 = (bf16[256,512]{1,0:T(8,128)(2,1)S(1)}, bf16[256,512]{1,0:T(8,128)(2,1)S(1)}, u32[]{:S(2)}, u32[]{:S(2)}) collective-permute-start(bf16[256,512]{1,0:T(8,128)(2,1)S(1)} %get-tuple-element.93), channel_id=1, source_target_pairs={{0,16},{8,24},{16,0},{24,8},{1,17},{9,25},{17,1},{25,9},{2,18},{10... | collective-permute-start | bytes 786440 | tf_op jit(solution)/shard_map/ppermute | solution.py:57
  90.3 8.6 %collective-permute-start.32 = (bf16[256,512]{1,0:T(8,128)(2,1)S(1)}, bf16[256,512]{1,0:T(8,128)(2,1)S(1)}, u32[]{:S(2)}, u32[]{:S(2)}) collective-permute-start(bf16[256,512]{1,0:T(8,128)(2,1)S(1)} %mine.5.refs_11_.refs_0_), channel_id=1, source_target_pairs={{0,1},{1,0},{2,3},{3,2},{4,5},{5,4},{6,7},{7,6},{8,9},{9,8},{10,11... | collective-permute-start | bytes 786440 | tf_op jit(solution)/shard_map/ppermute | solution.py:456
  92.4 10.1 %collective-permute-start.29 = (bf16[128,512]{1,0:T(8,128)(2,1)S(1)}, bf16[128,512]{1,0:T(8,128)(2,1)S(1)}, u32[]{:S(2)}, u32[]{:S(2)}) collective-permute-start(bf16[128,512]{1,0:T(8,128)(2,1)S(1)} %get-tuple-element.91), channel_id=1, source_target_pairs={{0,16},{8,24},{16,0},{24,8},{1,17},{9,25},{17,1},{25,9},{2,18},{10... | collective-permute-start | bytes 393224 | tf_op jit(solution)/shard_map/ppermute | solution.py:57
  100.0 8.3 %collective-permute-start.33 = (bf16[256,512]{1,0:T(8,128)(2,1)S(1)}, bf16[256,512]{1,0:T(8,128)(2,1)S(1)}, u32[]{:S(2)}, u32[]{:S(2)}) collective-permute-start(bf16[256,512]{1,0:T(8,128)(2,1)S(1)} %mine.7.refs_0_), channel_id=1, source_target_pairs={{0,1},{1,0},{2,3},{3,2},{4,5},{5,4},{6,7},{7,6},{8,9},{9,8},{10,11... | collective-permute-start | bytes 786440 | tf_op jit(solution)/shard_map/ppermute | solution.py:456
  101.6 5.0 %collective-permute-start.28 = (bf16[4,128,128]{2,1,0:T(8,128)(2,1)S(1)}, bf16[4,128,128]{2,1,0:T(8,128)(2,1)S(1)}, u32[]{:S(2)}, u32[]{:S(2)}) collective-permute-start(bf16[4,128,128]{2,1,0:T(8,128)(2,1)S(1)} %add.3.refs_0_), channel_id=1, source_target_pairs={{0,16},{8,24},{16,0},{24,8},{1,17},{9,25},{17,1},{25,9},{2,18},{10... | collective-permute-start | bytes 393224 | tf_op jit(solution)/shard_map/ppermute | solution.py:57
  102.5 7.2 %collective-permute-start.30 = (bf16[128,512]{1,0:T(8,128)(2,1)S(1)}, bf16[128,512]{1,0:T(8,128)(2,1)S(1)}, u32[]{:S(2)}, u32[]{:S(2)}) collective-permute-start(bf16[128,512]{1,0:T(8,128)(2,1)S(1)} %mine.6.refs_0_), channel_id=1, source_target_pairs={{0,1},{1,0},{2,3},{3,2},{4,5},{5,4},{6,7},{7,6},{8,9},{9,8},{10,11... | collective-permute-start | bytes 393224 | tf_op jit(solution)/shard_map/ppermute | solution.py:456
  (5 other events, 40.1 us)

commit v5 on v4

--- a/solution.py
+++ b/solution.py
@@ -14,10 +14,11 @@
 GROUPS = ((0,), (1, 2, 3))
 TOP_SENDS = (2, 1, 1, 1)
 LAST_SENDS = (1, 1, 1, 1)
-OG_SENDS = 4
+OG_SENDS = 2
 AFTER = {
     "cut": ("opened",),
-    "c1_1": ("b2_1", "c1_0"),
+    "c1_1": ("b2_0", "c1_0"),
+    "c2_1": ("b2_0",),
     "late": ("qg",),
     "mine_2": ("late", "last_1"),
     "fold_1": ("prev",),
@@ -302,7 +303,7 @@
     arrays = [own, a, b1, c1, b2, c2, opened, *ws] + ([] if acc is None else [acc])
     outs = [((half, width), F32)] + [((half // sends, width), BF16)] * sends
     if last:
-        outs += [((group, width), F32)] + [((group // og_sends, width), BF16)] * og_sends
+        outs += [((group, width), F32)] + [((group // og_sends, width), F32)] * og_sends
     else:
         outs.append(((length, width), F32))
 
@@ -350,7 +351,7 @@
             og_ref[...] = total[:group]
             for i, ref in enumerate(og_refs):
                 at = group + i * ref.shape[0]
-                ref[...] = total[at:at + ref.shape[0]].astype(BF16)
+                ref[...] = total[at:at + ref.shape[0]]
         else:
             og_ref[...] = total
 

time: 111 us -> 109 us (0.982)
    ppermute x6, waiting for transfers between devices: 29.6 us -> 28 us  [to_ends(): return lax.ppermute(x, 'tsp', [(1, 0), (2, 3)])]
    ppermute x16 -> x14, waiting for transfers between devices: 9.58 us -> 10.5 us  [swap(): return lax.ppermute(array, axis, [(i, i ^ bit) for i in range(count)])]
    ppermute x16 -> x14, starting transfers between devices: 12.1 us -> 11.5 us  [swap(): return lax.ppermute(array, axis, [(i, i ^ bit) for i in range(count)])]
  transfers between devices with their start and end apart: 34 -> 32, of which waited for: 13 -> 13; matrix products, arithmetic and copies ran while one was open for 0% -> 0% of each run, Pallas kernels for 14% -> 14%
where the time goes in v5:
time: 109 us
  waiting for transfers between devices  57.2 us (52%)
  starting transfers between devices  31.3 us (29%)
  Pallas kernels  18.2 us (17%)
    ppermute x6, waiting for transfers between devices, to_ends(): return lax.ppermute(x, 'tsp', [(1, 0), (2, 3)])  28 us
    ppermute x14, starting transfers between devices, swap(): return lax.ppermute(array, axis, [(i, i ^ bit) for i in range(count)])  11.5 us
    ppermute x14, waiting for transfers between devices, swap(): return lax.ppermute(array, axis, [(i, i ^ bit) for i in range(count)])  10.5 us
    ppermute x1, waiting for transfers between devices, outer(): return lax.ppermute(x, 'tsp', OUTER)  9.19 us
    ppermute x2, waiting for transfers between devices, to_other_core(): lax.ppermute(x, ('ctx', 'tsp'), [(t * 4 + i, (t ^ core) * 4 + j) for t in...  8.85 us
    ppermute x6, starting transfers between devices, to_ends(): return lax.ppermute(x, 'tsp', [(1, 0), (2, 3)])  7.73 us
    pallas_call x4, Pallas kernels, fold(): pl.pallas_call(kernel, in_specs=[VMEM] * len(arrays) + [ANY] * len(after)...  5.44 us
    ppermute x4, starting transfers between devices, other(): return lax.ppermute(x, 'dp', [(0, 1), (1, 0)])  5.26 us
  transfers between devices with their start and end apart: 32, of which 13 were waited for; matrix products, arithmetic and copies ran while one was open for 0% of the time, Pallas kernels for 14%

profile of v5, /device:TPU:0, one launch (start us, length us, event | category | flops | bytes accessed | tf_op | source)
XLA Modules:
  0.0 108.7 jit_solution(16710030132908538806)
XLA Ops:
  0.6 1.2 %load.2 = (bf16[128,2048]{1,0:T(8,128)(2,1)S(1)}, bf16[128,2048]{1,0:T(8,128)(2,1)S(1)}) custom-call(bf16[128,4096]{1,0:T(8,128)(2,1)} %bitcast.11, bf16[128,4096]{1,0:T(8,128)(2,1)} %bitcast.12), custom_call_target="tpu_custom_call" | custom-call | tf_op jit(solution)/shard_map/load/pallas_call | solution.py:120
  2.4 2.6 %collective-permute-start.2 = (bf16[128,2048]{1,0:T(8,128)(2,1)S(1)}, bf16[128,2048]{1,0:T(8,128)(2,1)S(1)}, u32[]{:S(2)}, u32[]{:S(2)}) collective-permute-start(bf16[128,2048]{1,0:T(8,128)(2,1)S(1)} %get-tuple-element.52.refs_2_), channel_id=1, source_target_pairs={{0,2},{2,0},{4,6},{6,4},{1,3},{3,1},{5,7},{7,5},{8,10},{10,8},{12,... | collective-permute-start | bytes 1572872 | tf_op jit(solution)/shard_map/ppermute | solution.py:444
  5.1 1.9 %load.3 = (bf16[512,512]{1,0:T(8,128)(2,1)S(1)}, bf16[512,512]{1,0:T(8,128)(2,1)S(1)}, bf16[512,512]{1,0:T(8,128)(2,1)S(1)}, bf16[512,512]{1,0:T(8,128)(2,1)S(1)}, bf16[1024,512]{1,0:T(8,128)(2,1)S(1)}) custom-call(bf16[512,512]{1,0:T(8,128)(2,1)} %bitcast.13, bf16[512,512]{1,0:T(8,128)(2,1)} %bitcast.14, bf16[512,512]{1,0:T(8,128)(2,1)} %bitcast.15, ...), custom_call_target="tpu_custom_call" | custom-call | tf_op jit(solution)/shard_map/load/pallas_call | solution.py:120
  8.6 9.2 %collective-permute-done.2.refs_0_ = bf16[128,2048]{1,0:T(8,128)(2,1)S(1)} collective-permute-done((bf16[128,2048]{1,0:T(8,128)(2,1)S(1)}, bf16[128,2048]{1,0:T(8,128)(2,1)S(1)}, u32[]{:S(2)}, u32[]{:S(2)}) %collective-permute-start.2) | collective-permute-done | bytes 524320 | tf_op jit(solution)/shard_map/ppermute | solution.py:444
  17.8 1.9 %collective-permute-start.11 = (bf16[1024,512]{1,0:T(8,128)(2,1)S(1)}, bf16[1024,512]{1,0:T(8,128)(2,1)S(1)}, u32[]{:S(2)}, u32[]{:S(2)}) collective-permute-start(bf16[1024,512]{1,0:T(8,128)(2,1)S(1)} %copy-done.2), channel_id=1, source_target_pairs={{0,16},{8,24},{16,0},{24,8},{1,17},{9,25},{17,1},{25,9},{2,18},{10... | collective-permute-start | bytes 3145736 | tf_op jit(solution)/shard_map/ppermute | solution.py:58
  19.7 8.8 %collective-permute-done.3.refs_1_ = bf16[128,2048]{1,0:T(8,128)(2,1)S(1)} collective-permute-done((bf16[128,2048]{1,0:T(8,128)(2,1)S(1)}, bf16[128,2048]{1,0:T(8,128)(2,1)S(1)}, u32[]{:S(2)}, u32[]{:S(2)}) %collective-permute-start.3) | collective-permute-done | bytes 524320 | tf_op jit(solution)/shard_map/ppermute | solution.py:453
  29.5 1.3 %collective-permute-start.7 = (bf16[256,768]{1,0:T(8,128)(2,1)S(1)}, bf16[256,768]{1,0:T(8,128)(2,1)S(1)}, u32[]{:S(2)}, u32[]{:S(2)}) collective-permute-start(bf16[256,768]{1,0:T(8,128)(2,1)S(1)} %get-tuple-element.57.refs_2_), channel_id=1, source_target_pairs={{2,0},{4,6},{3,1},{5,7},{10,8},{12,14},{11,9},{13,15},{18,16},{20,... | collective-permute-start | bytes 1179656 | tf_op jit(solution)/shard_map/ppermute | solution.py:450
  30.8 1.3 %collective-permute-start.16 = (bf16[256,768]{1,0:T(8,128)(2,1)S(1)}, bf16[256,768]{1,0:T(8,128)(2,1)S(1)}, u32[]{:S(2)}, u32[]{:S(2)}) collective-permute-start(bf16[256,768]{1,0:T(8,128)(2,1)S(1)} %collective-permute-done.6.refs_1_.refs_4_), channel_id=1, source_target_pairs={{2,0},{4,6},{3,1},{5,7},{10,8},{12,14},{11,9},{13,15},{18,16},{20,... | collective-permute-start | bytes 1179656 | tf_op jit(solution)/shard_map/ppermute | solution.py:450
  32.1 15.1 %collective-permute-done.7.refs_2_.refs_3_ = bf16[256,768]{1,0:T(8,128)(2,1)S(1)} collective-permute-done((bf16[256,768]{1,0:T(8,128)(2,1)S(1)}, bf16[256,768]{1,0:T(8,128)(2,1)S(1)}, u32[]{:S(2)}, u32[]{:S(2)}) %collective-permute-start.7) | collective-permute-done | bytes 393248 | tf_op jit(solution)/shard_map/ppermute | solution.py:450
  47.2 1.3 %collective-permute-start.8 = (bf16[256,1280]{1,0:T(8,128)(2,1)S(1)}, bf16[256,1280]{1,0:T(8,128)(2,1)S(1)}, u32[]{:S(2)}, u32[]{:S(2)}) collective-permute-start(bf16[256,1280]{1,0:T(8,128)(2,1)S(1)} %tie.2.refs_2_), channel_id=1, source_target_pairs={{2,0},{4,6},{3,1},{5,7},{10,8},{12,14},{11,9},{13,15},{18,16},{20,... | collective-permute-start | bytes 1966088 | tf_op jit(solution)/shard_map/ppermute | solution.py:450
  50.6 5.4 %collective-permute-done.16.refs_5_ = bf16[256,768]{1,0:T(8,128)(2,1)S(1)} collective-permute-done((bf16[256,768]{1,0:T(8,128)(2,1)S(1)}, bf16[256,768]{1,0:T(8,128)(2,1)S(1)}, u32[]{:S(2)}, u32[]{:S(2)}) %collective-permute-start.16) | collective-permute-done | bytes 393248 | tf_op jit(solution)/shard_map/ppermute | solution.py:450
  56.1 1.9 %fold.4 = (f32[384,512]{1,0:T(8,128)S(1)}, bf16[192,512]{1,0:T(8,128)(2,1)S(1)}, bf16[192,512]{1,0:T(8,128)(2,1)S(1)}, f32[1024,512]{1,0:T(8,128)S(1)}) custom-call(bf16[256,768]{1,0:T(8,128)(2,1)S(1)} %get-tuple-element.64.refs_0_, bf16[256,768]{1,0:T(8,128)(2,1)S(1)} %get-tuple-element.56.refs_1_, bf16[256,768]{1,0:T(8,128)(2,1)S(1)} %get-tuple-element.57.refs_2_, ...), custom_call_target="tpu_custom_call" | custom-call | tf_op jit(solution)/shard_map/fold/pallas_call | solution.py:358
  58.0 1.6 %collective-permute-start.19 = (bf16[192,512]{1,0:T(8,128)(2,1)S(1)}, bf16[192,512]{1,0:T(8,128)(2,1)S(1)}, u32[]{:S(2)}, u32[]{:S(2)}) collective-permute-start(bf16[192,512]{1,0:T(8,128)(2,1)S(1)} %get-tuple-element.70), channel_id=1, source_target_pairs={{0,16},{8,24},{16,0},{24,8},{1,17},{9,25},{17,1},{25,9},{2,18},{10... | collective-permute-start | bytes 589832 | tf_op jit(solution)/shard_map/ppermute | solution.py:58
  60.8 1.3 %collective-permute-start.15 = (bf16[256,512]{1,0:T(8,128)(2,1)S(1)}, bf16[256,512]{1,0:T(8,128)(2,1)S(1)}, u32[]{:S(2)}, u32[]{:S(2)}) collective-permute-start(bf16[256,512]{1,0:T(8,128)(2,1)S(1)} %tie.3.refs_4_), channel_id=1, source_target_pairs={{2,0},{4,6},{3,1},{5,7},{10,8},{12,14},{11,9},{13,15},{18,16},{20,... | collective-permute-start | bytes 786440 | tf_op jit(solution)/shard_map/ppermute | solution.py:450
  62.1 3.7 %collective-permute-done.19.refs_1_ = bf16[192,512]{1,0:T(8,128)(2,1)S(1)} collective-permute-done((bf16[192,512]{1,0:T(8,128)(2,1)S(1)}, bf16[192,512]{1,0:T(8,128)(2,1)S(1)}, u32[]{:S(2)}, u32[]{:S(2)}) %collective-permute-start.19) | collective-permute-done | bytes 196640 | tf_op jit(solution)/shard_map/ppermute | solution.py:58
  65.8 1.5 %collective-permute-start.18 = (bf16[4,128,128]{2,1,0:T(8,128)(2,1)S(1)}, bf16[4,128,128]{2,1,0:T(8,128)(2,1)S(1)}, u32[]{:S(2)}, u32[]{:S(2)}) collective-permute-start(bf16[4,128,128]{2,1,0:T(8,128)(2,1)S(1)} %add.2), channel_id=1, source_target_pairs={{0,16},{8,24},{16,0},{24,8},{1,17},{9,25},{17,1},{25,9},{2,18},{10... | collective-permute-start | bytes 393224 | tf_op jit(solution)/shard_map/ppermute | solution.py:58
  67.3 2.7 %collective-permute-done.20.refs_2_ = bf16[192,512]{1,0:T(8,128)(2,1)S(1)} collective-permute-done((bf16[192,512]{1,0:T(8,128)(2,1)S(1)}, bf16[192,512]{1,0:T(8,128)(2,1)S(1)}, u32[]{:S(2)}, u32[]{:S(2)}) %collective-permute-start.20) | collective-permute-done | bytes 196640 | tf_op jit(solution)/shard_map/ppermute | solution.py:58
  70.1 1.6 %collective-permute-start.21 = (bf16[384,512]{1,0:T(8,128)(2,1)S(1)}, bf16[384,512]{1,0:T(8,128)(2,1)S(1)}, u32[]{:S(2)}, u32[]{:S(2)}) collective-permute-start(bf16[384,512]{1,0:T(8,128)(2,1)S(1)} %mine.4.refs_0_), channel_id=1, source_target_pairs={{0,1},{1,0},{2,3},{3,2},{4,5},{5,4},{6,7},{7,6},{8,9},{9,8},{10,11... | collective-permute-start | bytes 1179656 | tf_op jit(solution)/shard_map/ppermute | solution.py:457
  72.5 1.3 %collective-permute-start.13 = (bf16[256,512]{1,0:T(8,128)(2,1)S(1)}, bf16[256,512]{1,0:T(8,128)(2,1)S(1)}, u32[]{:S(2)}, u32[]{:S(2)}) collective-permute-start(bf16[256,512]{1,0:T(8,128)(2,1)S(1)} %collective-permute-done.12.refs_4_), channel_id=1, source_target_pairs={{2,0},{4,6},{3,1},{5,7},{10,8},{12,14},{11,9},{13,15},{18,16},{20,... | collective-permute-start | bytes 786440 | tf_op jit(solution)/shard_map/ppermute | solution.py:450
  73.8 1.8 %collective-permute-done.15.refs_5_ = bf16[256,512]{1,0:T(8,128)(2,1)S(1)} collective-permute-done((bf16[256,512]{1,0:T(8,128)(2,1)S(1)}, bf16[256,512]{1,0:T(8,128)(2,1)S(1)}, u32[]{:S(2)}, u32[]{:S(2)}) %collective-permute-start.15) | collective-permute-done | bytes 262176 | tf_op jit(solution)/shard_map/ppermute | solution.py:450
  75.6 1.4 %fold.5 = (f32[256,512]{1,0:T(8,128)S(1)}, bf16[256,512]{1,0:T(8,128)(2,1)S(1)}, f32[1024,512]{1,0:T(8,128)S(1)}) custom-call(bf16[256,512]{1,0:T(8,128)(2,1)S(1)} %get-tuple-element.62.refs_0_, bf16[256,512]{1,0:T(8,128)(2,1)S(1)} %get-tuple-element.63.refs_1_, bf16[256,1280]{1,0:T(8,128)(2,1)S(1)} %tie.2.refs_2_, ...), custom_call_target="tpu_custom_call" | custom-call | tf_op jit(solution)/shard_map/fold/pallas_call | solution.py:358
  76.9 1.6 %collective-permute-start.22 = (bf16[256,512]{1,0:T(8,128)(2,1)S(1)}, bf16[256,512]{1,0:T(8,128)(2,1)S(1)}, u32[]{:S(2)}, u32[]{:S(2)}) collective-permute-start(bf16[256,512]{1,0:T(8,128)(2,1)S(1)} %get-tuple-element.73), channel_id=1, source_target_pairs={{0,16},{8,24},{16,0},{24,8},{1,17},{9,25},{17,1},{25,9},{2,18},{10... | collective-permute-start | bytes 786440 | tf_op jit(solution)/shard_map/ppermute | solution.py:58
  78.5 1.3 %collective-permute-start.10 = (bf16[256,256]{1,0:T(8,128)(2,1)S(1)}, bf16[256,256]{1,0:T(8,128)(2,1)S(1)}, u32[]{:S(2)}, u32[]{:S(2)}) collective-permute-start(bf16[256,256]{1,0:T(8,128)(2,1)S(1)} %collective-permute-done.9.refs_4_), channel_id=1, source_target_pairs={{2,0},{4,6},{3,1},{5,7},{10,8},{12,14},{11,9},{13,15},{18,16},{20,... | collective-permute-start | bytes 393224 | tf_op jit(solution)/shard_map/ppermute | solution.py:450
  79.8 5.7 %collective-permute-done.10.refs_10_.refs_5_ = bf16[256,256]{1,0:T(8,128)(2,1)S(1)} collective-permute-done((bf16[256,256]{1,0:T(8,128)(2,1)S(1)}, bf16[256,256]{1,0:T(8,128)(2,1)S(1)}, u32[]{:S(2)}, u32[]{:S(2)}) %collective-permute-start.10) | collective-permute-done | bytes 131104 | tf_op jit(solution)/shard_map/ppermute | solution.py:450
  85.5 1.4 %fold.6 = (f32[256,512]{1,0:T(8,128)S(1)}, bf16[256,512]{1,0:T(8,128)(2,1)S(1)}, f32[1024,512]{1,0:T(8,128)S(1)}) custom-call(bf16[256,512]{1,0:T(8,128)(2,1)S(1)} %get-tuple-element.60.refs_0_, bf16[256,512]{1,0:T(8,128)(2,1)S(1)} %get-tuple-element.61.refs_1_, bf16[256,1280]{1,0:T(8,128)(2,1)S(1)} %tie.2.refs_2_, ...), custom_call_target="tpu_custom_call" | custom-call | tf_op jit(solution)/shard_map/fold/pallas_call | solution.py:358
  88.8 1.5 %collective-permute-start.30 = (bf16[256,512]{1,0:T(8,128)(2,1)S(1)}, bf16[256,512]{1,0:T(8,128)(2,1)S(1)}, u32[]{:S(2)}, u32[]{:S(2)}) collective-permute-start(bf16[256,512]{1,0:T(8,128)(2,1)S(1)} %mine.5.refs_11_.refs_0_), channel_id=1, source_target_pairs={{0,1},{1,0},{2,3},{3,2},{4,5},{5,4},{6,7},{7,6},{8,9},{9,8},{10,11... | collective-permute-start | bytes 786440 | tf_op jit(solution)/shard_map/ppermute | solution.py:457
  91.2 1.4 %collective-permute-start.27 = (bf16[128,512]{1,0:T(8,128)(2,1)S(1)}, bf16[128,512]{1,0:T(8,128)(2,1)S(1)}, u32[]{:S(2)}, u32[]{:S(2)}) collective-permute-start(bf16[128,512]{1,0:T(8,128)(2,1)S(1)} %get-tuple-element.87), channel_id=1, source_target_pairs={{0,16},{8,24},{16,0},{24,8},{1,17},{9,25},{17,1},{25,9},{2,18},{10... | collective-permute-start | bytes 393224 | tf_op jit(solution)/shard_map/ppermute | solution.py:58
  92.5 2.6 %late.1 = (bf16[512,512]{1,0:T(8,128)(2,1)}, f32[512,512]{1,0:T(8,128)S(1)}, f32[512,512]{1,0:T(8,128)S(1)}) custom-call(bf16[512,512]{1,0:T(8,128)(2,1)S(1)} %get-tuple-element.48.refs_1_.refs_3_.q_ref, bf16[512,512]{1,0:T(8,128)(2,1)S(1)} %get-tuple-element.49.refs_2_.k_ref, bf16[512,512]{1,0:T(8,128)(2,1)S(1)} %get-tuple-element.50.refs_3_.v_ref, ...), custom_call_target="tpu_custom_call" | custom-call | tf_op jit(solution)/shard_map/late/pallas_call | solution.py:259
  95.2 2.3 %collective-permute-done.29.refs_1_ = bf16[256,512]{1,0:T(8,128)(2,1)S(1)} collective-permute-done((bf16[256,512]{1,0:T(8,128)(2,1)S(1)}, bf16[256,512]{1,0:T(8,128)(2,1)S(1)}, u32[]{:S(2)}, u32[]{:S(2)}) %collective-permute-start.29) | collective-permute-done | bytes 262176 | tf_op jit(solution)/shard_map/ppermute | solution.py:58
  98.6 1.6 %collective-permute-start.31 = (bf16[256,512]{1,0:T(8,128)(2,1)S(1)}, bf16[256,512]{1,0:T(8,128)(2,1)S(1)}, u32[]{:S(2)}, u32[]{:S(2)}) collective-permute-start(bf16[256,512]{1,0:T(8,128)(2,1)S(1)} %mine.7.refs_0_), channel_id=1, source_target_pairs={{0,1},{1,0},{2,3},{3,2},{4,5},{5,4},{6,7},{7,6},{8,9},{9,8},{10,11... | collective-permute-start | bytes 786440 | tf_op jit(solution)/shard_map/ppermute | solution.py:457
  103.5 1.7 %collective-permute-done.26.refs_1_ = bf16[4,128,128]{2,1,0:T(8,128)(2,1)S(1)} collective-permute-done((bf16[4,128,128]{2,1,0:T(8,128)(2,1)S(1)}, bf16[4,128,128]{2,1,0:T(8,128)(2,1)S(1)}, u32[]{:S(2)}, u32[]{:S(2)}) %collective-permute-start.26) | collective-permute-done | bytes 131104 | tf_op jit(solution)/shard_map/ppermute | solution.py:58
  105.2 1.3 %final.1 = (bf16[512,512]{1,0:T(8,128)(2,1)}, bf16[512,512]{1,0:T(8,128)(2,1)}) custom-call(bf16[512,512]{1,0:T(8,128)(2,1)S(1)} %get-tuple-element.49.refs_2_.k_ref, bf16[512,512]{1,0:T(8,128)(2,1)S(1)} %get-tuple-element.50.refs_3_.v_ref, bf16[4,128,128]{2,1,0:T(8,128)(2,1)S(1)} %states.3.later_ref, f32[512,512]{1,0:T(8,128)S(1)} %get-tuple-element.82.dkp_ref.refs_3_, ...), custom_call_target="tpu_custom_call" | custom-call | tf_op jit(solution)/shard_map/final/pallas_call | solution.py:286
  (65 shorter events, 16.7 us)
Async XLA Ops:
  1.9 3.2 %collective-permute-start = (bf16[128,2048]{1,0:T(8,128)(2,1)S(1)}, bf16[128,2048]{1,0:T(8,128)(2,1)S(1)}, u32[]{:S(2)}, u32[]{:S(2)}) collective-permute-start(bf16[128,2048]{1,0:T(8,128)(2,1)S(1)} %get-tuple-element.47), channel_id=1, source_target_pairs={{0,8},{8,0},{16,24},{24,16},{1,9},{9,1},{17,25},{25,17},{2,10},{10... | collective-permute-start | bytes 1572872 | tf_op jit(solution)/shard_map/ppermute | solution.py:58
  2.4 15.4 %collective-permute-start.2 = (bf16[128,2048]{1,0:T(8,128)(2,1)S(1)}, bf16[128,2048]{1,0:T(8,128)(2,1)S(1)}, u32[]{:S(2)}, u32[]{:S(2)}) collective-permute-start(bf16[128,2048]{1,0:T(8,128)(2,1)S(1)} %get-tuple-element.52.refs_2_), channel_id=1, source_target_pairs={{0,2},{2,0},{4,6},{6,4},{1,3},{3,1},{5,7},{7,5},{8,10},{10,8},{12,... | collective-permute-start | bytes 1572872 | tf_op jit(solution)/shard_map/ppermute | solution.py:444
  5.1 23.5 %collective-permute-start.3 = (bf16[128,2048]{1,0:T(8,128)(2,1)S(1)}, bf16[128,2048]{1,0:T(8,128)(2,1)S(1)}, u32[]{:S(2)}, u32[]{:S(2)}) collective-permute-start(bf16[128,2048]{1,0:T(8,128)(2,1)S(1)} %get-tuple-element.47), channel_id=1, source_target_pairs={{0,10},{2,8},{4,14},{6,12},{8,2},{10,0},{12,6},{14,4},{16,26},{18,... | collective-permute-start | bytes 1572872 | tf_op jit(solution)/shard_map/ppermute | solution.py:453
  7.1 21.5 %collective-permute-start.1 = (bf16[512,512]{1,0:T(8,128)(2,1)S(1)}, bf16[512,512]{1,0:T(8,128)(2,1)S(1)}, u32[]{:S(2)}, u32[]{:S(2)}) collective-permute-start(bf16[512,512]{1,0:T(8,128)(2,1)S(1)} %get-tuple-element.51.refs_0_), channel_id=1, source_target_pairs={{0,8},{8,0},{16,24},{24,16},{1,9},{9,1},{17,25},{25,17},{2,10},{10... | collective-permute-start | bytes 1572872 | tf_op jit(solution)/shard_map/ppermute | solution.py:58
  7.3 22.1 %collective-permute-start.4 = (bf16[128,2048]{1,0:T(8,128)(2,1)S(1)}, bf16[128,2048]{1,0:T(8,128)(2,1)S(1)}, u32[]{:S(2)}, u32[]{:S(2)}) collective-permute-start(bf16[128,2048]{1,0:T(8,128)(2,1)S(1)} %get-tuple-element.52.refs_2_), channel_id=1, source_target_pairs={{2,4},{4,2},{3,5},{5,3},{10,12},{12,10},{11,13},{13,11},{18,20},{2... | collective-permute-start | bytes 1572872 | tf_op jit(solution)/shard_map/ppermute | solution.py:447
  7.9 21.4 %collective-permute-start.5 = (bf16[128,2048]{1,0:T(8,128)(2,1)S(1)}, bf16[128,2048]{1,0:T(8,128)(2,1)S(1)}, u32[]{:S(2)}, u32[]{:S(2)}) collective-permute-start(bf16[128,2048]{1,0:T(8,128)(2,1)S(1)} %get-tuple-element.47), channel_id=1, source_target_pairs={{2,12},{4,10},{10,4},{12,2},{18,28},{20,26},{26,20},{28,18},{3,13}... | collective-permute-start | bytes 1572872 | tf_op jit(solution)/shard_map/ppermute | solution.py:453
  17.8 32.8 %collective-permute-start.11 = (bf16[1024,512]{1,0:T(8,128)(2,1)S(1)}, bf16[1024,512]{1,0:T(8,128)(2,1)S(1)}, u32[]{:S(2)}, u32[]{:S(2)}) collective-permute-start(bf16[1024,512]{1,0:T(8,128)(2,1)S(1)} %copy-done.2), channel_id=1, source_target_pairs={{0,16},{8,24},{16,0},{24,8},{1,17},{9,25},{17,1},{25,9},{2,18},{10... | collective-permute-start | bytes 3145736 | tf_op jit(solution)/shard_map/ppermute | solution.py:58
  28.7 2.1 %collective-permute-start.6 = (bf16[256,768]{1,0:T(8,128)(2,1)S(1)}, bf16[256,768]{1,0:T(8,128)(2,1)S(1)}, u32[]{:S(2)}, u32[]{:S(2)}) collective-permute-start(bf16[256,768]{1,0:T(8,128)(2,1)S(1)} %get-tuple-element.56.refs_1_), channel_id=1, source_target_pairs={{2,4},{4,2},{3,5},{5,3},{10,12},{12,10},{11,13},{13,11},{18,20},{2... | collective-permute-start | bytes 1179656 | tf_op jit(solution)/shard_map/ppermute | solution.py:447
  29.5 17.7 %collective-permute-start.7 = (bf16[256,768]{1,0:T(8,128)(2,1)S(1)}, bf16[256,768]{1,0:T(8,128)(2,1)S(1)}, u32[]{:S(2)}, u32[]{:S(2)}) collective-permute-start(bf16[256,768]{1,0:T(8,128)(2,1)S(1)} %get-tuple-element.57.refs_2_), channel_id=1, source_target_pairs={{2,0},{4,6},{3,1},{5,7},{10,8},{12,14},{11,9},{13,15},{18,16},{20,... | collective-permute-start | bytes 1179656 | tf_op jit(solution)/shard_map/ppermute | solution.py:450
  30.8 25.3 %collective-permute-start.16 = (bf16[256,768]{1,0:T(8,128)(2,1)S(1)}, bf16[256,768]{1,0:T(8,128)(2,1)S(1)}, u32[]{:S(2)}, u32[]{:S(2)}) collective-permute-start(bf16[256,768]{1,0:T(8,128)(2,1)S(1)} %collective-permute-done.6.refs_1_.refs_4_), channel_id=1, source_target_pairs={{2,0},{4,6},{3,1},{5,7},{10,8},{12,14},{11,9},{13,15},{18,16},{20,... | collective-permute-start | bytes 1179656 | tf_op jit(solution)/shard_map/ppermute | solution.py:450
  47.2 28.4 %collective-permute-start.8 = (bf16[256,1280]{1,0:T(8,128)(2,1)S(1)}, bf16[256,1280]{1,0:T(8,128)(2,1)S(1)}, u32[]{:S(2)}, u32[]{:S(2)}) collective-permute-start(bf16[256,1280]{1,0:T(8,128)(2,1)S(1)} %tie.2.refs_2_), channel_id=1, source_target_pairs={{2,0},{4,6},{3,1},{5,7},{10,8},{12,14},{11,9},{13,15},{18,16},{20,... | collective-permute-start | bytes 1966088 | tf_op jit(solution)/shard_map/ppermute | solution.py:450
  48.4 11.6 %collective-permute-start.14 = (bf16[256,512]{1,0:T(8,128)(2,1)S(1)}, bf16[256,512]{1,0:T(8,128)(2,1)S(1)}, u32[]{:S(2)}, u32[]{:S(2)}) collective-permute-start(bf16[256,512]{1,0:T(8,128)(2,1)S(1)} %get-tuple-element.63.refs_1_), channel_id=1, source_target_pairs={{2,4},{4,2},{3,5},{5,3},{10,12},{12,10},{11,13},{13,11},{18,20},{2... | collective-permute-start | bytes 786440 | tf_op jit(solution)/shard_map/ppermute | solution.py:447
  50.2 10.5 %collective-permute-start.17 = (bf16[4,128,128]{2,1,0:T(8,128)(2,1)S(1)}, bf16[4,128,128]{2,1,0:T(8,128)(2,1)S(1)}, u32[]{:S(2)}, u32[]{:S(2)}) collective-permute-start(bf16[4,128,128]{2,1,0:T(8,128)(2,1)S(1)} %get-tuple-element.66.refs_0_), channel_id=1, source_target_pairs={{0,8},{8,0},{16,24},{24,16},{1,9},{9,1},{17,25},{25,17},{2,10},{10... | collective-permute-start | bytes 393224 | tf_op jit(solution)/shard_map/ppermute | solution.py:58
  58.0 7.9 %collective-permute-start.19 = (bf16[192,512]{1,0:T(8,128)(2,1)S(1)}, bf16[192,512]{1,0:T(8,128)(2,1)S(1)}, u32[]{:S(2)}, u32[]{:S(2)}) collective-permute-start(bf16[192,512]{1,0:T(8,128)(2,1)S(1)} %get-tuple-element.70), channel_id=1, source_target_pairs={{0,16},{8,24},{16,0},{24,8},{1,17},{9,25},{17,1},{25,9},{2,18},{10... | collective-permute-start | bytes 589832 | tf_op jit(solution)/shard_map/ppermute | solution.py:58
  59.5 10.5 %collective-permute-start.20 = (bf16[192,512]{1,0:T(8,128)(2,1)S(1)}, bf16[192,512]{1,0:T(8,128)(2,1)S(1)}, u32[]{:S(2)}, u32[]{:S(2)}) collective-permute-start(bf16[192,512]{1,0:T(8,128)(2,1)S(1)} %get-tuple-element.71), channel_id=1, source_target_pairs={{0,16},{8,24},{16,0},{24,8},{1,17},{9,25},{17,1},{25,9},{2,18},{10... | collective-permute-start | bytes 589832 | tf_op jit(solution)/shard_map/ppermute | solution.py:58
  60.1 12.4 %collective-permute-start.12 = (bf16[256,512]{1,0:T(8,128)(2,1)S(1)}, bf16[256,512]{1,0:T(8,128)(2,1)S(1)}, u32[]{:S(2)}, u32[]{:S(2)}) collective-permute-start(bf16[256,512]{1,0:T(8,128)(2,1)S(1)} %get-tuple-element.61.refs_1_), channel_id=1, source_target_pairs={{2,4},{4,2},{3,5},{5,3},{10,12},{12,10},{11,13},{13,11},{18,20},{2... | collective-permute-start | bytes 786440 | tf_op jit(solution)/shard_map/ppermute | solution.py:447
  60.8 14.8 %collective-permute-start.15 = (bf16[256,512]{1,0:T(8,128)(2,1)S(1)}, bf16[256,512]{1,0:T(8,128)(2,1)S(1)}, u32[]{:S(2)}, u32[]{:S(2)}) collective-permute-start(bf16[256,512]{1,0:T(8,128)(2,1)S(1)} %tie.3.refs_4_), channel_id=1, source_target_pairs={{2,0},{4,6},{3,1},{5,7},{10,8},{12,14},{11,9},{13,15},{18,16},{20,... | collective-permute-start | bytes 786440 | tf_op jit(solution)/shard_map/ppermute | solution.py:450
  65.8 5.9 %collective-permute-start.18 = (bf16[4,128,128]{2,1,0:T(8,128)(2,1)S(1)}, bf16[4,128,128]{2,1,0:T(8,128)(2,1)S(1)}, u32[]{:S(2)}, u32[]{:S(2)}) collective-permute-start(bf16[4,128,128]{2,1,0:T(8,128)(2,1)S(1)} %add.2), channel_id=1, source_target_pairs={{0,16},{8,24},{16,0},{24,8},{1,17},{9,25},{17,1},{25,9},{2,18},{10... | collective-permute-start | bytes 393224 | tf_op jit(solution)/shard_map/ppermute | solution.py:58
  70.1 16.8 %collective-permute-start.21 = (bf16[384,512]{1,0:T(8,128)(2,1)S(1)}, bf16[384,512]{1,0:T(8,128)(2,1)S(1)}, u32[]{:S(2)}, u32[]{:S(2)}) collective-permute-start(bf16[384,512]{1,0:T(8,128)(2,1)S(1)} %mine.4.refs_0_), channel_id=1, source_target_pairs={{0,1},{1,0},{2,3},{3,2},{4,5},{5,4},{6,7},{7,6},{8,9},{9,8},{10,11... | collective-permute-start | bytes 1179656 | tf_op jit(solution)/shard_map/ppermute | solution.py:457
  71.8 6.7 %collective-permute-start.9 = (bf16[256,256]{1,0:T(8,128)(2,1)S(1)}, bf16[256,256]{1,0:T(8,128)(2,1)S(1)}, u32[]{:S(2)}, u32[]{:S(2)}) collective-permute-start(bf16[256,256]{1,0:T(8,128)(2,1)S(1)} %get-tuple-element.54.refs_1_), channel_id=1, source_target_pairs={{2,4},{4,2},{3,5},{5,3},{10,12},{12,10},{11,13},{13,11},{18,20},{2... | collective-permute-start | bytes 393224 | tf_op jit(solution)/shard_map/ppermute | solution.py:447
  72.5 13.0 %collective-permute-start.13 = (bf16[256,512]{1,0:T(8,128)(2,1)S(1)}, bf16[256,512]{1,0:T(8,128)(2,1)S(1)}, u32[]{:S(2)}, u32[]{:S(2)}) collective-permute-start(bf16[256,512]{1,0:T(8,128)(2,1)S(1)} %collective-permute-done.12.refs_4_), channel_id=1, source_target_pairs={{2,0},{4,6},{3,1},{5,7},{10,8},{12,14},{11,9},{13,15},{18,16},{20,... | collective-permute-start | bytes 786440 | tf_op jit(solution)/shard_map/ppermute | solution.py:450
  76.9 9.9 %collective-permute-start.22 = (bf16[256,512]{1,0:T(8,128)(2,1)S(1)}, bf16[256,512]{1,0:T(8,128)(2,1)S(1)}, u32[]{:S(2)}, u32[]{:S(2)}) collective-permute-start(bf16[256,512]{1,0:T(8,128)(2,1)S(1)} %get-tuple-element.73), channel_id=1, source_target_pairs={{0,16},{8,24},{16,0},{24,8},{1,17},{9,25},{17,1},{25,9},{2,18},{10... | collective-permute-start | bytes 786440 | tf_op jit(solution)/shard_map/ppermute | solution.py:58
  78.5 7.0 %collective-permute-start.10 = (bf16[256,256]{1,0:T(8,128)(2,1)S(1)}, bf16[256,256]{1,0:T(8,128)(2,1)S(1)}, u32[]{:S(2)}, u32[]{:S(2)}) collective-permute-start(bf16[256,256]{1,0:T(8,128)(2,1)S(1)} %collective-permute-done.9.refs_4_), channel_id=1, source_target_pairs={{2,0},{4,6},{3,1},{5,7},{10,8},{12,14},{11,9},{13,15},{18,16},{20,... | collective-permute-start | bytes 393224 | tf_op jit(solution)/shard_map/ppermute | solution.py:450
  87.7 2.6 %collective-permute-start.23 = (f32[256,512]{1,0:T(8,128)S(1)}, f32[256,512]{1,0:T(8,128)S(1)}, u32[]{:S(2)}, u32[]{:S(2)}) collective-permute-start(f32[256,512]{1,0:T(8,128)S(1)} %get-tuple-element.75), channel_id=1, source_target_pairs={{0,8},{8,0},{16,24},{24,16},{1,9},{9,1},{17,25},{25,17},{2,10},{10... | collective-permute-start | bytes 1572872 | tf_op jit(solution)/shard_map/ppermute | solution.py:58
  87.8 2.6 %collective-permute-start.24 = (f32[256,512]{1,0:T(8,128)S(1)}, f32[256,512]{1,0:T(8,128)S(1)}, u32[]{:S(2)}, u32[]{:S(2)}) collective-permute-start(f32[256,512]{1,0:T(8,128)S(1)} %get-tuple-element.76), channel_id=1, source_target_pairs={{0,8},{8,0},{16,24},{24,16},{1,9},{9,1},{17,25},{25,17},{2,10},{10... | collective-permute-start | bytes 1572872 | tf_op jit(solution)/shard_map/ppermute | solution.py:58
  88.3 9.2 %collective-permute-start.29 = (bf16[256,512]{1,0:T(8,128)(2,1)S(1)}, bf16[256,512]{1,0:T(8,128)(2,1)S(1)}, u32[]{:S(2)}, u32[]{:S(2)}) collective-permute-start(bf16[256,512]{1,0:T(8,128)(2,1)S(1)} %get-tuple-element.89), channel_id=1, source_target_pairs={{0,16},{8,24},{16,0},{24,8},{1,17},{9,25},{17,1},{25,9},{2,18},{10... | collective-permute-start | bytes 786440 | tf_op jit(solution)/shard_map/ppermute | solution.py:58
  88.8 8.6 %collective-permute-start.30 = (bf16[256,512]{1,0:T(8,128)(2,1)S(1)}, bf16[256,512]{1,0:T(8,128)(2,1)S(1)}, u32[]{:S(2)}, u32[]{:S(2)}) collective-permute-start(bf16[256,512]{1,0:T(8,128)(2,1)S(1)} %mine.5.refs_11_.refs_0_), channel_id=1, source_target_pairs={{0,1},{1,0},{2,3},{3,2},{4,5},{5,4},{6,7},{7,6},{8,9},{9,8},{10,11... | collective-permute-start | bytes 786440 | tf_op jit(solution)/shard_map/ppermute | solution.py:457
  91.0 1.6 %collective-permute-start.25 = (bf16[4,128,128]{2,1,0:T(8,128)(2,1)S(1)}, bf16[4,128,128]{2,1,0:T(8,128)(2,1)S(1)}, u32[]{:S(2)}, u32[]{:S(2)}) collective-permute-start(bf16[4,128,128]{2,1,0:T(8,128)(2,1)S(1)} %get-tuple-element.80.refs_0_), channel_id=1, source_target_pairs={{0,8},{8,0},{16,24},{24,16},{1,9},{9,1},{17,25},{25,17},{2,10},{10... | collective-permute-start | bytes 393224 | tf_op jit(solution)/shard_map/ppermute | solution.py:58
  91.2 9.9 %collective-permute-start.27 = (bf16[128,512]{1,0:T(8,128)(2,1)S(1)}, bf16[128,512]{1,0:T(8,128)(2,1)S(1)}, u32[]{:S(2)}, u32[]{:S(2)}) collective-permute-start(bf16[128,512]{1,0:T(8,128)(2,1)S(1)} %get-tuple-element.87), channel_id=1, source_target_pairs={{0,16},{8,24},{16,0},{24,8},{1,17},{9,25},{17,1},{25,9},{2,18},{10... | collective-permute-start | bytes 393224 | tf_op jit(solution)/shard_map/ppermute | solution.py:58
  98.6 8.0 %collective-permute-start.31 = (bf16[256,512]{1,0:T(8,128)(2,1)S(1)}, bf16[256,512]{1,0:T(8,128)(2,1)S(1)}, u32[]{:S(2)}, u32[]{:S(2)}) collective-permute-start(bf16[256,512]{1,0:T(8,128)(2,1)S(1)} %mine.7.refs_0_), channel_id=1, source_target_pairs={{0,1},{1,0},{2,3},{3,2},{4,5},{5,4},{6,7},{7,6},{8,9},{9,8},{10,11... | collective-permute-start | bytes 786440 | tf_op jit(solution)/shard_map/ppermute | solution.py:457
  100.2 5.0 %collective-permute-start.26 = (bf16[4,128,128]{2,1,0:T(8,128)(2,1)S(1)}, bf16[4,128,128]{2,1,0:T(8,128)(2,1)S(1)}, u32[]{:S(2)}, u32[]{:S(2)}) collective-permute-start(bf16[4,128,128]{2,1,0:T(8,128)(2,1)S(1)} %add.3.refs_0_), channel_id=1, source_target_pairs={{0,16},{8,24},{16,0},{24,8},{1,17},{9,25},{17,1},{25,9},{2,18},{10... | collective-permute-start | bytes 393224 | tf_op jit(solution)/shard_map/ppermute | solution.py:58
  101.1 7.0 %collective-permute-start.28 = (bf16[128,512]{1,0:T(8,128)(2,1)S(1)}, bf16[128,512]{1,0:T(8,128)(2,1)S(1)}, u32[]{:S(2)}, u32[]{:S(2)}) collective-permute-start(bf16[128,512]{1,0:T(8,128)(2,1)S(1)} %mine.6.refs_0_), channel_id=1, source_target_pairs={{0,1},{1,0},{2,3},{3,2},{4,5},{5,4},{6,7},{7,6},{8,9},{9,8},{10,11... | collective-permute-start | bytes 393224 | tf_op jit(solution)/shard_map/ppermute | solution.py:457
  (3 other events, 37.5 us)

commit v6 on v5

--- a/solution.py
+++ b/solution.py
@@ -22,7 +22,7 @@
     "late": ("qg",),
     "mine_2": ("late", "last_1"),
     "fold_1": ("prev",),
-    "fold_2": ("c2_3",),
+    "fold_2": ("c2_3", "b2_3"),
     "fold_3": ("last_0", "mine_1"),
 }
 F32 = jnp.float32

time: 109 us -> 109 us (level)
  no operation moved by 1% of the time
where the time goes in v6:
time: 109 us
  waiting for transfers between devices  57.2 us (52%)
  starting transfers between devices  31.3 us (29%)
  Pallas kernels  18.2 us (17%)
    ppermute x6, waiting for transfers between devices, to_ends(): return lax.ppermute(x, 'tsp', [(1, 0), (2, 3)])  28 us
    ppermute x14, starting transfers between devices, swap(): return lax.ppermute(array, axis, [(i, i ^ bit) for i in range(count)])  11.5 us
    ppermute x14, waiting for transfers between devices, swap(): return lax.ppermute(array, axis, [(i, i ^ bit) for i in range(count)])  10.5 us
    ppermute x1, waiting for transfers between devices, outer(): return lax.ppermute(x, 'tsp', OUTER)  9.19 us
    ppermute x2, waiting for transfers between devices, to_other_core(): lax.ppermute(x, ('ctx', 'tsp'), [(t * 4 + i, (t ^ core) * 4 + j) for t in...  8.85 us
    ppermute x6, starting transfers between devices, to_ends(): return lax.ppermute(x, 'tsp', [(1, 0), (2, 3)])  7.73 us
    pallas_call x4, Pallas kernels, fold(): pl.pallas_call(kernel, in_specs=[VMEM] * len(arrays) + [ANY] * len(after)...  5.44 us
    ppermute x4, starting transfers between devices, other(): return lax.ppermute(x, 'dp', [(0, 1), (1, 0)])  5.26 us
  transfers between devices with their start and end apart: 32, of which 13 were waited for; matrix products, arithmetic and copies ran while one was open for 0% of the time, Pallas kernels for 14%

profile of v6, /device:TPU:0, one launch (start us, length us, event | category | flops | bytes accessed | tf_op | source)
XLA Modules:
  0.0 108.7 jit_solution(5997374188814276333)
XLA Ops:
  0.6 1.2 %load.2 = (bf16[128,2048]{1,0:T(8,128)(2,1)S(1)}, bf16[128,2048]{1,0:T(8,128)(2,1)S(1)}) custom-call(bf16[128,4096]{1,0:T(8,128)(2,1)} %bitcast.11, bf16[128,4096]{1,0:T(8,128)(2,1)} %bitcast.12), custom_call_target="tpu_custom_call" | custom-call | tf_op jit(solution)/shard_map/load/pallas_call | solution.py:120
  2.4 2.6 %collective-permute-start.2 = (bf16[128,2048]{1,0:T(8,128)(2,1)S(1)}, bf16[128,2048]{1,0:T(8,128)(2,1)S(1)}, u32[]{:S(2)}, u32[]{:S(2)}) collective-permute-start(bf16[128,2048]{1,0:T(8,128)(2,1)S(1)} %get-tuple-element.52.refs_2_), channel_id=1, source_target_pairs={{0,2},{2,0},{4,6},{6,4},{1,3},{3,1},{5,7},{7,5},{8,10},{10,8},{12,... | collective-permute-start | bytes 1572872 | tf_op jit(solution)/shard_map/ppermute | solution.py:444
  5.1 1.9 %load.3 = (bf16[512,512]{1,0:T(8,128)(2,1)S(1)}, bf16[512,512]{1,0:T(8,128)(2,1)S(1)}, bf16[512,512]{1,0:T(8,128)(2,1)S(1)}, bf16[512,512]{1,0:T(8,128)(2,1)S(1)}, bf16[1024,512]{1,0:T(8,128)(2,1)S(1)}) custom-call(bf16[512,512]{1,0:T(8,128)(2,1)} %bitcast.13, bf16[512,512]{1,0:T(8,128)(2,1)} %bitcast.14, bf16[512,512]{1,0:T(8,128)(2,1)} %bitcast.15, ...), custom_call_target="tpu_custom_call" | custom-call | tf_op jit(solution)/shard_map/load/pallas_call | solution.py:120
  8.6 9.2 %collective-permute-done.2.refs_0_ = bf16[128,2048]{1,0:T(8,128)(2,1)S(1)} collective-permute-done((bf16[128,2048]{1,0:T(8,128)(2,1)S(1)}, bf16[128,2048]{1,0:T(8,128)(2,1)S(1)}, u32[]{:S(2)}, u32[]{:S(2)}) %collective-permute-start.2) | collective-permute-done | bytes 524320 | tf_op jit(solution)/shard_map/ppermute | solution.py:444
  17.8 1.9 %collective-permute-start.11 = (bf16[1024,512]{1,0:T(8,128)(2,1)S(1)}, bf16[1024,512]{1,0:T(8,128)(2,1)S(1)}, u32[]{:S(2)}, u32[]{:S(2)}) collective-permute-start(bf16[1024,512]{1,0:T(8,128)(2,1)S(1)} %copy-done.2), channel_id=1, source_target_pairs={{0,16},{8,24},{16,0},{24,8},{1,17},{9,25},{17,1},{25,9},{2,18},{10... | collective-permute-start | bytes 3145736 | tf_op jit(solution)/shard_map/ppermute | solution.py:58
  19.7 8.8 %collective-permute-done.3.refs_1_ = bf16[128,2048]{1,0:T(8,128)(2,1)S(1)} collective-permute-done((bf16[128,2048]{1,0:T(8,128)(2,1)S(1)}, bf16[128,2048]{1,0:T(8,128)(2,1)S(1)}, u32[]{:S(2)}, u32[]{:S(2)}) %collective-permute-start.3) | collective-permute-done | bytes 524320 | tf_op jit(solution)/shard_map/ppermute | solution.py:453
  29.5 1.3 %collective-permute-start.7 = (bf16[256,768]{1,0:T(8,128)(2,1)S(1)}, bf16[256,768]{1,0:T(8,128)(2,1)S(1)}, u32[]{:S(2)}, u32[]{:S(2)}) collective-permute-start(bf16[256,768]{1,0:T(8,128)(2,1)S(1)} %get-tuple-element.57.refs_2_), channel_id=1, source_target_pairs={{2,0},{4,6},{3,1},{5,7},{10,8},{12,14},{11,9},{13,15},{18,16},{20,... | collective-permute-start | bytes 1179656 | tf_op jit(solution)/shard_map/ppermute | solution.py:450
  30.8 1.3 %collective-permute-start.16 = (bf16[256,768]{1,0:T(8,128)(2,1)S(1)}, bf16[256,768]{1,0:T(8,128)(2,1)S(1)}, u32[]{:S(2)}, u32[]{:S(2)}) collective-permute-start(bf16[256,768]{1,0:T(8,128)(2,1)S(1)} %collective-permute-done.6.refs_1_.refs_4_), channel_id=1, source_target_pairs={{2,0},{4,6},{3,1},{5,7},{10,8},{12,14},{11,9},{13,15},{18,16},{20,... | collective-permute-start | bytes 1179656 | tf_op jit(solution)/shard_map/ppermute | solution.py:450
  32.1 15.1 %collective-permute-done.7.refs_2_.refs_3_ = bf16[256,768]{1,0:T(8,128)(2,1)S(1)} collective-permute-done((bf16[256,768]{1,0:T(8,128)(2,1)S(1)}, bf16[256,768]{1,0:T(8,128)(2,1)S(1)}, u32[]{:S(2)}, u32[]{:S(2)}) %collective-permute-start.7) | collective-permute-done | bytes 393248 | tf_op jit(solution)/shard_map/ppermute | solution.py:450
  47.2 1.3 %collective-permute-start.8 = (bf16[256,1280]{1,0:T(8,128)(2,1)S(1)}, bf16[256,1280]{1,0:T(8,128)(2,1)S(1)}, u32[]{:S(2)}, u32[]{:S(2)}) collective-permute-start(bf16[256,1280]{1,0:T(8,128)(2,1)S(1)} %tie.2.refs_2_), channel_id=1, source_target_pairs={{2,0},{4,6},{3,1},{5,7},{10,8},{12,14},{11,9},{13,15},{18,16},{20,... | collective-permute-start | bytes 1966088 | tf_op jit(solution)/shard_map/ppermute | solution.py:450
  50.6 5.4 %collective-permute-done.16.refs_5_ = bf16[256,768]{1,0:T(8,128)(2,1)S(1)} collective-permute-done((bf16[256,768]{1,0:T(8,128)(2,1)S(1)}, bf16[256,768]{1,0:T(8,128)(2,1)S(1)}, u32[]{:S(2)}, u32[]{:S(2)}) %collective-permute-start.16) | collective-permute-done | bytes 393248 | tf_op jit(solution)/shard_map/ppermute | solution.py:450
  56.1 1.9 %fold.4 = (f32[384,512]{1,0:T(8,128)S(1)}, bf16[192,512]{1,0:T(8,128)(2,1)S(1)}, bf16[192,512]{1,0:T(8,128)(2,1)S(1)}, f32[1024,512]{1,0:T(8,128)S(1)}) custom-call(bf16[256,768]{1,0:T(8,128)(2,1)S(1)} %get-tuple-element.64.refs_0_, bf16[256,768]{1,0:T(8,128)(2,1)S(1)} %get-tuple-element.56.refs_1_, bf16[256,768]{1,0:T(8,128)(2,1)S(1)} %get-tuple-element.57.refs_2_, ...), custom_call_target="tpu_custom_call" | custom-call | tf_op jit(solution)/shard_map/fold/pallas_call | solution.py:358
  58.0 1.6 %collective-permute-start.19 = (bf16[192,512]{1,0:T(8,128)(2,1)S(1)}, bf16[192,512]{1,0:T(8,128)(2,1)S(1)}, u32[]{:S(2)}, u32[]{:S(2)}) collective-permute-start(bf16[192,512]{1,0:T(8,128)(2,1)S(1)} %get-tuple-element.70), channel_id=1, source_target_pairs={{0,16},{8,24},{16,0},{24,8},{1,17},{9,25},{17,1},{25,9},{2,18},{10... | collective-permute-start | bytes 589832 | tf_op jit(solution)/shard_map/ppermute | solution.py:58
  60.8 1.3 %collective-permute-start.15 = (bf16[256,512]{1,0:T(8,128)(2,1)S(1)}, bf16[256,512]{1,0:T(8,128)(2,1)S(1)}, u32[]{:S(2)}, u32[]{:S(2)}) collective-permute-start(bf16[256,512]{1,0:T(8,128)(2,1)S(1)} %tie.3.refs_4_), channel_id=1, source_target_pairs={{2,0},{4,6},{3,1},{5,7},{10,8},{12,14},{11,9},{13,15},{18,16},{20,... | collective-permute-start | bytes 786440 | tf_op jit(solution)/shard_map/ppermute | solution.py:450
  62.1 3.7 %collective-permute-done.19.refs_1_ = bf16[192,512]{1,0:T(8,128)(2,1)S(1)} collective-permute-done((bf16[192,512]{1,0:T(8,128)(2,1)S(1)}, bf16[192,512]{1,0:T(8,128)(2,1)S(1)}, u32[]{:S(2)}, u32[]{:S(2)}) %collective-permute-start.19) | collective-permute-done | bytes 196640 | tf_op jit(solution)/shard_map/ppermute | solution.py:58
  65.8 1.5 %collective-permute-start.18 = (bf16[4,128,128]{2,1,0:T(8,128)(2,1)S(1)}, bf16[4,128,128]{2,1,0:T(8,128)(2,1)S(1)}, u32[]{:S(2)}, u32[]{:S(2)}) collective-permute-start(bf16[4,128,128]{2,1,0:T(8,128)(2,1)S(1)} %add.2), channel_id=1, source_target_pairs={{0,16},{8,24},{16,0},{24,8},{1,17},{9,25},{17,1},{25,9},{2,18},{10... | collective-permute-start | bytes 393224 | tf_op jit(solution)/shard_map/ppermute | solution.py:58
  67.3 2.7 %collective-permute-done.20.refs_2_ = bf16[192,512]{1,0:T(8,128)(2,1)S(1)} collective-permute-done((bf16[192,512]{1,0:T(8,128)(2,1)S(1)}, bf16[192,512]{1,0:T(8,128)(2,1)S(1)}, u32[]{:S(2)}, u32[]{:S(2)}) %collective-permute-start.20) | collective-permute-done | bytes 196640 | tf_op jit(solution)/shard_map/ppermute | solution.py:58
  70.1 1.6 %collective-permute-start.21 = (bf16[384,512]{1,0:T(8,128)(2,1)S(1)}, bf16[384,512]{1,0:T(8,128)(2,1)S(1)}, u32[]{:S(2)}, u32[]{:S(2)}) collective-permute-start(bf16[384,512]{1,0:T(8,128)(2,1)S(1)} %mine.4.refs_0_), channel_id=1, source_target_pairs={{0,1},{1,0},{2,3},{3,2},{4,5},{5,4},{6,7},{7,6},{8,9},{9,8},{10,11... | collective-permute-start | bytes 1179656 | tf_op jit(solution)/shard_map/ppermute | solution.py:457
  72.5 1.3 %collective-permute-start.13 = (bf16[256,512]{1,0:T(8,128)(2,1)S(1)}, bf16[256,512]{1,0:T(8,128)(2,1)S(1)}, u32[]{:S(2)}, u32[]{:S(2)}) collective-permute-start(bf16[256,512]{1,0:T(8,128)(2,1)S(1)} %collective-permute-done.12.refs_4_), channel_id=1, source_target_pairs={{2,0},{4,6},{3,1},{5,7},{10,8},{12,14},{11,9},{13,15},{18,16},{20,... | collective-permute-start | bytes 786440 | tf_op jit(solution)/shard_map/ppermute | solution.py:450
  73.8 1.8 %collective-permute-done.15.refs_5_ = bf16[256,512]{1,0:T(8,128)(2,1)S(1)} collective-permute-done((bf16[256,512]{1,0:T(8,128)(2,1)S(1)}, bf16[256,512]{1,0:T(8,128)(2,1)S(1)}, u32[]{:S(2)}, u32[]{:S(2)}) %collective-permute-start.15) | collective-permute-done | bytes 262176 | tf_op jit(solution)/shard_map/ppermute | solution.py:450
  75.6 1.4 %fold.5 = (f32[256,512]{1,0:T(8,128)S(1)}, bf16[256,512]{1,0:T(8,128)(2,1)S(1)}, f32[1024,512]{1,0:T(8,128)S(1)}) custom-call(bf16[256,512]{1,0:T(8,128)(2,1)S(1)} %get-tuple-element.62.refs_0_, bf16[256,512]{1,0:T(8,128)(2,1)S(1)} %get-tuple-element.63.refs_1_, bf16[256,1280]{1,0:T(8,128)(2,1)S(1)} %tie.2.refs_2_, ...), custom_call_target="tpu_custom_call" | custom-call | tf_op jit(solution)/shard_map/fold/pallas_call | solution.py:358
  76.9 1.6 %collective-permute-start.22 = (bf16[256,512]{1,0:T(8,128)(2,1)S(1)}, bf16[256,512]{1,0:T(8,128)(2,1)S(1)}, u32[]{:S(2)}, u32[]{:S(2)}) collective-permute-start(bf16[256,512]{1,0:T(8,128)(2,1)S(1)} %get-tuple-element.73), channel_id=1, source_target_pairs={{0,16},{8,24},{16,0},{24,8},{1,17},{9,25},{17,1},{25,9},{2,18},{10... | collective-permute-start | bytes 786440 | tf_op jit(solution)/shard_map/ppermute | solution.py:58
  78.5 1.3 %collective-permute-start.10 = (bf16[256,256]{1,0:T(8,128)(2,1)S(1)}, bf16[256,256]{1,0:T(8,128)(2,1)S(1)}, u32[]{:S(2)}, u32[]{:S(2)}) collective-permute-start(bf16[256,256]{1,0:T(8,128)(2,1)S(1)} %collective-permute-done.9.refs_11_.refs_4_), channel_id=1, source_target_pairs={{2,0},{4,6},{3,1},{5,7},{10,8},{12,14},{11,9},{13,15},{18,16},{20,... | collective-permute-start | bytes 393224 | tf_op jit(solution)/shard_map/ppermute | solution.py:450
  79.8 5.7 %collective-permute-done.10.refs_10_.refs_5_ = bf16[256,256]{1,0:T(8,128)(2,1)S(1)} collective-permute-done((bf16[256,256]{1,0:T(8,128)(2,1)S(1)}, bf16[256,256]{1,0:T(8,128)(2,1)S(1)}, u32[]{:S(2)}, u32[]{:S(2)}) %collective-permute-start.10) | collective-permute-done | bytes 131104 | tf_op jit(solution)/shard_map/ppermute | solution.py:450
  85.5 1.4 %fold.6 = (f32[256,512]{1,0:T(8,128)S(1)}, bf16[256,512]{1,0:T(8,128)(2,1)S(1)}, f32[1024,512]{1,0:T(8,128)S(1)}) custom-call(bf16[256,512]{1,0:T(8,128)(2,1)S(1)} %get-tuple-element.60.refs_0_, bf16[256,512]{1,0:T(8,128)(2,1)S(1)} %get-tuple-element.61.refs_1_, bf16[256,1280]{1,0:T(8,128)(2,1)S(1)} %tie.2.refs_2_, ...), custom_call_target="tpu_custom_call" | custom-call | tf_op jit(solution)/shard_map/fold/pallas_call | solution.py:358
  88.8 1.5 %collective-permute-start.30 = (bf16[256,512]{1,0:T(8,128)(2,1)S(1)}, bf16[256,512]{1,0:T(8,128)(2,1)S(1)}, u32[]{:S(2)}, u32[]{:S(2)}) collective-permute-start(bf16[256,512]{1,0:T(8,128)(2,1)S(1)} %mine.5.refs_11_.refs_0_), channel_id=1, source_target_pairs={{0,1},{1,0},{2,3},{3,2},{4,5},{5,4},{6,7},{7,6},{8,9},{9,8},{10,11... | collective-permute-start | bytes 786440 | tf_op jit(solution)/shard_map/ppermute | solution.py:457
  91.2 1.4 %collective-permute-start.27 = (bf16[128,512]{1,0:T(8,128)(2,1)S(1)}, bf16[128,512]{1,0:T(8,128)(2,1)S(1)}, u32[]{:S(2)}, u32[]{:S(2)}) collective-permute-start(bf16[128,512]{1,0:T(8,128)(2,1)S(1)} %get-tuple-element.87), channel_id=1, source_target_pairs={{0,16},{8,24},{16,0},{24,8},{1,17},{9,25},{17,1},{25,9},{2,18},{10... | collective-permute-start | bytes 393224 | tf_op jit(solution)/shard_map/ppermute | solution.py:58
  92.5 2.6 %late.1 = (bf16[512,512]{1,0:T(8,128)(2,1)}, f32[512,512]{1,0:T(8,128)S(1)}, f32[512,512]{1,0:T(8,128)S(1)}) custom-call(bf16[512,512]{1,0:T(8,128)(2,1)S(1)} %get-tuple-element.48.refs_1_.refs_3_.q_ref, bf16[512,512]{1,0:T(8,128)(2,1)S(1)} %get-tuple-element.49.refs_2_.k_ref, bf16[512,512]{1,0:T(8,128)(2,1)S(1)} %get-tuple-element.50.refs_3_.v_ref, ...), custom_call_target="tpu_custom_call" | custom-call | tf_op jit(solution)/shard_map/late/pallas_call | solution.py:259
  95.2 2.3 %collective-permute-done.29.refs_1_ = bf16[256,512]{1,0:T(8,128)(2,1)S(1)} collective-permute-done((bf16[256,512]{1,0:T(8,128)(2,1)S(1)}, bf16[256,512]{1,0:T(8,128)(2,1)S(1)}, u32[]{:S(2)}, u32[]{:S(2)}) %collective-permute-start.29) | collective-permute-done | bytes 262176 | tf_op jit(solution)/shard_map/ppermute | solution.py:58
  98.6 1.6 %collective-permute-start.31 = (bf16[256,512]{1,0:T(8,128)(2,1)S(1)}, bf16[256,512]{1,0:T(8,128)(2,1)S(1)}, u32[]{:S(2)}, u32[]{:S(2)}) collective-permute-start(bf16[256,512]{1,0:T(8,128)(2,1)S(1)} %mine.7.refs_0_), channel_id=1, source_target_pairs={{0,1},{1,0},{2,3},{3,2},{4,5},{5,4},{6,7},{7,6},{8,9},{9,8},{10,11... | collective-permute-start | bytes 786440 | tf_op jit(solution)/shard_map/ppermute | solution.py:457
  103.5 1.7 %collective-permute-done.26.refs_1_ = bf16[4,128,128]{2,1,0:T(8,128)(2,1)S(1)} collective-permute-done((bf16[4,128,128]{2,1,0:T(8,128)(2,1)S(1)}, bf16[4,128,128]{2,1,0:T(8,128)(2,1)S(1)}, u32[]{:S(2)}, u32[]{:S(2)}) %collective-permute-start.26) | collective-permute-done | bytes 131104 | tf_op jit(solution)/shard_map/ppermute | solution.py:58
  105.2 1.3 %final.1 = (bf16[512,512]{1,0:T(8,128)(2,1)}, bf16[512,512]{1,0:T(8,128)(2,1)}) custom-call(bf16[512,512]{1,0:T(8,128)(2,1)S(1)} %get-tuple-element.49.refs_2_.k_ref, bf16[512,512]{1,0:T(8,128)(2,1)S(1)} %get-tuple-element.50.refs_3_.v_ref, bf16[4,128,128]{2,1,0:T(8,128)(2,1)S(1)} %states.3.later_ref, f32[512,512]{1,0:T(8,128)S(1)} %get-tuple-element.82.dkp_ref.refs_3_, ...), custom_call_target="tpu_custom_call" | custom-call | tf_op jit(solution)/shard_map/final/pallas_call | solution.py:286
  (65 shorter events, 16.7 us)
Async XLA Ops:
  1.9 3.2 %collective-permute-start = (bf16[128,2048]{1,0:T(8,128)(2,1)S(1)}, bf16[128,2048]{1,0:T(8,128)(2,1)S(1)}, u32[]{:S(2)}, u32[]{:S(2)}) collective-permute-start(bf16[128,2048]{1,0:T(8,128)(2,1)S(1)} %get-tuple-element.47), channel_id=1, source_target_pairs={{0,8},{8,0},{16,24},{24,16},{1,9},{9,1},{17,25},{25,17},{2,10},{10... | collective-permute-start | bytes 1572872 | tf_op jit(solution)/shard_map/ppermute | solution.py:58
  2.4 15.4 %collective-permute-start.2 = (bf16[128,2048]{1,0:T(8,128)(2,1)S(1)}, bf16[128,2048]{1,0:T(8,128)(2,1)S(1)}, u32[]{:S(2)}, u32[]{:S(2)}) collective-permute-start(bf16[128,2048]{1,0:T(8,128)(2,1)S(1)} %get-tuple-element.52.refs_2_), channel_id=1, source_target_pairs={{0,2},{2,0},{4,6},{6,4},{1,3},{3,1},{5,7},{7,5},{8,10},{10,8},{12,... | collective-permute-start | bytes 1572872 | tf_op jit(solution)/shard_map/ppermute | solution.py:444
  5.1 23.5 %collective-permute-start.3 = (bf16[128,2048]{1,0:T(8,128)(2,1)S(1)}, bf16[128,2048]{1,0:T(8,128)(2,1)S(1)}, u32[]{:S(2)}, u32[]{:S(2)}) collective-permute-start(bf16[128,2048]{1,0:T(8,128)(2,1)S(1)} %get-tuple-element.47), channel_id=1, source_target_pairs={{0,10},{2,8},{4,14},{6,12},{8,2},{10,0},{12,6},{14,4},{16,26},{18,... | collective-permute-start | bytes 1572872 | tf_op jit(solution)/shard_map/ppermute | solution.py:453
  7.1 21.5 %collective-permute-start.1 = (bf16[512,512]{1,0:T(8,128)(2,1)S(1)}, bf16[512,512]{1,0:T(8,128)(2,1)S(1)}, u32[]{:S(2)}, u32[]{:S(2)}) collective-permute-start(bf16[512,512]{1,0:T(8,128)(2,1)S(1)} %get-tuple-element.51.refs_0_), channel_id=1, source_target_pairs={{0,8},{8,0},{16,24},{24,16},{1,9},{9,1},{17,25},{25,17},{2,10},{10... | collective-permute-start | bytes 1572872 | tf_op jit(solution)/shard_map/ppermute | solution.py:58
  7.3 22.1 %collective-permute-start.4 = (bf16[128,2048]{1,0:T(8,128)(2,1)S(1)}, bf16[128,2048]{1,0:T(8,128)(2,1)S(1)}, u32[]{:S(2)}, u32[]{:S(2)}) collective-permute-start(bf16[128,2048]{1,0:T(8,128)(2,1)S(1)} %get-tuple-element.52.refs_2_), channel_id=1, source_target_pairs={{2,4},{4,2},{3,5},{5,3},{10,12},{12,10},{11,13},{13,11},{18,20},{2... | collective-permute-start | bytes 1572872 | tf_op jit(solution)/shard_map/ppermute | solution.py:447
  7.9 21.4 %collective-permute-start.5 = (bf16[128,2048]{1,0:T(8,128)(2,1)S(1)}, bf16[128,2048]{1,0:T(8,128)(2,1)S(1)}, u32[]{:S(2)}, u32[]{:S(2)}) collective-permute-start(bf16[128,2048]{1,0:T(8,128)(2,1)S(1)} %get-tuple-element.47), channel_id=1, source_target_pairs={{2,12},{4,10},{10,4},{12,2},{18,28},{20,26},{26,20},{28,18},{3,13}... | collective-permute-start | bytes 1572872 | tf_op jit(solution)/shard_map/ppermute | solution.py:453
  17.8 32.8 %collective-permute-start.11 = (bf16[1024,512]{1,0:T(8,128)(2,1)S(1)}, bf16[1024,512]{1,0:T(8,128)(2,1)S(1)}, u32[]{:S(2)}, u32[]{:S(2)}) collective-permute-start(bf16[1024,512]{1,0:T(8,128)(2,1)S(1)} %copy-done.2), channel_id=1, source_target_pairs={{0,16},{8,24},{16,0},{24,8},{1,17},{9,25},{17,1},{25,9},{2,18},{10... | collective-permute-start | bytes 3145736 | tf_op jit(solution)/shard_map/ppermute | solution.py:58
  28.7 2.1 %collective-permute-start.6 = (bf16[256,768]{1,0:T(8,128)(2,1)S(1)}, bf16[256,768]{1,0:T(8,128)(2,1)S(1)}, u32[]{:S(2)}, u32[]{:S(2)}) collective-permute-start(bf16[256,768]{1,0:T(8,128)(2,1)S(1)} %get-tuple-element.56.refs_1_), channel_id=1, source_target_pairs={{2,4},{4,2},{3,5},{5,3},{10,12},{12,10},{11,13},{13,11},{18,20},{2... | collective-permute-start | bytes 1179656 | tf_op jit(solution)/shard_map/ppermute | solution.py:447
  29.5 17.7 %collective-permute-start.7 = (bf16[256,768]{1,0:T(8,128)(2,1)S(1)}, bf16[256,768]{1,0:T(8,128)(2,1)S(1)}, u32[]{:S(2)}, u32[]{:S(2)}) collective-permute-start(bf16[256,768]{1,0:T(8,128)(2,1)S(1)} %get-tuple-element.57.refs_2_), channel_id=1, source_target_pairs={{2,0},{4,6},{3,1},{5,7},{10,8},{12,14},{11,9},{13,15},{18,16},{20,... | collective-permute-start | bytes 1179656 | tf_op jit(solution)/shard_map/ppermute | solution.py:450
  30.8 25.3 %collective-permute-start.16 = (bf16[256,768]{1,0:T(8,128)(2,1)S(1)}, bf16[256,768]{1,0:T(8,128)(2,1)S(1)}, u32[]{:S(2)}, u32[]{:S(2)}) collective-permute-start(bf16[256,768]{1,0:T(8,128)(2,1)S(1)} %collective-permute-done.6.refs_1_.refs_4_), channel_id=1, source_target_pairs={{2,0},{4,6},{3,1},{5,7},{10,8},{12,14},{11,9},{13,15},{18,16},{20,... | collective-permute-start | bytes 1179656 | tf_op jit(solution)/shard_map/ppermute | solution.py:450
  47.2 28.4 %collective-permute-start.8 = (bf16[256,1280]{1,0:T(8,128)(2,1)S(1)}, bf16[256,1280]{1,0:T(8,128)(2,1)S(1)}, u32[]{:S(2)}, u32[]{:S(2)}) collective-permute-start(bf16[256,1280]{1,0:T(8,128)(2,1)S(1)} %tie.2.refs_2_), channel_id=1, source_target_pairs={{2,0},{4,6},{3,1},{5,7},{10,8},{12,14},{11,9},{13,15},{18,16},{20,... | collective-permute-start | bytes 1966088 | tf_op jit(solution)/shard_map/ppermute | solution.py:450
  48.4 11.6 %collective-permute-start.14 = (bf16[256,512]{1,0:T(8,128)(2,1)S(1)}, bf16[256,512]{1,0:T(8,128)(2,1)S(1)}, u32[]{:S(2)}, u32[]{:S(2)}) collective-permute-start(bf16[256,512]{1,0:T(8,128)(2,1)S(1)} %get-tuple-element.63.refs_1_), channel_id=1, source_target_pairs={{2,4},{4,2},{3,5},{5,3},{10,12},{12,10},{11,13},{13,11},{18,20},{2... | collective-permute-start | bytes 786440 | tf_op jit(solution)/shard_map/ppermute | solution.py:447
  50.2 10.5 %collective-permute-start.17 = (bf16[4,128,128]{2,1,0:T(8,128)(2,1)S(1)}, bf16[4,128,128]{2,1,0:T(8,128)(2,1)S(1)}, u32[]{:S(2)}, u32[]{:S(2)}) collective-permute-start(bf16[4,128,128]{2,1,0:T(8,128)(2,1)S(1)} %get-tuple-element.66.refs_0_), channel_id=1, source_target_pairs={{0,8},{8,0},{16,24},{24,16},{1,9},{9,1},{17,25},{25,17},{2,10},{10... | collective-permute-start | bytes 393224 | tf_op jit(solution)/shard_map/ppermute | solution.py:58
  58.0 7.9 %collective-permute-start.19 = (bf16[192,512]{1,0:T(8,128)(2,1)S(1)}, bf16[192,512]{1,0:T(8,128)(2,1)S(1)}, u32[]{:S(2)}, u32[]{:S(2)}) collective-permute-start(bf16[192,512]{1,0:T(8,128)(2,1)S(1)} %get-tuple-element.70), channel_id=1, source_target_pairs={{0,16},{8,24},{16,0},{24,8},{1,17},{9,25},{17,1},{25,9},{2,18},{10... | collective-permute-start | bytes 589832 | tf_op jit(solution)/shard_map/ppermute | solution.py:58
  59.5 10.5 %collective-permute-start.20 = (bf16[192,512]{1,0:T(8,128)(2,1)S(1)}, bf16[192,512]{1,0:T(8,128)(2,1)S(1)}, u32[]{:S(2)}, u32[]{:S(2)}) collective-permute-start(bf16[192,512]{1,0:T(8,128)(2,1)S(1)} %get-tuple-element.71), channel_id=1, source_target_pairs={{0,16},{8,24},{16,0},{24,8},{1,17},{9,25},{17,1},{25,9},{2,18},{10... | collective-permute-start | bytes 589832 | tf_op jit(solution)/shard_map/ppermute | solution.py:58
  60.1 12.4 %collective-permute-start.12 = (bf16[256,512]{1,0:T(8,128)(2,1)S(1)}, bf16[256,512]{1,0:T(8,128)(2,1)S(1)}, u32[]{:S(2)}, u32[]{:S(2)}) collective-permute-start(bf16[256,512]{1,0:T(8,128)(2,1)S(1)} %get-tuple-element.61.refs_1_), channel_id=1, source_target_pairs={{2,4},{4,2},{3,5},{5,3},{10,12},{12,10},{11,13},{13,11},{18,20},{2... | collective-permute-start | bytes 786440 | tf_op jit(solution)/shard_map/ppermute | solution.py:447
  60.8 14.8 %collective-permute-start.15 = (bf16[256,512]{1,0:T(8,128)(2,1)S(1)}, bf16[256,512]{1,0:T(8,128)(2,1)S(1)}, u32[]{:S(2)}, u32[]{:S(2)}) collective-permute-start(bf16[256,512]{1,0:T(8,128)(2,1)S(1)} %tie.3.refs_4_), channel_id=1, source_target_pairs={{2,0},{4,6},{3,1},{5,7},{10,8},{12,14},{11,9},{13,15},{18,16},{20,... | collective-permute-start | bytes 786440 | tf_op jit(solution)/shard_map/ppermute | solution.py:450
  65.8 5.9 %collective-permute-start.18 = (bf16[4,128,128]{2,1,0:T(8,128)(2,1)S(1)}, bf16[4,128,128]{2,1,0:T(8,128)(2,1)S(1)}, u32[]{:S(2)}, u32[]{:S(2)}) collective-permute-start(bf16[4,128,128]{2,1,0:T(8,128)(2,1)S(1)} %add.2), channel_id=1, source_target_pairs={{0,16},{8,24},{16,0},{24,8},{1,17},{9,25},{17,1},{25,9},{2,18},{10... | collective-permute-start | bytes 393224 | tf_op jit(solution)/shard_map/ppermute | solution.py:58
  70.1 16.8 %collective-permute-start.21 = (bf16[384,512]{1,0:T(8,128)(2,1)S(1)}, bf16[384,512]{1,0:T(8,128)(2,1)S(1)}, u32[]{:S(2)}, u32[]{:S(2)}) collective-permute-start(bf16[384,512]{1,0:T(8,128)(2,1)S(1)} %mine.4.refs_0_), channel_id=1, source_target_pairs={{0,1},{1,0},{2,3},{3,2},{4,5},{5,4},{6,7},{7,6},{8,9},{9,8},{10,11... | collective-permute-start | bytes 1179656 | tf_op jit(solution)/shard_map/ppermute | solution.py:457
  71.8 6.7 %collective-permute-start.9 = (bf16[256,256]{1,0:T(8,128)(2,1)S(1)}, bf16[256,256]{1,0:T(8,128)(2,1)S(1)}, u32[]{:S(2)}, u32[]{:S(2)}) collective-permute-start(bf16[256,256]{1,0:T(8,128)(2,1)S(1)} %get-tuple-element.54.refs_1_), channel_id=1, source_target_pairs={{2,4},{4,2},{3,5},{5,3},{10,12},{12,10},{11,13},{13,11},{18,20},{2... | collective-permute-start | bytes 393224 | tf_op jit(solution)/shard_map/ppermute | solution.py:447
  72.5 13.0 %collective-permute-start.13 = (bf16[256,512]{1,0:T(8,128)(2,1)S(1)}, bf16[256,512]{1,0:T(8,128)(2,1)S(1)}, u32[]{:S(2)}, u32[]{:S(2)}) collective-permute-start(bf16[256,512]{1,0:T(8,128)(2,1)S(1)} %collective-permute-done.12.refs_4_), channel_id=1, source_target_pairs={{2,0},{4,6},{3,1},{5,7},{10,8},{12,14},{11,9},{13,15},{18,16},{20,... | collective-permute-start | bytes 786440 | tf_op jit(solution)/shard_map/ppermute | solution.py:450
  76.9 9.9 %collective-permute-start.22 = (bf16[256,512]{1,0:T(8,128)(2,1)S(1)}, bf16[256,512]{1,0:T(8,128)(2,1)S(1)}, u32[]{:S(2)}, u32[]{:S(2)}) collective-permute-start(bf16[256,512]{1,0:T(8,128)(2,1)S(1)} %get-tuple-element.73), channel_id=1, source_target_pairs={{0,16},{8,24},{16,0},{24,8},{1,17},{9,25},{17,1},{25,9},{2,18},{10... | collective-permute-start | bytes 786440 | tf_op jit(solution)/shard_map/ppermute | solution.py:58
  78.5 7.0 %collective-permute-start.10 = (bf16[256,256]{1,0:T(8,128)(2,1)S(1)}, bf16[256,256]{1,0:T(8,128)(2,1)S(1)}, u32[]{:S(2)}, u32[]{:S(2)}) collective-permute-start(bf16[256,256]{1,0:T(8,128)(2,1)S(1)} %collective-permute-done.9.refs_11_.refs_4_), channel_id=1, source_target_pairs={{2,0},{4,6},{3,1},{5,7},{10,8},{12,14},{11,9},{13,15},{18,16},{20,... | collective-permute-start | bytes 393224 | tf_op jit(solution)/shard_map/ppermute | solution.py:450
  87.7 2.6 %collective-permute-start.23 = (f32[256,512]{1,0:T(8,128)S(1)}, f32[256,512]{1,0:T(8,128)S(1)}, u32[]{:S(2)}, u32[]{:S(2)}) collective-permute-start(f32[256,512]{1,0:T(8,128)S(1)} %get-tuple-element.75), channel_id=1, source_target_pairs={{0,8},{8,0},{16,24},{24,16},{1,9},{9,1},{17,25},{25,17},{2,10},{10... | collective-permute-start | bytes 1572872 | tf_op jit(solution)/shard_map/ppermute | solution.py:58
  87.8 2.6 %collective-permute-start.24 = (f32[256,512]{1,0:T(8,128)S(1)}, f32[256,512]{1,0:T(8,128)S(1)}, u32[]{:S(2)}, u32[]{:S(2)}) collective-permute-start(f32[256,512]{1,0:T(8,128)S(1)} %get-tuple-element.76), channel_id=1, source_target_pairs={{0,8},{8,0},{16,24},{24,16},{1,9},{9,1},{17,25},{25,17},{2,10},{10... | collective-permute-start | bytes 1572872 | tf_op jit(solution)/shard_map/ppermute | solution.py:58
  88.3 9.2 %collective-permute-start.29 = (bf16[256,512]{1,0:T(8,128)(2,1)S(1)}, bf16[256,512]{1,0:T(8,128)(2,1)S(1)}, u32[]{:S(2)}, u32[]{:S(2)}) collective-permute-start(bf16[256,512]{1,0:T(8,128)(2,1)S(1)} %get-tuple-element.89), channel_id=1, source_target_pairs={{0,16},{8,24},{16,0},{24,8},{1,17},{9,25},{17,1},{25,9},{2,18},{10... | collective-permute-start | bytes 786440 | tf_op jit(solution)/shard_map/ppermute | solution.py:58
  88.8 8.6 %collective-permute-start.30 = (bf16[256,512]{1,0:T(8,128)(2,1)S(1)}, bf16[256,512]{1,0:T(8,128)(2,1)S(1)}, u32[]{:S(2)}, u32[]{:S(2)}) collective-permute-start(bf16[256,512]{1,0:T(8,128)(2,1)S(1)} %mine.5.refs_11_.refs_0_), channel_id=1, source_target_pairs={{0,1},{1,0},{2,3},{3,2},{4,5},{5,4},{6,7},{7,6},{8,9},{9,8},{10,11... | collective-permute-start | bytes 786440 | tf_op jit(solution)/shard_map/ppermute | solution.py:457
  91.0 1.6 %collective-permute-start.25 = (bf16[4,128,128]{2,1,0:T(8,128)(2,1)S(1)}, bf16[4,128,128]{2,1,0:T(8,128)(2,1)S(1)}, u32[]{:S(2)}, u32[]{:S(2)}) collective-permute-start(bf16[4,128,128]{2,1,0:T(8,128)(2,1)S(1)} %get-tuple-element.80.refs_0_), channel_id=1, source_target_pairs={{0,8},{8,0},{16,24},{24,16},{1,9},{9,1},{17,25},{25,17},{2,10},{10... | collective-permute-start | bytes 393224 | tf_op jit(solution)/shard_map/ppermute | solution.py:58
  91.2 9.9 %collective-permute-start.27 = (bf16[128,512]{1,0:T(8,128)(2,1)S(1)}, bf16[128,512]{1,0:T(8,128)(2,1)S(1)}, u32[]{:S(2)}, u32[]{:S(2)}) collective-permute-start(bf16[128,512]{1,0:T(8,128)(2,1)S(1)} %get-tuple-element.87), channel_id=1, source_target_pairs={{0,16},{8,24},{16,0},{24,8},{1,17},{9,25},{17,1},{25,9},{2,18},{10... | collective-permute-start | bytes 393224 | tf_op jit(solution)/shard_map/ppermute | solution.py:58
  98.6 8.0 %collective-permute-start.31 = (bf16[256,512]{1,0:T(8,128)(2,1)S(1)}, bf16[256,512]{1,0:T(8,128)(2,1)S(1)}, u32[]{:S(2)}, u32[]{:S(2)}) collective-permute-start(bf16[256,512]{1,0:T(8,128)(2,1)S(1)} %mine.7.refs_0_), channel_id=1, source_target_pairs={{0,1},{1,0},{2,3},{3,2},{4,5},{5,4},{6,7},{7,6},{8,9},{9,8},{10,11... | collective-permute-start | bytes 786440 | tf_op jit(solution)/shard_map/ppermute | solution.py:457
  100.2 5.0 %collective-permute-start.26 = (bf16[4,128,128]{2,1,0:T(8,128)(2,1)S(1)}, bf16[4,128,128]{2,1,0:T(8,128)(2,1)S(1)}, u32[]{:S(2)}, u32[]{:S(2)}) collective-permute-start(bf16[4,128,128]{2,1,0:T(8,128)(2,1)S(1)} %add.3.refs_0_), channel_id=1, source_target_pairs={{0,16},{8,24},{16,0},{24,8},{1,17},{9,25},{17,1},{25,9},{2,18},{10... | collective-permute-start | bytes 393224 | tf_op jit(solution)/shard_map/ppermute | solution.py:58
  101.1 7.0 %collective-permute-start.28 = (bf16[128,512]{1,0:T(8,128)(2,1)S(1)}, bf16[128,512]{1,0:T(8,128)(2,1)S(1)}, u32[]{:S(2)}, u32[]{:S(2)}) collective-permute-start(bf16[128,512]{1,0:T(8,128)(2,1)S(1)} %mine.6.refs_0_), channel_id=1, source_target_pairs={{0,1},{1,0},{2,3},{3,2},{4,5},{5,4},{6,7},{7,6},{8,9},{9,8},{10,11... | collective-permute-start | bytes 393224 | tf_op jit(solution)/shard_map/ppermute | solution.py:457
  (3 other events, 37.5 us)
